TPU v7x, 256 devices: a whole 4x4x8 slice. The times are simulated.
256 devices in a mesh: gx: 8 (over y, core), gy: 4 (over x), gz: 8 (over z).
Axes of the slice: x: 4, y: 4, z: 8, core: 2. Of those that a mesh axis runs over, the one named last changes fastest.
Arguments:
- phase_stack: float32 [512, 524288], P(None, ('gx', 'gy', 'gz')), may hold values from -40 to 40
- start_basis: float32 [512, 64], replicated, may hold values from -6 to 6
Outputs:
- corrected: float32 [512, 524288], P(None, ('gx', 'gy', 'gz'))
All inputs are finite; a program needn't handle non-finite values.
Results may differ from a plain program's by a relative error of at most 0.0003.
Values sent between devices are 32-bit elements; how exact they have to be, the bound alone decides.
No kernel may reach another device: no remote copies, remote signals or barrier semaphores. Data moves between devices by JAX's collectives and lax.ppermute only.
A program may use at most 64 MiB of HBM per device.

v0:
```python
import jax
import jax.numpy as jnp
from jax import lax
from jax.sharding import Mesh
from jax.sharding import PartitionSpec as P

ITERS = 3
GX_GY_GZ = ("gx_0", "gx_1", "gy", "gz")


HIGHEST = lax.Precision.HIGHEST
EPSILON = 1e-06


def split_up(x, dim, peers):
    dims = x.shape
    tiles = x.reshape(*dims[:dim], peers, dims[dim] // peers, *dims[dim + 1 :])
    return jnp.moveaxis(tiles, dim, 0)


def summed_on_arrival(x, axis, dim):
    tiles = split_up(x, dim, lax.axis_size(axis))
    arrived = lax.all_to_all(tiles, axis, split_axis=0, concat_axis=0, tiled=True)
    return arrived.sum(axis=0)


def summed_rows(x, axes, dim):
    far, near = axes
    tiles = split_up(x, dim, lax.axis_size(far))
    nearer = summed_on_arrival(tiles, near, dim + 1)
    arrived = lax.all_to_all(nearer, far, split_axis=0, concat_axis=0, tiled=True)
    return arrived.sum(axis=0)


def padded_to(lines, peers):
    spare = -len(lines) % peers
    return jnp.pad(lines, [(0, spare)] + [(0, 0)] * (lines.ndim - 1))


def from_everyone(x, axis):
    peers = lax.axis_size(axis)
    return lax.all_to_all(jnp.broadcast_to(x[None], (peers, *x.shape)), axis, 0, 0, tiled=True)


def joined_along(tiles, dim):
    tiles = jnp.moveaxis(tiles, 0, dim)
    dims = tiles.shape
    return tiles.reshape(*dims[:dim], dims[dim] * dims[dim + 1], *dims[dim + 2 :])


def whole_of(x, axes, dim):
    far, near = axes
    tiles = from_everyone(from_everyone(x, far), near)
    return joined_along(tiles.swapaxes(0, 1).reshape(-1, *x.shape), dim)


def sum_by_parts(x, axes):
    lines = x.reshape(-1, x.shape[-1])
    own = summed_rows(padded_to(lines, lax.axis_size(axes[0]) * lax.axis_size(axes[1])), axes, 0)
    whole = whole_of(own, axes, 0)
    return whole[: len(lines)].reshape(x.shape)


def taken_together(x, axis):
    everything = from_everyone(x, axis)
    return jnp.sum(everything, axis=0)


def over_axes(x, axes):
    far, near = axes
    nearer = taken_together(x, near)
    return taken_together(nearer, far)


def orthonormal(columns):
    inner_gram = jnp.dot(columns.T, columns, precision=HIGHEST)
    cholesky_factor = jnp.linalg.cholesky(inner_gram)
    return jax.scipy.linalg.solve_triangular(cholesky_factor, columns.T, lower=True).T


def on_device(phase_stack, start_basis):
    pixel_total = phase_stack.shape[1] * lax.axis_size(GX_GY_GZ)
    subspace = orthonormal(start_basis)
    local_gram = jnp.dot(phase_stack, phase_stack.T, precision=HIGHEST)
    gram_matrix = sum_by_parts(local_gram, (("gx_0", "gx_1"), ("gy", "gz"))) / pixel_total
    for sweep in range(ITERS):
        subspace = orthonormal(jnp.dot(gram_matrix, subspace, precision=HIGHEST))
    loadings = jnp.dot(subspace.T, phase_stack, precision=HIGHEST)
    residual = phase_stack - jnp.dot(subspace, loadings, precision=HIGHEST)
    row_power = (
        over_axes(jnp.sum(residual * residual, axis=1), (("gx_0", "gx_1"), ("gy", "gz")))
        / pixel_total
    )
    return residual * lax.rsqrt(row_power + EPSILON)[:, None]


def solution(mesh):
    split = Mesh(
        mesh.devices.reshape(4, 2, mesh.shape["gy"], mesh.shape["gz"]), ("gx_0", "gx_1", "gy", "gz")
    )
    placed = (P(None, GX_GY_GZ), P())
    return jax.shard_map(
        on_device, mesh=split, in_specs=placed, out_specs=P(None, GX_GY_GZ), check_vma=False
    )
```

profile of v0, /device:TPU:1, one launch (start us, length us, event | category | flops | bytes accessed | tf_op | source)
XLA Modules:
  0.0 185.4 jit_solution(7357504424811120509)
XLA Ops:
  0.0 9.3 %fusion.26 = f32[512,512]{1,0:T(8,128)S(1)} fusion(f32[512,2048]{1,0:T(8,128)} %param.5), kind=kOutput, calls=%fused_computation.47 | convolution fusion | flops 6442450944 | bytes 5242880 | tf_op jit(solution)/shard_map/dot_general | solution.py:84
  9.4 0.6 reshape_reshape.4
  10.0 0.6 copy.36
  10.6 36.3 %all_to_all.32 = f32[32,8,2,512]{3,2,1,0:T(2,128)S(1)} all-to-all(f32[32,8,2,512]{3,2,1,0:T(2,128)S(1)} %bitcast.73), channel_id=1, replica_groups=mesh['gx_0'=4,'gx_1'=2,'gy'=4,'gz'=8] {'gy','gz'}, dimensions={0} | all-to-all | bytes 2097152 | tf_op jit(solution)/shard_map/all_to_all | solution.py:23
  46.9 0.3 reduce_sum.45
  47.2 13.9 %all_to_all.33 = f32[8,2,512]{2,1,0:T(2,128)S(1)} all-to-all(f32[8,2,512]{2,1,0:T(2,128)S(1)} %reduce_sum.45), channel_id=1, replica_groups=mesh['gx_0'=4,'gx_1'=2,'gy'=4,'gz'=8] {'gx_0','gx_1'}, dimensions={0} | all-to-all | bytes 65536 | tf_op jit(solution)/shard_map/all_to_all | solution.py:31
  61.2 7.8 %all_to_all.34 = f32[8,2,512]{2,1,0:T(2,128)S(1)} all-to-all(f32[8,2,512]{2,1,0:T(2,128)S(1)} %broadcast_in_dim.9), channel_id=1, replica_groups=mesh['gx_0'=4,'gx_1'=2,'gy'=4,'gz'=8] {'gx_0','gx_1'}, dimensions={0} | all-to-all | bytes 65536 | tf_op jit(solution)/shard_map/all_to_all | solution.py:42
  69.0 1.4 broadcast_in_dim.10
  70.4 5.0 %all-to-all-start.3 = ((f32[32,8,2,512]{3,2,1,0:T(2,128)}), f32[32,8,2,512]{3,2,1,0:T(2,128)S(1)}, u32[]{:S(2)}, u32[]{:S(2)}) async-start(f32[32,8,2,512]{3,2,1,0:T(2,128)} %broadcast_in_dim.10), calls=%async_computation.3 | async-start | bytes 2097152 | tf_op jit(solution)/shard_map/all_to_all | solution.py:42
  75.4 0.3 fusion.27
  75.7 0.1 copy.26
  75.8 5.8 %cholesky.74 = f32[64,64]{1,0:T(8,128)S(1)} custom-call(f32[64,64]{1,0:T(8,128)S(1)} %fusion.19), custom_call_target="Cholesky" | custom-call | tf_op jit(solution)/shard_map/jit(cholesky)/cholesky | solution.py:77
  81.7 0.7 compare_reduce_fusion.3
  82.4 0.7 fusion.8
  83.1 4.9 %custom-call.8 = f32[1,64,64]{1,2,0:T(8,128)S(1)} custom-call(f32[1,64,64]{2,1,0:T(8,128)S(1)} %fusion.8), custom_call_target="InvertDiagBlocksLowerTriangular" | custom-call | tf_op jit(solution)/shard_map/jit(_solve_triangular)/triangular_solve | solution.py:78
  88.0 0.3 fusion.6
  88.3 11.5 %all-to-all-done.3 = f32[32,8,2,512]{3,2,1,0:T(2,128)S(1)} async-done(((f32[32,8,2,512]{3,2,1,0:T(2,128)}), f32[32,8,2,512]{3,2,1,0:T(2,128)S(1)}, u32[]{:S(2)}, u32[]{:S(2)}) %all-to-all-start.3) | async-done | bytes 1048608 | tf_op jit(solution)/shard_map/all_to_all | solution.py:42
  99.8 0.5 multiply_bitcast_fusion
  100.4 0.4 copy.25
  100.8 0.7 div.25
  101.5 1.1 fusion.28
  102.6 0.3 fusion.29
  102.9 0.1 copy.27
  103.0 5.8 %cholesky.85 = f32[64,64]{1,0:T(8,128)S(1)} custom-call(f32[64,64]{1,0:T(8,128)S(1)} %fusion.17), custom_call_target="Cholesky" | custom-call | tf_op jit(solution)/shard_map/jit(cholesky)/cholesky | solution.py:77
  108.9 0.6 compare_reduce_fusion.2
  109.5 0.7 fusion.9
  110.2 4.9 %custom-call.9 = f32[1,64,64]{1,2,0:T(8,128)S(1)} custom-call(f32[1,64,64]{2,1,0:T(8,128)S(1)} %fusion.9), custom_call_target="InvertDiagBlocksLowerTriangular" | custom-call | tf_op jit(solution)/shard_map/jit(_solve_triangular)/triangular_solve | solution.py:78
  115.1 0.3 fusion.4
  115.4 1.1 fusion.30
  116.6 0.3 fusion.31
  116.9 5.8 %cholesky.96 = f32[64,64]{1,0:T(8,128)S(1)} custom-call(f32[64,64]{1,0:T(8,128)S(1)} %fusion.15), custom_call_target="Cholesky" | custom-call | tf_op jit(solution)/shard_map/jit(cholesky)/cholesky | solution.py:77
  122.8 0.6 compare_reduce_fusion.1
  123.5 0.7 fusion.10
  124.1 4.9 %custom-call.10 = f32[1,64,64]{1,2,0:T(8,128)S(1)} custom-call(f32[1,64,64]{2,1,0:T(8,128)S(1)} %fusion.10), custom_call_target="InvertDiagBlocksLowerTriangular" | custom-call | tf_op jit(solution)/shard_map/jit(_solve_triangular)/triangular_solve | solution.py:78
  129.0 0.3 fusion.2
  129.4 1.1 fusion.32
  130.5 0.3 fusion.33
  130.8 0.1 copy.29
  130.9 5.8 %cholesky.107 = f32[64,64]{1,0:T(8,128)S(1)} custom-call(f32[64,64]{1,0:T(8,128)S(1)} %fusion.13), custom_call_target="Cholesky" | custom-call | tf_op jit(solution)/shard_map/jit(cholesky)/cholesky | solution.py:77
  136.7 0.6 compare_reduce_fusion
  137.4 0.7 fusion.11
  138.0 5.0 %custom-call.11 = f32[1,64,64]{1,2,0:T(8,128)S(1)} custom-call(f32[1,64,64]{2,1,0:T(8,128)S(1)} %fusion.11), custom_call_target="InvertDiagBlocksLowerTriangular" | custom-call | tf_op jit(solution)/shard_map/jit(_solve_triangular)/triangular_solve | solution.py:78
  143.1 0.3 fusion
  143.4 5.0 %fusion.34 = f32[64,2048]{1,0:T(8,128)S(1)} fusion(f32[64,512]{1,0:T(8,128)S(1)} %fusion, f32[512,2048]{1,0:T(8,128)} %param.5), kind=kOutput, calls=%fused_computation.55 | convolution fusion | flops 805306368 | bytes 4849664 | tf_op jit(solution)/shard_map/dot_general | solution.py:88
  148.4 5.5 %multiply_reduce_fusion = (f32[512]{0:T(512)S(1)}, f32[512,2048]{1,0:T(8,128)}) fusion(f32[512,2048]{1,0:T(8,128)S(1)} %copy-done.1, f32[64,512]{1,0:T(8,128)S(1)} %fusion, f32[64,2048]{1,0:T(8,128)S(1)} %fusion.34), kind=kOutput, calls=%fused_computation | convolution fusion | flops 808451584 | bytes 9046016 | tf_op jit(solution)/shard_map/dot_general | solution.py:89
  153.9 17.3 %all_to_all.35 = f32[32,1,512]{2,1,0:T(1,128)S(1)} all-to-all(f32[32,1,512]{2,1,0:T(1,128)S(1)} %broadcast_in_dim.11), channel_id=1, replica_groups=mesh['gx_0'=4,'gx_1'=2,'gy'=4,'gz'=8] {'gy','gz'}, dimensions={0} | all-to-all | bytes 131072 | tf_op jit(solution)/shard_map/all_to_all | solution.py:42
  171.2 9.6 %all_to_all.36 = f32[8,1,512]{2,1,0:T(1,128)S(1)} all-to-all(f32[8,1,512]{2,1,0:T(1,128)S(1)} %broadcast_in_dim.12), channel_id=1, replica_groups=mesh['gx_0'=4,'gx_1'=2,'gy'=4,'gz'=8] {'gx_0','gx_1'}, dimensions={0} | all-to-all | bytes 32768 | tf_op jit(solution)/shard_map/all_to_all | solution.py:42
  180.9 4.5 %broadcast_multiply_fusion = f32[512,2048]{1,0:T(8,128)} fusion(f32[512,2048]{1,0:T(8,128)} %get-tuple-element.8, f32[512]{0:T(512)S(1)} %add_rsqrt_fusion), kind=kLoop, calls=%fused_computation.2 | loop fusion | flops 1048576 | bytes 8390656 | tf_op jit(solution)/shard_map/mul | solution.py:94
  (20 shorter events, 0.4 us)
Async XLA Ops:
  0.0 75.4 %copy-start = (f32[512,64]{0,1:T(8,128)S(1)}, f32[512,64]{0,1:T(8,128)}, u32[]{:S(2)}) copy-start(f32[512,64]{0,1:T(8,128)} %param.6) | copy-start | bytes 393220
  70.4 29.4 %all-to-all-start.3 = ((f32[32,8,2,512]{3,2,1,0:T(2,128)}), f32[32,8,2,512]{3,2,1,0:T(2,128)S(1)}, u32[]{:S(2)}, u32[]{:S(2)}) async-start(f32[32,8,2,512]{3,2,1,0:T(2,128)} %broadcast_in_dim.10), calls=%async_computation.3 | async-start | bytes 2097152 | tf_op jit(solution)/shard_map/all_to_all | solution.py:42
  143.0 5.3 %copy-start.1 = (f32[512,2048]{1,0:T(8,128)S(1)}, f32[512,2048]{1,0:T(8,128)}, u32[]{:S(2)}) copy-start(f32[512,2048]{1,0:T(8,128)} %param.5) | copy-start | bytes 12582916
where the time goes:
time: 186 us; the launch traced here: 185 us
  blocking collectives  84.9 us (46%)
  other arithmetic  54.1 us (29%)
  matrix products  25.6 us (14%)
  waiting for transfers between devices  11.5 us (6%)
  starting transfers between devices  4.97 us (3%)
  local copies, waits for them, and re-layouts  4.11 us (2%)
    all_to_all x1, blocking collectives, summed_on_arrival(): lax.all_to_all(tiles, axis, split_axis=0, concat_axis=0, tiled=True)  36.3 us
    all_to_all x3, blocking collectives, from_everyone(): lax.all_to_all(jnp.broadcast_to(x[None], (peers, *x.shape)), axis, 0, 0,...  34.7 us
    another operation x12, other arithmetic, orthonormal(): cholesky_factor = jnp.linalg.cholesky(inner_gram)  26.2 us
    another operation x8, other arithmetic, orthonormal(): jax.scipy.linalg.solve_triangular(cholesky_factor, columns.T, lower=True)  22.3 us
    all_to_all x1, blocking collectives, summed_rows(): lax.all_to_all(nearer, far, split_axis=0, concat_axis=0, tiled=True)  13.9 us
    all_to_all x1, waiting for transfers between devices, from_everyone(): lax.all_to_all(jnp.broadcast_to(x[None], (peers, *x.shape)), axis, 0, 0,...  11.5 us
    dot_general x1, matrix products, on_device(): local_gram = jnp.dot(phase_stack, phase_stack.T, precision=HIGHEST)  9.34 us
    dot_general x1, matrix products, on_device(): residual = phase_stack - jnp.dot(subspace, loadings, precision=HIGHEST)  5.46 us
  transfers between devices with their start and end apart: 1, of which 1 were waited for; matrix products, arithmetic and copies ran while one was open for 7% of the time, Pallas kernels for 0%

commit v1 on v0

v1 whole, which is shorter than its diff:
```python
import jax
import jax.numpy as jnp
from jax import lax
from jax.sharding import Mesh
from jax.sharding import PartitionSpec as P

ITERS = 3
AXES = ("y", "c", "x", "z")
HIGH = lax.Precision.HIGH
HIGHEST = lax.Precision.HIGHEST
EPSILON = 1e-06
TILE = 128


def shifted(v, axis, step):
    n = lax.axis_size(axis)
    return lax.ppermute(v, axis, [(i, (i + step) % n) for i in range(n)])


def share_of_sum(v, axis):
    n, me = lax.axis_size(axis), lax.axis_index(axis)
    rows = v.shape[0] // n
    piece = lambda k: lax.dynamic_slice_in_dim(v, lax.rem(me + k, n) * rows, rows, 0)
    arrived = [shifted(piece(k), axis, k) for k in range(1, n)]
    total = piece(0)
    for part in arrived:
        total = total + part
    return total


def joined(v, axis):
    n, me = lax.axis_size(axis), lax.axis_index(axis)
    rows = v.shape[0]
    arrived = [shifted(v, axis, k) for k in range(1, n)]
    whole = jnp.zeros((n * rows, *v.shape[1:]), v.dtype)
    whole = lax.dynamic_update_slice_in_dim(whole, v, me * rows, 0)
    for k, part in enumerate(arrived, 1):
        whole = lax.dynamic_update_slice_in_dim(whole, part, lax.rem(me - k + n, n) * rows, 0)
    return whole


def summed(v, axis):
    n = lax.axis_size(axis)
    copies = jnp.broadcast_to(v[None], (n, *v.shape)).reshape(n * v.shape[0], *v.shape[1:])
    arrived = lax.all_to_all(copies, axis, 0, 0, tiled=True)
    return arrived.reshape(n, *v.shape).sum(axis=0)


def sum_everywhere(v):
    v = share_of_sum(v, "c")
    v = share_of_sum(v, "y")
    v = share_of_sum(v, "x")
    v = summed(v, "z")
    v = joined(v, "x")
    v = joined(v, "y")
    return joined(v, "c")


def packed(gram):
    n = gram.shape[0] // TILE
    tiles = gram.reshape(n, TILE, n, TILE)
    return jnp.concatenate([tiles[i, :, j] for i in range(n) for j in range(i, n)], axis=0)


def unpacked(lines, n):
    tiles = {}
    place = 0
    for i in range(n):
        for j in range(i, n):
            tile = lines[place * TILE : (place + 1) * TILE]
            tiles[i, j] = tile
            tiles[j, i] = tile.T
            place += 1
    return jnp.block([[tiles[i, j] for j in range(n)] for i in range(n)])


def orthonormal(columns):
    inner_gram = jnp.dot(columns.T, columns, precision=HIGHEST)
    cholesky_factor = jnp.linalg.cholesky(inner_gram)
    return jax.scipy.linalg.solve_triangular(cholesky_factor, columns.T, lower=True).T


def on_device(phase_stack, start_basis):
    pixel_total = phase_stack.shape[1] * lax.axis_size(AXES)
    subspace = orthonormal(start_basis)
    local_gram = jnp.dot(phase_stack, phase_stack.T, precision=HIGHEST)
    lines = sum_everywhere(packed(local_gram))
    gram_matrix = unpacked(lines, local_gram.shape[0] // TILE) / pixel_total
    for sweep in range(ITERS):
        subspace = orthonormal(jnp.dot(gram_matrix, subspace, precision=HIGHEST))
    left = gram_matrix - jnp.dot(
        subspace, jnp.dot(subspace.T, gram_matrix, precision=HIGHEST), precision=HIGHEST
    )
    across = jnp.dot(left, subspace, precision=HIGHEST)
    row_power = jnp.diagonal(left) - jnp.sum(across * subspace, axis=1)
    row_scale = lax.rsqrt(jnp.maximum(row_power, 0.0) + EPSILON)[:, None]
    loadings = jnp.dot(subspace.T, phase_stack, precision=HIGH)
    return (phase_stack - jnp.dot(subspace, loadings, precision=HIGH)) * row_scale


def solution(mesh):
    split = Mesh(mesh.devices.reshape(-1, 2, mesh.shape["gy"], mesh.shape["gz"]), AXES)
    placed = (P(None, AXES), P())
    return jax.shard_map(
        on_device, mesh=split, in_specs=placed, out_specs=P(None, AXES), check_vma=False
    )
```

time: 186 us -> 138 us (0.74)
  blocking collectives: 84.9 us -> 0 us
  starting transfers between devices: 4.97 us -> 28.4 us
  local copies, waits for them, and re-layouts: 4.11 us -> 15 us
  other arithmetic: 54.1 us -> 48.7 us
  waiting for transfers between devices: 11.5 us -> 16.9 us
  matrix products: 25.6 us -> 28.2 us
    all_to_all x5 -> x0, blocking collectives: 84.9 us -> none  [the longest x1 36.3 us: summed_on_arrival(): lax.all_to_all(tiles, axis, split_axis=0, concat_axis=0, tiled=True)]
    ppermute x0 -> x14, starting transfers between devices: none -> 21.8 us  [shifted(): return lax.ppermute(v, axis, [(i, (i + step) % n) for i in range(n)])]
    ppermute x0 -> x14, waiting for transfers between devices: none -> 15.2 us  [shifted(): return lax.ppermute(v, axis, [(i, (i + step) % n) for i in range(n)])]
    all_to_all x1, waiting for transfers between devices: 11.5 us -> 1.67 us  [summed(): arrived = lax.all_to_all(copies, axis, 0, 0, tiled=True)]
    dynamic_update_slice x0 -> x10, local copies, waits for them, and re-layouts: none -> 7.49 us  [the longest x7 5.73 us: joined(): lax.dynamic_update_slice_in_dim(whole, part, lax.rem(me - k + n, n) * row...]
    mul x1 -> x0, other arithmetic: 4.54 us -> none  [on_device(): return residual * lax.rsqrt(row_power + EPSILON)[:, None]]
    gather x0 -> x1, local copies, waits for them, and re-layouts: none -> 4.52 us  [on_device(): row_power = jnp.diagonal(left) - jnp.sum(across * subspace, axis=1)]
    dot_general x2 -> x5, matrix products: 10.4 us -> 13.1 us  [the longest x1 6.21 us: on_device(): jnp.dot(subspace, loadings, precision=HIGH)]
  transfers between devices with their start and end apart: 1 -> 15, of which waited for: 1 -> 9; matrix products, arithmetic and copies ran while one was open for 7% -> 13% of each run, Pallas kernels for 0% -> 0%
where the time goes in v1:
time: 138 us
  other arithmetic  48.7 us (35%)
  starting transfers between devices  28.4 us (21%)
  matrix products  28.2 us (20%)
  waiting for transfers between devices  16.9 us (12%)
  local copies, waits for them, and re-layouts  15 us (11%)
    another operation x12, other arithmetic, orthonormal(): cholesky_factor = jnp.linalg.cholesky(inner_gram)  26.2 us
    another operation x8, other arithmetic, orthonormal(): jax.scipy.linalg.solve_triangular(cholesky_factor, columns.T, lower=True)  22.2 us
    ppermute x14, starting transfers between devices, shifted(): return lax.ppermute(v, axis, [(i, (i + step) % n) for i in range(n)])  21.8 us
    ppermute x14, waiting for transfers between devices, shifted(): return lax.ppermute(v, axis, [(i, (i + step) % n) for i in range(n)])  15.2 us
    dot_general x1, matrix products, on_device(): local_gram = jnp.dot(phase_stack, phase_stack.T, precision=HIGHEST)  9.34 us
    all_to_all x1, starting transfers between devices, summed(): arrived = lax.all_to_all(copies, axis, 0, 0, tiled=True)  6.6 us
    dot_general x1, matrix products, on_device(): jnp.dot(subspace, loadings, precision=HIGH)  6.21 us
    dynamic_update_slice x7, local copies, waits for them, and re-layouts, joined(): lax.dynamic_update_slice_in_dim(whole, part, lax.rem(me - k + n, n) * row...  5.73 us
  transfers between devices with their start and end apart: 15, of which 9 were waited for; matrix products, arithmetic and copies ran while one was open for 13% of the time, Pallas kernels for 0%

profile of v1, /device:TPU:1, one launch (start us, length us, event | category | flops | bytes accessed | tf_op | source)
XLA Modules:
  0.0 137.8 jit_solution(2896122042690884774)
XLA Ops:
  0.0 9.3 %fusion.29 = f32[512,512]{1,0:T(8,128)S(1)} fusion(f32[512,2048]{1,0:T(8,128)} %param.5), kind=kOutput, calls=%fused_computation.82 | convolution fusion | flops 6442450944 | bytes 5242880 | tf_op jit(solution)/shard_map/dot_general | solution.py:86
  10.5 3.3 %collective-permute-start = (f32[640,128]{1,0:T(8,128)S(1)}, f32[640,128]{1,0:T(8,128)S(1)}, u32[]{:S(2)}, u32[]{:S(2)}) collective-permute-start(f32[640,128]{1,0:T(8,128)S(1)} %constant_dynamic-slice_fusion.6), channel_id=1, source_target_pairs={{0,32},{32,0},{1,33},{33,1},{2,34},{34,2},{3,35},{35,3},{4,36},{36... | collective-permute-start | bytes 983048 | tf_op jit(solution)/shard_map/ppermute | solution.py:17
  13.8 1.3 collective-permute-done
  15.2 2.7 %collective-permute-start.3 = (f32[160,128]{1,0:T(8,128)S(1)}, f32[160,128]{1,0:T(8,128)S(1)}, u32[]{:S(2)}, u32[]{:S(2)}) collective-permute-start(f32[160,128]{1,0:T(8,128)S(1)} %get-tuple-element.33), channel_id=1, source_target_pairs={{0,192},{64,0},{128,64},{192,128},{1,193},{65,1},{129,65},{193,129... | collective-permute-start | bytes 245768 | tf_op jit(solution)/shard_map/ppermute | solution.py:17
  17.9 2.2 %collective-permute-done.1 = f32[160,128]{1,0:T(8,128)S(1)} collective-permute-done((f32[160,128]{1,0:T(8,128)S(1)}, f32[160,128]{1,0:T(8,128)S(1)}, u32[]{:S(2)}, u32[]{:S(2)}) %collective-permute-start.1) | collective-permute-done | bytes 81952 | tf_op jit(solution)/shard_map/ppermute | solution.py:17
  20.1 1.3 collective-permute-done.3
  21.4 1.3 collective-permute-done.2
  22.8 2.7 %collective-permute-start.6 = (f32[40,128]{1,0:T(8,128)S(1)}, f32[40,128]{1,0:T(8,128)S(1)}, u32[]{:S(2)}, u32[]{:S(2)}) collective-permute-start(f32[40,128]{1,0:T(8,128)S(1)} %get-tuple-element.36), channel_id=1, source_target_pairs={{0,24},{8,0},{16,8},{24,16},{1,25},{9,1},{17,9},{25,17},{2,26},{10... | collective-permute-start | bytes 61448 | tf_op jit(solution)/shard_map/ppermute | solution.py:17
  25.8 0.8 collective-permute-done.4
  26.7 3.0 %collective-permute-done.5 = f32[40,128]{1,0:T(8,128)S(1)} collective-permute-done((f32[40,128]{1,0:T(8,128)S(1)}, f32[40,128]{1,0:T(8,128)S(1)}, u32[]{:S(2)}, u32[]{:S(2)}) %collective-permute-start.5) | collective-permute-done | bytes 20512 | tf_op jit(solution)/shard_map/ppermute | solution.py:17
  29.6 0.7 broadcast_in_dim.24
  30.3 6.6 %all-to-all-start = ((f32[8,40,128]{2,1,0:T(8,128)}), f32[8,40,128]{2,1,0:T(8,128)S(1)}, u32[]{:S(2)}, u32[]{:S(2)}) async-start(f32[8,40,128]{2,1,0:T(8,128)} %broadcast_in_dim.24), calls=%async_computation | async-start | bytes 327680 | tf_op jit(solution)/shard_map/all_to_all | solution.py:45
  36.9 5.8 %cholesky.74 = f32[64,64]{1,0:T(8,128)S(1)} custom-call(f32[64,64]{1,0:T(8,128)S(1)} %fusion.20), custom_call_target="Cholesky" | custom-call | tf_op jit(solution)/shard_map/jit(cholesky)/cholesky | solution.py:79
  42.8 0.7 compare_reduce_fusion.3
  43.5 1.7 %all-to-all-done = f32[8,40,128]{2,1,0:T(8,128)S(1)} async-done(((f32[8,40,128]{2,1,0:T(8,128)}), f32[8,40,128]{2,1,0:T(8,128)S(1)}, u32[]{:S(2)}, u32[]{:S(2)}) %all-to-all-start) | async-done | bytes 163872 | tf_op jit(solution)/shard_map/all_to_all | solution.py:45
  45.3 1.5 %collective-permute-start.9 = (f32[40,128]{0,1:T(8,128)S(1)}, f32[40,128]{0,1:T(8,128)S(1)}, u32[]{:S(2)}, u32[]{:S(2)}) collective-permute-start(f32[40,128]{0,1:T(8,128)S(1)} %copy.54), channel_id=1, source_target_pairs={{0,24},{8,0},{16,8},{24,16},{1,25},{9,1},{17,9},{25,17},{2,26},{10... | collective-permute-start | bytes 61448 | tf_op jit(solution)/shard_map/ppermute | solution.py:17
  48.0 0.7 fusion.9
  48.7 4.9 %custom-call.10 = f32[1,64,64]{1,2,0:T(8,128)S(1)} custom-call(f32[1,64,64]{2,1,0:T(8,128)S(1)} %fusion.9), custom_call_target="InvertDiagBlocksLowerTriangular" | custom-call | tf_op jit(solution)/shard_map/jit(_solve_triangular)/triangular_solve | solution.py:80
  53.6 0.7 dynamic_update_slice.30
  54.3 0.8 dynamic_update_slice.31
  55.1 0.8 dynamic_update_slice.32
  56.0 0.8 dynamic_update_slice.33
  56.8 1.6 %collective-permute-start.12 = (f32[160,128]{0,1:T(8,128)S(1)}, f32[160,128]{0,1:T(8,128)S(1)}, u32[]{:S(2)}, u32[]{:S(2)}) collective-permute-start(f32[160,128]{0,1:T(8,128)S(1)} %dynamic_update_slice.33), channel_id=1, source_target_pairs={{0,192},{64,0},{128,64},{192,128},{1,193},{65,1},{129,65},{193,129... | collective-permute-start | bytes 245768 | tf_op jit(solution)/shard_map/ppermute | solution.py:17
  58.4 1.1 collective-permute-start.11
  59.5 1.1 dynamic_update_slice.34
  60.6 4.5 %collective-permute-done.10 = f32[160,128]{0,1:T(8,128)S(1)} collective-permute-done((f32[160,128]{0,1:T(8,128)S(1)}, f32[160,128]{0,1:T(8,128)S(1)}, u32[]{:S(2)}, u32[]{:S(2)}) %collective-permute-start.10) | collective-permute-done | bytes 81952 | tf_op jit(solution)/shard_map/ppermute | solution.py:17
  65.1 0.8 dynamic_update_slice.35
  65.9 1.1 dynamic_update_slice.36
  67.0 1.3 dynamic_update_slice.37
  68.3 7.7 %collective-permute-start.13 = (f32[640,128]{0,1:T(8,128)S(1)}, f32[640,128]{0,1:T(8,128)S(1)}, u32[]{:S(2)}, u32[]{:S(2)}) collective-permute-start(f32[640,128]{0,1:T(8,128)S(1)} %dynamic_update_slice.37), channel_id=1, source_target_pairs={{0,32},{32,0},{1,33},{33,1},{2,34},{34,2},{3,35},{35,3},{4,36},{36... | collective-permute-start | bytes 983048 | tf_op jit(solution)/shard_map/ppermute | solution.py:17
  76.5 0.8 collective-permute-done.13
  78.3 1.1 fusion.31
  79.8 5.8 %cholesky.85 = f32[64,64]{1,0:T(8,128)S(1)} custom-call(f32[64,64]{1,0:T(8,128)S(1)} %fusion.18), custom_call_target="Cholesky" | custom-call | tf_op jit(solution)/shard_map/jit(cholesky)/cholesky | solution.py:79
  86.4 0.7 fusion.10
  87.0 4.9 %custom-call.11 = f32[1,64,64]{1,2,0:T(8,128)S(1)} custom-call(f32[1,64,64]{2,1,0:T(8,128)S(1)} %fusion.10), custom_call_target="InvertDiagBlocksLowerTriangular" | custom-call | tf_op jit(solution)/shard_map/jit(_solve_triangular)/triangular_solve | solution.py:80
  92.3 1.1 fusion.33
  93.8 5.8 %cholesky.96 = f32[64,64]{1,0:T(8,128)S(1)} custom-call(f32[64,64]{1,0:T(8,128)S(1)} %fusion.16), custom_call_target="Cholesky" | custom-call | tf_op jit(solution)/shard_map/jit(cholesky)/cholesky | solution.py:79
  100.9 4.9 %custom-call.12 = f32[1,64,64]{1,2,0:T(8,128)S(1)} custom-call(f32[1,64,64]{2,1,0:T(8,128)S(1)} %fusion.11), custom_call_target="InvertDiagBlocksLowerTriangular" | custom-call | tf_op jit(solution)/shard_map/jit(_solve_triangular)/triangular_solve | solution.py:80
  106.2 1.1 fusion.35
  107.7 5.8 %cholesky.107 = f32[64,64]{1,0:T(8,128)S(1)} custom-call(f32[64,64]{1,0:T(8,128)S(1)} %fusion.14), custom_call_target="Cholesky" | custom-call | tf_op jit(solution)/shard_map/jit(cholesky)/cholesky | solution.py:79
  114.2 0.7 fusion.12
  114.9 4.9 %custom-call.13 = f32[1,64,64]{1,2,0:T(8,128)S(1)} custom-call(f32[1,64,64]{2,1,0:T(8,128)S(1)} %fusion.12), custom_call_target="InvertDiagBlocksLowerTriangular" | custom-call | tf_op jit(solution)/shard_map/jit(_solve_triangular)/triangular_solve | solution.py:80
  120.1 0.8 fusion.38
  120.9 3.6 %fusion.37 = f32[64,2048]{1,0:T(8,128)S(1)} fusion(f32[64,512]{1,0:T(8,128)S(1)} %fusion.1, f32[512,2048]{1,0:T(8,128)} %param.5), kind=kOutput, calls=%fused_computation.90 | convolution fusion | flops 402653184 | bytes 4849664 | tf_op jit(solution)/shard_map/dot_general | solution.py:97
  124.5 1.4 convolution_subtract_fusion
  125.9 1.2 fusion
  127.0 4.5 %gather_fusion = f32[512]{0:T(512)S(1)} fusion(f32[512,512]{1,0:T(8,128)S(1)} %convolution_subtract_fusion, s32[512]{0:T(512)S(1)} %bitcast.123), kind=kCustom, calls=%fused_computation | custom fusion | bytes 8192 | tf_op jit(solution)/shard_map/jit(diagonal)/cond/branch_0_fun/gather | solution.py:95
  131.6 6.2 %subtract_multiply_fusion = f32[512,2048]{1,0:T(8,128)} fusion(f32[512,2048]{1,0:T(8,128)} %param.5, f32[64,512]{1,0:T(8,128)S(1)} %fusion.1, f32[64,2048]{1,0:T(8,128)S(1)} %fusion.37, f32[512]{0:T(512)S(1)} %add_rsqrt_fusion), kind=kOutput, calls=%fused_computation.1 | convolution fusion | flops 404750336 | bytes 9046016 | tf_op jit(solution)/shard_map/dot_general | solution.py:98
  (76 shorter events, 9.0 us)
Async XLA Ops:
  0.0 25.5 %copy-start = (f32[512,64]{0,1:T(8,128)S(1)}, f32[512,64]{0,1:T(8,128)}, u32[]{:S(2)}) copy-start(f32[512,64]{0,1:T(8,128)} %param.6) | copy-start | bytes 393220
  10.5 4.6 %collective-permute-start = (f32[640,128]{1,0:T(8,128)S(1)}, f32[640,128]{1,0:T(8,128)S(1)}, u32[]{:S(2)}, u32[]{:S(2)}) collective-permute-start(f32[640,128]{1,0:T(8,128)S(1)} %constant_dynamic-slice_fusion.6), channel_id=1, source_target_pairs={{0,32},{32,0},{1,33},{33,1},{2,34},{34,2},{3,35},{35,3},{4,36},{36... | collective-permute-start | bytes 983048 | tf_op jit(solution)/shard_map/ppermute | solution.py:17
  15.1 4.9 %collective-permute-start.1 = (f32[160,128]{1,0:T(8,128)S(1)}, f32[160,128]{1,0:T(8,128)S(1)}, u32[]{:S(2)}, u32[]{:S(2)}) collective-permute-start(f32[160,128]{1,0:T(8,128)S(1)} %get-tuple-element.32), channel_id=1, source_target_pairs={{0,64},{64,128},{128,192},{192,0},{1,65},{65,129},{129,193},{193,1... | collective-permute-start | bytes 245768 | tf_op jit(solution)/shard_map/ppermute | solution.py:17
  15.2 6.1 %collective-permute-start.3 = (f32[160,128]{1,0:T(8,128)S(1)}, f32[160,128]{1,0:T(8,128)S(1)}, u32[]{:S(2)}, u32[]{:S(2)}) collective-permute-start(f32[160,128]{1,0:T(8,128)S(1)} %get-tuple-element.33), channel_id=1, source_target_pairs={{0,192},{64,0},{128,64},{192,128},{1,193},{65,1},{129,65},{193,129... | collective-permute-start | bytes 245768 | tf_op jit(solution)/shard_map/ppermute | solution.py:17
  17.9 4.8 %collective-permute-start.2 = (f32[160,128]{1,0:T(8,128)S(1)}, f32[160,128]{1,0:T(8,128)S(1)}, u32[]{:S(2)}, u32[]{:S(2)}) collective-permute-start(f32[160,128]{1,0:T(8,128)S(1)} %get-tuple-element.34), channel_id=1, source_target_pairs={{0,128},{64,192},{128,0},{192,64},{1,129},{65,193},{129,1},{193,65... | collective-permute-start | bytes 245768 | tf_op jit(solution)/shard_map/ppermute | solution.py:17
  22.7 3.9 %collective-permute-start.4 = (f32[40,128]{1,0:T(8,128)S(1)}, f32[40,128]{1,0:T(8,128)S(1)}, u32[]{:S(2)}, u32[]{:S(2)}) collective-permute-start(f32[40,128]{1,0:T(8,128)S(1)} %get-tuple-element.35), channel_id=1, source_target_pairs={{0,8},{8,16},{16,24},{24,0},{1,9},{9,17},{17,25},{25,1},{2,10},{10... | collective-permute-start | bytes 61448 | tf_op jit(solution)/shard_map/ppermute | solution.py:17
  22.8 3.8 %collective-permute-start.6 = (f32[40,128]{1,0:T(8,128)S(1)}, f32[40,128]{1,0:T(8,128)S(1)}, u32[]{:S(2)}, u32[]{:S(2)}) collective-permute-start(f32[40,128]{1,0:T(8,128)S(1)} %get-tuple-element.36), channel_id=1, source_target_pairs={{0,24},{8,0},{16,8},{24,16},{1,25},{9,1},{17,9},{25,17},{2,26},{10... | collective-permute-start | bytes 61448 | tf_op jit(solution)/shard_map/ppermute | solution.py:17
  25.5 4.1 %collective-permute-start.5 = (f32[40,128]{1,0:T(8,128)S(1)}, f32[40,128]{1,0:T(8,128)S(1)}, u32[]{:S(2)}, u32[]{:S(2)}) collective-permute-start(f32[40,128]{1,0:T(8,128)S(1)} %get-tuple-element.37), channel_id=1, source_target_pairs={{0,16},{8,24},{16,0},{24,8},{1,17},{9,25},{17,1},{25,9},{2,18},{10... | collective-permute-start | bytes 61448 | tf_op jit(solution)/shard_map/ppermute | solution.py:17
  30.3 14.9 %all-to-all-start = ((f32[8,40,128]{2,1,0:T(8,128)}), f32[8,40,128]{2,1,0:T(8,128)S(1)}, u32[]{:S(2)}, u32[]{:S(2)}) async-start(f32[8,40,128]{2,1,0:T(8,128)} %broadcast_in_dim.24), calls=%async_computation | async-start | bytes 327680 | tf_op jit(solution)/shard_map/all_to_all | solution.py:45
  45.3 10.7 %collective-permute-start.9 = (f32[40,128]{0,1:T(8,128)S(1)}, f32[40,128]{0,1:T(8,128)S(1)}, u32[]{:S(2)}, u32[]{:S(2)}) collective-permute-start(f32[40,128]{0,1:T(8,128)S(1)} %copy.54), channel_id=1, source_target_pairs={{0,24},{8,0},{16,8},{24,16},{1,25},{9,1},{17,9},{25,17},{2,26},{10... | collective-permute-start | bytes 61448 | tf_op jit(solution)/shard_map/ppermute | solution.py:17
  46.8 8.3 %collective-permute-start.8 = (f32[40,128]{0,1:T(8,128)S(1)}, f32[40,128]{0,1:T(8,128)S(1)}, u32[]{:S(2)}, u32[]{:S(2)}) collective-permute-start(f32[40,128]{0,1:T(8,128)S(1)} %copy.54), channel_id=1, source_target_pairs={{0,16},{8,24},{16,0},{24,8},{1,17},{9,25},{17,1},{25,9},{2,18},{10... | collective-permute-start | bytes 61448 | tf_op jit(solution)/shard_map/ppermute | solution.py:17
  47.4 6.9 %collective-permute-start.7 = (f32[40,128]{0,1:T(8,128)S(1)}, f32[40,128]{0,1:T(8,128)S(1)}, u32[]{:S(2)}, u32[]{:S(2)}) collective-permute-start(f32[40,128]{0,1:T(8,128)S(1)} %copy.54), channel_id=1, source_target_pairs={{0,8},{8,16},{16,24},{24,0},{1,9},{9,17},{17,25},{25,1},{2,10},{10... | collective-permute-start | bytes 61448 | tf_op jit(solution)/shard_map/ppermute | solution.py:17
  56.8 10.2 %collective-permute-start.12 = (f32[160,128]{0,1:T(8,128)S(1)}, f32[160,128]{0,1:T(8,128)S(1)}, u32[]{:S(2)}, u32[]{:S(2)}) collective-permute-start(f32[160,128]{0,1:T(8,128)S(1)} %dynamic_update_slice.33), channel_id=1, source_target_pairs={{0,192},{64,0},{128,64},{192,128},{1,193},{65,1},{129,65},{193,129... | collective-permute-start | bytes 245768 | tf_op jit(solution)/shard_map/ppermute | solution.py:17
  58.4 7.5 %collective-permute-start.11 = (f32[160,128]{0,1:T(8,128)S(1)}, f32[160,128]{0,1:T(8,128)S(1)}, u32[]{:S(2)}, u32[]{:S(2)}) collective-permute-start(f32[160,128]{0,1:T(8,128)S(1)} %dynamic_update_slice.33), channel_id=1, source_target_pairs={{0,128},{64,192},{128,0},{192,64},{1,129},{65,193},{129,1},{193,65... | collective-permute-start | bytes 245768 | tf_op jit(solution)/shard_map/ppermute | solution.py:17
  59.5 5.7 %collective-permute-start.10 = (f32[160,128]{0,1:T(8,128)S(1)}, f32[160,128]{0,1:T(8,128)S(1)}, u32[]{:S(2)}, u32[]{:S(2)}) collective-permute-start(f32[160,128]{0,1:T(8,128)S(1)} %dynamic_update_slice.33), channel_id=1, source_target_pairs={{0,64},{64,128},{128,192},{192,0},{1,65},{65,129},{129,193},{193,1... | collective-permute-start | bytes 245768 | tf_op jit(solution)/shard_map/ppermute | solution.py:17
  68.3 8.9 %collective-permute-start.13 = (f32[640,128]{0,1:T(8,128)S(1)}, f32[640,128]{0,1:T(8,128)S(1)}, u32[]{:S(2)}, u32[]{:S(2)}) collective-permute-start(f32[640,128]{0,1:T(8,128)S(1)} %dynamic_update_slice.37), channel_id=1, source_target_pairs={{0,32},{32,0},{1,33},{33,1},{2,34},{34,2},{3,35},{35,3},{4,36},{36... | collective-permute-start | bytes 983048 | tf_op jit(solution)/shard_map/ppermute | solution.py:17

commit v2 on v1

v2 whole, which is shorter than its diff:
```python
import functools

import jax
import jax.numpy as jnp
from jax import lax
from jax.experimental import pallas as pl
from jax.experimental.pallas import tpu as pltpu
from jax.sharding import Mesh
from jax.sharding import PartitionSpec as P

ITERS = 3
AXES = ("y", "c", "x", "z")
HIGHEST = lax.Precision.HIGHEST
EPSILON = 1e-06
TILE = 128
WIDE = 256
ROWS = 8
F32 = jnp.float32
BF16 = jnp.bfloat16
NT = (((1,), (1,)), ((), ()))


def partner(v, axis, k):
    return lax.ppermute(v, axis, [(i, i ^ k) for i in range(lax.axis_size(axis))])


def share_of_sum(v, axis):
    n, me = lax.axis_size(axis), lax.axis_index(axis)
    rows = v.shape[0] // n
    piece = lambda k: lax.dynamic_slice_in_dim(v, (me ^ k) * rows, rows, 0)
    arrived = [partner(piece(k), axis, k) for k in range(1, n)]
    total = piece(0)
    for part in arrived:
        total = total + part
    return total


def joined(v, axis):
    return jnp.concatenate([v] + [partner(v, axis, k) for k in range(1, lax.axis_size(axis))], axis=0)


def summed(v, axis):
    n = lax.axis_size(axis)
    copies = jnp.broadcast_to(v[None], (n, *v.shape)).reshape(n * v.shape[0], *v.shape[1:])
    arrived = lax.all_to_all(copies, axis, 0, 0, tiled=True)
    return arrived.reshape(n, *v.shape).sum(axis=0)


def sum_everywhere(v):
    v = share_of_sum(v, "c")
    v = share_of_sum(v, "y")
    v = share_of_sum(v, "x")
    v = summed(v, "z")
    v = joined(v, "x")
    v = joined(v, "y")
    return joined(v, "c")


def two_parts(x):
    hi = x.astype(BF16)
    return hi, (x - hi.astype(F32)).astype(BF16)


def three_parts(x):
    hi = x.astype(BF16)
    rest = x - hi.astype(F32)
    mid = rest.astype(BF16)
    return hi, mid, (rest - mid.astype(F32)).astype(BF16)


def dot(a, b):
    return jnp.dot(a, b, preferred_element_type=F32)


def dot_nt(a, b, precision=None):
    return lax.dot_general(a, b, NT, precision=precision, preferred_element_type=F32)


def iota(shape, dim):
    return lax.broadcasted_iota(jnp.int32, shape, dim)


def gram_kernel(x_ref, out_ref, total):
    step = pl.program_id(0)
    m = x_ref.shape[0]

    @pl.when(step == 0)
    def _():
        total[...] = jnp.zeros_like(total)

    hi, lo = two_parts(x_ref[...])
    for j in range(m // WIDE):
        rows, here = slice(0, (j + 1) * WIDE), slice(j * WIDE, (j + 1) * WIDE)
        total[rows, here] += (
            dot_nt(hi[rows], hi[here]) + dot_nt(lo[rows], hi[here]) + dot_nt(hi[rows], lo[here])
        )

    @pl.when(step == pl.num_programs(0) - 1)
    def _():
        place = 0
        for i in range(m // TILE):
            for j in range(i, m // TILE):
                out_ref[place * TILE : (place + 1) * TILE, :] = total[
                    i * TILE : (i + 1) * TILE, j * TILE : (j + 1) * TILE
                ]
                place += 1


def upper_gram(x, chunk=512):
    m, n = x.shape
    tiles = m // TILE
    lines = tiles * (tiles + 1) // 2 * TILE
    return pl.pallas_call(
        gram_kernel,
        out_shape=jax.ShapeDtypeStruct((lines, TILE), F32),
        grid=(n // chunk,),
        in_specs=[pl.BlockSpec((m, chunk), lambda i: (0, i))],
        out_specs=pl.BlockSpec((lines, TILE), lambda i: (0, 0)),
        scratch_shapes=[pltpu.VMEM((m, m), F32)],
        compiler_params=pltpu.CompilerParams(vmem_limit_bytes=32 * 2**20),
        cost_estimate=pl.CostEstimate(flops=6 * m * m * n, bytes_accessed=4 * m * n, transcendentals=0),
        name="gram",
    )(x)


def inverse_factor(b):
    k = b.shape[0]
    blocks = k // ROWS
    eye = (iota((k, k), 0) == iota((k, k), 1)).astype(F32)
    both = jnp.concatenate([b, eye], axis=1)
    line = [both[ROWS * q : ROWS * (q + 1), :] for q in range(blocks)]
    sub = iota((ROWS, 2 * k), 0)
    for p in range(blocks):
        column = {
            (q, i): jnp.broadcast_to(line[q][:, ROWS * p + i : ROWS * p + i + 1], (ROWS, 2 * k))
            for q in range(p, blocks)
            for i in range(ROWS)
        }
        for i in range(ROWS):
            inverse = 1.0 / column[p, i][i : i + 1, :]
            pivot_row = line[p][i : i + 1, :] * inverse
            ahead = {j: column[p, j][i : i + 1, :] * inverse for j in range(i + 1, ROWS)}
            for q in range(p, blocks):
                factor = column[q, i]
                if q == p:
                    factor = jnp.where(sub > i, factor, 0.0)
                for j in range(i + 1, ROWS):
                    column[q, j] = column[q, j] - factor * ahead[j]
                line[q] = line[q] - factor * pivot_row
    both = jnp.concatenate(line, axis=0)
    pivots = jnp.sum(
        jnp.where(iota(both.shape, 0) == iota(both.shape, 1), both, 0.0), axis=1, keepdims=True
    )
    return (both * lax.rsqrt(pivots))[:, k:]


def orthonormal(y):
    return jnp.dot(inverse_factor(dot_nt(y, y, HIGHEST)), y, precision=HIGHEST)


def start_kernel(s_ref, v_ref):
    v_ref[...] = orthonormal(s_ref[...].T)


def start_rows(s):
    m, k = s.shape
    return pl.pallas_call(
        start_kernel,
        out_shape=jax.ShapeDtypeStruct((k, m), F32),
        cost_estimate=pl.CostEstimate(flops=8 * 10**9, bytes_accessed=8 * m * k, transcendentals=0),
        name="start_rows",
    )(s)


def times_gram(v, gram):
    k = v.shape[0]
    v0, v1, v2 = three_parts(v)
    first = dot(jnp.concatenate([v0, v1, v2], axis=0), gram[0][...])
    second = dot(jnp.concatenate([v0, v1], axis=0), gram[1][...])
    third = dot(v0, gram[2][...])
    return first[:k] + (
        (first[k : 2 * k] + second[:k]) + ((first[2 * k :] + second[k:]) + third)
    )


def finish_kernel(pixel_total, chunk, me_ref, lines_ref, v_ref, x_hbm, out_hbm, x, out, ordered, g0, g1, g2, x_sem, out_sem):
    m, n = x_hbm.shape
    k = v_ref.shape[0]
    tiles = m // TILE
    load = pltpu.make_async_copy(x_hbm, x, x_sem)
    load.start()
    slots = 32
    rows = lines_ref.shape[0] // slots
    me = me_ref[0]
    for slot in range(slots):
        place = pl.multiple_of((me ^ slot) * rows, ROWS)
        ordered[pl.ds(place, rows), :] = lines_ref[slot * rows : (slot + 1) * rows, :]

    gram = (g0, g1, g2)
    diagonal = []
    place = 0
    for i in range(tiles):
        for j in range(i, tiles):
            tile = ordered[place * TILE : (place + 1) * TILE, :] * (1.0 / pixel_total)
            place += 1
            at_i, at_j = slice(i * TILE, (i + 1) * TILE), slice(j * TILE, (j + 1) * TILE)
            for ref, part in zip(gram, three_parts(tile)):
                ref[at_i, at_j] = part
            if i == j:
                eye = iota((TILE, TILE), 0) == iota((TILE, TILE), 1)
                diagonal.append(jnp.sum(jnp.where(eye, tile, 0.0), axis=0, keepdims=True))
            else:
                for ref, part in zip(gram, three_parts(tile.T)):
                    ref[at_j, at_i] = part

    v = v_ref[...]
    for sweep in range(ITERS):
        v = orthonormal(times_gram(v, gram))
    w = times_gram(v, gram)
    inner = dot_nt(w, v, HIGHEST)
    twice = jnp.dot(inner, v, precision=HIGHEST) - 2.0 * w
    power = jnp.concatenate(diagonal, axis=1) + jnp.sum(v * twice, axis=0, keepdims=True)
    scale = lax.rsqrt(jnp.maximum(power, 0.0) + EPSILON)
    scale = jnp.concatenate(
        [
            jnp.broadcast_to(scale[:, i * TILE : (i + 1) * TILE], (TILE, TILE)).T
            for i in range(tiles)
        ],
        axis=0,
    )
    q0, q1 = two_parts(v.T)
    spread = jnp.concatenate([q0, q1, q0], axis=1)
    v0, v1 = two_parts(v)
    v01 = jnp.concatenate([v0, v1], axis=0)
    load.wait()
    for c in range(n // chunk):
        here = slice(c * chunk, (c + 1) * chunk)
        xc = x[:, here]
        x0, x1 = two_parts(xc)
        both = dot(v01, x0)
        l0, l1 = two_parts(both[:k] + (both[k:] + dot(v0, x1)))
        common = dot(spread, jnp.concatenate([l0, l0, l1], axis=0))
        for t in range(chunk // TILE):
            at = slice(t * TILE, (t + 1) * TILE)
            out[:, c * chunk + t * TILE : c * chunk + (t + 1) * TILE] = (xc[:, at] - common[:, at]) * scale
        pltpu.make_async_copy(out.at[:, here], out_hbm.at[:, here], out_sem.at[c]).start()
    for c in range(n // chunk):
        here = slice(c * chunk, (c + 1) * chunk)
        pltpu.make_async_copy(out.at[:, here], out_hbm.at[:, here], out_sem.at[c]).wait()


def corrected(lines, me, v, x, pixel_total, chunk=512):
    m, n = x.shape
    k = v.shape[0]
    return pl.pallas_call(
        functools.partial(finish_kernel, pixel_total, chunk),
        out_shape=jax.ShapeDtypeStruct((m, n), F32),
        in_specs=[
            pl.BlockSpec(memory_space=pltpu.SMEM),
            pl.BlockSpec(memory_space=pltpu.VMEM),
            pl.BlockSpec(memory_space=pltpu.VMEM),
            pl.BlockSpec(memory_space=pl.ANY),
        ],
        out_specs=pl.BlockSpec(memory_space=pl.ANY),
        scratch_shapes=[
            pltpu.VMEM((m, n), F32),
            pltpu.VMEM((m, n), F32),
            pltpu.VMEM(lines.shape, F32),
            pltpu.VMEM((m, m), BF16),
            pltpu.VMEM((m, m), BF16),
            pltpu.VMEM((m, m), BF16),
            pltpu.SemaphoreType.DMA,
            pltpu.SemaphoreType.DMA((n // chunk,)),
        ],
        compiler_params=pltpu.CompilerParams(vmem_limit_bytes=48 * 2**20),
        cost_estimate=pl.CostEstimate(flops=12 * m * k * n, bytes_accessed=8 * m * n, transcendentals=0),
        name="finish",
    )(me, lines, v, x)


def on_device(phase_stack, start_basis):
    pixel_total = phase_stack.shape[1] * lax.axis_size(AXES)
    v = start_rows(start_basis)
    lines = sum_everywhere(upper_gram(phase_stack))
    me = (lax.axis_index("c") * 4 + lax.axis_index("y")) * 4 + lax.axis_index("x")
    return corrected(lines, me.astype(jnp.int32).reshape(1), v, phase_stack, pixel_total)


def solution(mesh):
    split = Mesh(mesh.devices.reshape(-1, 2, mesh.shape["gy"], mesh.shape["gz"]), AXES)
    placed = (P(None, AXES), P())
    return jax.shard_map(
        on_device, mesh=split, in_specs=placed, out_specs=P(None, AXES), check_vma=False
    )
```

time: 138 us -> 80.9 us (0.59)
  other arithmetic: 48.7 us -> 0.08 us
  matrix products: 28.2 us -> 0 us
  Pallas kernels: 0 us -> 20 us
  local copies, waits for them, and re-layouts: 15 us -> 6.95 us
  starting transfers between devices: 28.4 us -> 33.3 us
  waiting for transfers between devices: 16.9 us -> 19.9 us
    another operation x20 -> x0, other arithmetic: 48.4 us -> none  [the longest x12 26.2 us: orthonormal(): cholesky_factor = jnp.linalg.cholesky(inner_gram)]
    dot_general x13 -> x0, matrix products: 26.9 us -> none  [the longest x1 9.34 us: on_device(): local_gram = jnp.dot(phase_stack, phase_stack.T, precision=HIGHEST)]
    pallas_call x0 -> x3, Pallas kernels: none -> 20 us  [the longest x1 12.4 us: corrected(): pl.pallas_call(functools.partial(finish_kernel, pixel_total, chunk), out_...]
    dynamic_update_slice x10 -> x0, local copies, waits for them, and re-layouts: 7.49 us -> none  [the longest x7 5.73 us: joined(): lax.dynamic_update_slice_in_dim(whole, part, lax.rem(me - k + n, n) * row...]
    all_to_all x1, waiting for transfers between devices: 1.67 us -> 7.44 us  [summed(): arrived = lax.all_to_all(copies, axis, 0, 0, tiled=True)]
    unnamed x15, local copies, waits for them, and re-layouts: 0.44 us -> 6.16 us
    gather x1 -> x0, local copies, waits for them, and re-layouts: 4.52 us -> none  [on_device(): row_power = jnp.diagonal(left) - jnp.sum(across * subspace, axis=1)]
    ppermute x14, starting transfers between devices: 21.8 us -> 25.1 us  [partner(): lax.ppermute(v, axis, [(i, i ^ k) for i in range(lax.axis_size(axis))])]
  transfers between devices with their start and end apart: 15 -> 15, of which waited for: 9 -> 10; matrix products, arithmetic and copies ran while one was open for 13% -> 1% of each run, Pallas kernels for 0% -> 5%
where the time goes in v2:
time: 80.9 us; the launch traced here: 80.6 us
  starting transfers between devices  33.3 us (41%)
  Pallas kernels  20 us (25%)
  waiting for transfers between devices  19.9 us (25%)
  local copies, waits for them, and re-layouts  6.95 us (9%)
    ppermute x14, starting transfers between devices, partner(): lax.ppermute(v, axis, [(i, i ^ k) for i in range(lax.axis_size(axis))])  25.1 us
    ppermute x14, waiting for transfers between devices, partner(): lax.ppermute(v, axis, [(i, i ^ k) for i in range(lax.axis_size(axis))])  12.5 us
    pallas_call x1, Pallas kernels, corrected(): pl.pallas_call(functools.partial(finish_kernel, pixel_total, chunk), out_...  12.4 us
    all_to_all x1, starting transfers between devices, summed(): arrived = lax.all_to_all(copies, axis, 0, 0, tiled=True)  8.19 us
    all_to_all x1, waiting for transfers between devices, summed(): arrived = lax.all_to_all(copies, axis, 0, 0, tiled=True)  7.44 us
    unnamed x15, local copies, waits for them, and re-layouts  6.16 us
    pallas_call x1, Pallas kernels, start_rows(): pl.pallas_call(start_kernel, out_shape=jax.ShapeDtypeStruct((k, m), F32),...  3.95 us
    pallas_call x1, Pallas kernels, upper_gram(): pl.pallas_call(gram_kernel, out_shape=jax.ShapeDtypeStruct((lines, TILE),...  3.72 us
  transfers between devices with their start and end apart: 15, of which 10 were waited for; matrix products, arithmetic and copies ran while one was open for 1% of the time, Pallas kernels for 5%

profile of v2, /device:TPU:1, one launch (start us, length us, event | category | flops | bytes accessed | tf_op | source)
XLA Modules:
  0.0 80.6 jit_solution(982792735265416275)
XLA Ops:
  0.0 0.0 copy-start
  0.0 2.2 %copy-done = f32[512,2048]{1,0:T(8,128)S(1)} copy-done((f32[512,2048]{1,0:T(8,128)S(1)}, f32[512,2048]{1,0:T(8,128)}, u32[]{:S(2)}) %copy-start) | copy-done | bytes 4194328
  2.2 0.0 copy-start.3
  2.2 3.7 %gram.1 = f32[1280,128]{1,0:T(8,128)S(1)} custom-call(f32[512,2048]{1,0:T(8,128)S(1)} %copy-done), custom_call_target="tpu_custom_call" | custom-call | flops 3221225472 | bytes 4194304 | tf_op jit(solution)/shard_map/gram/pallas_call | solution.py:113
  6.0 3.3 %collective-permute-start = (f32[640,128]{1,0:T(8,128)S(1)}, f32[640,128]{1,0:T(8,128)S(1)}, u32[]{:S(2)}, u32[]{:S(2)}) collective-permute-start(f32[640,128]{1,0:T(8,128)S(1)} %constant_dynamic-slice_fusion.6), channel_id=1, source_target_pairs={{0,32},{32,0},{1,33},{33,1},{2,34},{34,2},{3,35},{35,3},{4,36},{36... | collective-permute-start | bytes 983048 | tf_op jit(solution)/shard_map/ppermute | solution.py:24
  9.3 1.3 %collective-permute-done = f32[640,128]{1,0:T(8,128)S(1)} collective-permute-done((f32[640,128]{1,0:T(8,128)S(1)}, f32[640,128]{1,0:T(8,128)S(1)}, u32[]{:S(2)}, u32[]{:S(2)}) %collective-permute-start) | collective-permute-done | bytes 327712 | tf_op jit(solution)/shard_map/ppermute | solution.py:24
  10.6 0.1 collective-permute-start.1
  10.7 1.5 %collective-permute-start.3 = (f32[160,128]{1,0:T(8,128)S(1)}, f32[160,128]{1,0:T(8,128)S(1)}, u32[]{:S(2)}, u32[]{:S(2)}) collective-permute-start(f32[160,128]{1,0:T(8,128)S(1)} %get-tuple-element.6), channel_id=1, source_target_pairs={{0,192},{64,128},{128,64},{192,0},{1,193},{65,129},{129,65},{193,1... | collective-permute-start | bytes 245768 | tf_op jit(solution)/shard_map/ppermute | solution.py:24
  12.2 1.8 %collective-permute-start.2 = (f32[160,128]{1,0:T(8,128)S(1)}, f32[160,128]{1,0:T(8,128)S(1)}, u32[]{:S(2)}, u32[]{:S(2)}) collective-permute-start(f32[160,128]{1,0:T(8,128)S(1)} %get-tuple-element.7), channel_id=1, source_target_pairs={{0,128},{64,192},{128,0},{192,64},{1,129},{65,193},{129,1},{193,65... | collective-permute-start | bytes 245768 | tf_op jit(solution)/shard_map/ppermute | solution.py:24
  14.0 0.4 collective-permute-done.1
  14.4 1.3 %collective-permute-done.3 = f32[160,128]{1,0:T(8,128)S(1)} collective-permute-done((f32[160,128]{1,0:T(8,128)S(1)}, f32[160,128]{1,0:T(8,128)S(1)}, u32[]{:S(2)}, u32[]{:S(2)}) %collective-permute-start.3) | collective-permute-done | bytes 81952 | tf_op jit(solution)/shard_map/ppermute | solution.py:24
  15.7 1.4 %collective-permute-done.2 = f32[160,128]{1,0:T(8,128)S(1)} collective-permute-done((f32[160,128]{1,0:T(8,128)S(1)}, f32[160,128]{1,0:T(8,128)S(1)}, u32[]{:S(2)}, u32[]{:S(2)}) %collective-permute-start.2) | collective-permute-done | bytes 81952 | tf_op jit(solution)/shard_map/ppermute | solution.py:24
  17.1 1.2 %collective-permute-start.4 = (f32[40,128]{1,0:T(8,128)S(1)}, f32[40,128]{1,0:T(8,128)S(1)}, u32[]{:S(2)}, u32[]{:S(2)}) collective-permute-start(f32[40,128]{1,0:T(8,128)S(1)} %get-tuple-element.14), channel_id=1, source_target_pairs={{0,8},{8,0},{16,24},{24,16},{1,9},{9,1},{17,25},{25,17},{2,10},{10... | collective-permute-start | bytes 61448 | tf_op jit(solution)/shard_map/ppermute | solution.py:24
  18.3 1.8 %collective-permute-start.6 = (f32[40,128]{1,0:T(8,128)S(1)}, f32[40,128]{1,0:T(8,128)S(1)}, u32[]{:S(2)}, u32[]{:S(2)}) collective-permute-start(f32[40,128]{1,0:T(8,128)S(1)} %get-tuple-element.15), channel_id=1, source_target_pairs={{0,24},{8,16},{16,8},{24,0},{1,25},{9,17},{17,9},{25,1},{2,26},{10... | collective-permute-start | bytes 61448 | tf_op jit(solution)/shard_map/ppermute | solution.py:24
  20.1 0.6 collective-permute-start.5
  20.8 0.0 collective-permute-done.4
  20.8 1.4 %collective-permute-done.6 = f32[40,128]{1,0:T(8,128)S(1)} collective-permute-done((f32[40,128]{1,0:T(8,128)S(1)}, f32[40,128]{1,0:T(8,128)S(1)}, u32[]{:S(2)}, u32[]{:S(2)}) %collective-permute-start.6) | collective-permute-done | bytes 20512 | tf_op jit(solution)/shard_map/ppermute | solution.py:24
  22.1 2.1 %collective-permute-done.5 = f32[40,128]{1,0:T(8,128)S(1)} collective-permute-done((f32[40,128]{1,0:T(8,128)S(1)}, f32[40,128]{1,0:T(8,128)S(1)}, u32[]{:S(2)}, u32[]{:S(2)}) %collective-permute-start.5) | collective-permute-done | bytes 20512 | tf_op jit(solution)/shard_map/ppermute | solution.py:24
  24.3 0.7 broadcast_in_dim.2
  25.0 8.2 %all-to-all-start = ((f32[8,40,128]{2,1,0:T(8,128)}), f32[8,40,128]{2,1,0:T(8,128)S(1)}, u32[]{:S(2)}, u32[]{:S(2)}) async-start(f32[8,40,128]{2,1,0:T(8,128)} %broadcast_in_dim.2), calls=%async_computation | async-start | bytes 327680 | tf_op jit(solution)/shard_map/all_to_all | solution.py:45
  33.2 0.0 copy-done.3
  33.2 0.8 %copy.4.s_ref = f32[512,64]{1,0:T(8,128)} copy(f32[512,64]{0,1:T(8,128)S(1)} %copy-done.3) | data formatting | bytes 262144 | tf_op args[1]
  34.0 7.4 %all-to-all-done = f32[8,40,128]{2,1,0:T(8,128)S(1)} async-done(((f32[8,40,128]{2,1,0:T(8,128)}), f32[8,40,128]{2,1,0:T(8,128)S(1)}, u32[]{:S(2)}, u32[]{:S(2)}) %all-to-all-start) | async-done | bytes 163872 | tf_op jit(solution)/shard_map/all_to_all | solution.py:45
  41.4 0.9 %collective-permute-start.9 = (f32[40,128]{1,0:T(8,128)S(1)}, f32[40,128]{1,0:T(8,128)S(1)}, u32[]{:S(2)}, u32[]{:S(2)}) collective-permute-start(f32[40,128]{1,0:T(8,128)S(1)} %reduce_sum.9), channel_id=1, source_target_pairs={{0,24},{8,16},{16,8},{24,0},{1,25},{9,17},{17,9},{25,1},{2,26},{10... | collective-permute-start | bytes 61448 | tf_op jit(solution)/shard_map/ppermute | solution.py:24
  42.4 1.3 %collective-permute-start.8 = (f32[40,128]{1,0:T(8,128)S(1)}, f32[40,128]{1,0:T(8,128)S(1)}, u32[]{:S(2)}, u32[]{:S(2)}) collective-permute-start(f32[40,128]{1,0:T(8,128)S(1)} %reduce_sum.9), channel_id=1, source_target_pairs={{0,16},{8,24},{16,0},{24,8},{1,17},{9,25},{17,1},{25,9},{2,18},{10... | collective-permute-start | bytes 61448 | tf_op jit(solution)/shard_map/ppermute | solution.py:24
  43.7 1.1 %collective-permute-start.7 = (f32[40,128]{1,0:T(8,128)S(1)}, f32[40,128]{1,0:T(8,128)S(1)}, u32[]{:S(2)}, u32[]{:S(2)}) collective-permute-start(f32[40,128]{1,0:T(8,128)S(1)} %reduce_sum.9), channel_id=1, source_target_pairs={{0,8},{8,0},{16,24},{24,16},{1,9},{9,1},{17,25},{25,17},{2,10},{10... | collective-permute-start | bytes 61448 | tf_op jit(solution)/shard_map/ppermute | solution.py:24
  44.8 0.9 %collective-permute-done.9 = f32[40,128]{1,0:T(8,128)S(1)} collective-permute-done((f32[40,128]{1,0:T(8,128)S(1)}, f32[40,128]{1,0:T(8,128)S(1)}, u32[]{:S(2)}, u32[]{:S(2)}) %collective-permute-start.9) | collective-permute-done | bytes 20512 | tf_op jit(solution)/shard_map/ppermute | solution.py:24
  45.7 0.8 %collective-permute-done.8 = f32[40,128]{1,0:T(8,128)S(1)} collective-permute-done((f32[40,128]{1,0:T(8,128)S(1)}, f32[40,128]{1,0:T(8,128)S(1)}, u32[]{:S(2)}, u32[]{:S(2)}) %collective-permute-start.8) | collective-permute-done | bytes 20512 | tf_op jit(solution)/shard_map/ppermute | solution.py:24
  46.5 0.0 collective-permute-done.7
  46.5 1.0 %collective-permute-start.12 = (f32[160,128]{1,0:T(8,128)S(1)}, f32[160,128]{1,0:T(8,128)S(1)}, u32[]{:S(2)}, u32[]{:S(2)}) collective-permute-start(f32[160,128]{1,0:T(8,128)S(1)} %pad_maximum_fusion), channel_id=1, source_target_pairs={{0,192},{64,128},{128,64},{192,0},{1,193},{65,129},{129,65},{193,1... | collective-permute-start | bytes 245768 | tf_op jit(solution)/shard_map/ppermute | solution.py:24
  47.5 1.3 %collective-permute-start.11 = (f32[160,128]{1,0:T(8,128)S(1)}, f32[160,128]{1,0:T(8,128)S(1)}, u32[]{:S(2)}, u32[]{:S(2)}) collective-permute-start(f32[160,128]{1,0:T(8,128)S(1)} %pad_maximum_fusion), channel_id=1, source_target_pairs={{0,128},{64,192},{128,0},{192,64},{1,129},{65,193},{129,1},{193,65... | collective-permute-start | bytes 245768 | tf_op jit(solution)/shard_map/ppermute | solution.py:24
  48.8 1.1 %collective-permute-start.10 = (f32[160,128]{1,0:T(8,128)S(1)}, f32[160,128]{1,0:T(8,128)S(1)}, u32[]{:S(2)}, u32[]{:S(2)}) collective-permute-start(f32[160,128]{1,0:T(8,128)S(1)} %pad_maximum_fusion), channel_id=1, source_target_pairs={{0,64},{64,0},{128,192},{192,128},{1,65},{65,1},{129,193},{193,129... | collective-permute-start | bytes 245768 | tf_op jit(solution)/shard_map/ppermute | solution.py:24
  49.9 2.9 %collective-permute-done.10 = f32[160,128]{1,0:T(8,128)S(1)} collective-permute-done((f32[160,128]{1,0:T(8,128)S(1)}, f32[160,128]{1,0:T(8,128)S(1)}, u32[]{:S(2)}, u32[]{:S(2)}) %collective-permute-start.10) | collective-permute-done | bytes 81952 | tf_op jit(solution)/shard_map/ppermute | solution.py:24
  52.8 0.0 collective-permute-done.11
  52.8 0.0 collective-permute-done.12
  52.9 8.1 %collective-permute-start.13 = (f32[640,128]{1,0:T(8,128)S(1)}, f32[640,128]{1,0:T(8,128)S(1)}, u32[]{:S(2)}, u32[]{:S(2)}) collective-permute-start(f32[640,128]{1,0:T(8,128)S(1)} %get-tuple-element.8), channel_id=1, source_target_pairs={{0,32},{32,0},{1,33},{33,1},{2,34},{34,2},{3,35},{35,3},{4,36},{36... | collective-permute-start | bytes 983048 | tf_op jit(solution)/shard_map/ppermute | solution.py:24
  61.0 3.9 %start_rows.1.v_ref = f32[64,512]{1,0:T(8,128)} custom-call(f32[512,64]{1,0:T(8,128)} %copy.4.s_ref), custom_call_target="tpu_custom_call" | custom-call | flops 8000000000 | bytes 262144 | tf_op jit(solution)/shard_map/start_rows/pallas_call | solution.py:167
  65.0 0.0 collective-permute-done.13
  65.0 0.0 copy-start.1
  65.0 2.2 %copy-done.1 = f32[512,2048]{1,0:T(8,128)S(1)} copy-done((f32[512,2048]{1,0:T(8,128)S(1)}, f32[512,2048]{1,0:T(8,128)}, u32[]{:S(2)}) %copy-start.1) | copy-done | bytes 4194328
  67.2 0.0 copy-start.2
  67.2 0.9 %copy-done.2 = f32[64,512]{1,0:T(8,128)S(1)} copy-done((f32[64,512]{1,0:T(8,128)S(1)}, f32[64,512]{1,0:T(8,128)}, u32[]{:S(2)}) %copy-start.2) | copy-done | bytes 131096
  68.1 12.4 %finish.1 = f32[512,2048]{1,0:T(8,128)} custom-call(s32[1]{0:T(128)} %bitcast.me_ref, f32[1280,128]{1,0:T(8,128)S(1)} %constant_dynamic-update-slice_fusion.7.lines_ref, f32[64,512]{1,0:T(8,128)S(1)} %copy-done.2, f32[512,2048]{1,0:T(8,128)S(1)} %copy-done.1), custom_call_target="tpu_custom_call" | custom-call | flops 805306368 | bytes 8388608 | tf_op jit(solution)/shard_map/finish/pallas_call | solution.py:255
  (16 shorter events, 0.2 us)
Async XLA Ops:
  0.0 2.2 %copy-start = (f32[512,2048]{1,0:T(8,128)S(1)}, f32[512,2048]{1,0:T(8,128)}, u32[]{:S(2)}) copy-start(f32[512,2048]{1,0:T(8,128)} %x_hbm.1) | copy-start | bytes 12582916
  2.2 31.0 %copy-start.3 = (f32[512,64]{0,1:T(8,128)S(1)}, f32[512,64]{0,1:T(8,128)}, u32[]{:S(2)}) copy-start(f32[512,64]{0,1:T(8,128)} %param.3) | copy-start | bytes 393220
  6.0 4.6 %collective-permute-start = (f32[640,128]{1,0:T(8,128)S(1)}, f32[640,128]{1,0:T(8,128)S(1)}, u32[]{:S(2)}, u32[]{:S(2)}) collective-permute-start(f32[640,128]{1,0:T(8,128)S(1)} %constant_dynamic-slice_fusion.6), channel_id=1, source_target_pairs={{0,32},{32,0},{1,33},{33,1},{2,34},{34,2},{3,35},{35,3},{4,36},{36... | collective-permute-start | bytes 983048 | tf_op jit(solution)/shard_map/ppermute | solution.py:24
  10.6 3.7 %collective-permute-start.1 = (f32[160,128]{1,0:T(8,128)S(1)}, f32[160,128]{1,0:T(8,128)S(1)}, u32[]{:S(2)}, u32[]{:S(2)}) collective-permute-start(f32[160,128]{1,0:T(8,128)S(1)} %get-tuple-element.5), channel_id=1, source_target_pairs={{0,64},{64,0},{128,192},{192,128},{1,65},{65,1},{129,193},{193,129... | collective-permute-start | bytes 245768 | tf_op jit(solution)/shard_map/ppermute | solution.py:24
  10.7 5.0 %collective-permute-start.3 = (f32[160,128]{1,0:T(8,128)S(1)}, f32[160,128]{1,0:T(8,128)S(1)}, u32[]{:S(2)}, u32[]{:S(2)}) collective-permute-start(f32[160,128]{1,0:T(8,128)S(1)} %get-tuple-element.6), channel_id=1, source_target_pairs={{0,192},{64,128},{128,64},{192,0},{1,193},{65,129},{129,65},{193,1... | collective-permute-start | bytes 245768 | tf_op jit(solution)/shard_map/ppermute | solution.py:24
  12.2 4.9 %collective-permute-start.2 = (f32[160,128]{1,0:T(8,128)S(1)}, f32[160,128]{1,0:T(8,128)S(1)}, u32[]{:S(2)}, u32[]{:S(2)}) collective-permute-start(f32[160,128]{1,0:T(8,128)S(1)} %get-tuple-element.7), channel_id=1, source_target_pairs={{0,128},{64,192},{128,0},{192,64},{1,129},{65,193},{129,1},{193,65... | collective-permute-start | bytes 245768 | tf_op jit(solution)/shard_map/ppermute | solution.py:24
  17.1 3.7 %collective-permute-start.4 = (f32[40,128]{1,0:T(8,128)S(1)}, f32[40,128]{1,0:T(8,128)S(1)}, u32[]{:S(2)}, u32[]{:S(2)}) collective-permute-start(f32[40,128]{1,0:T(8,128)S(1)} %get-tuple-element.14), channel_id=1, source_target_pairs={{0,8},{8,0},{16,24},{24,16},{1,9},{9,1},{17,25},{25,17},{2,10},{10... | collective-permute-start | bytes 61448 | tf_op jit(solution)/shard_map/ppermute | solution.py:24
  18.3 3.8 %collective-permute-start.6 = (f32[40,128]{1,0:T(8,128)S(1)}, f32[40,128]{1,0:T(8,128)S(1)}, u32[]{:S(2)}, u32[]{:S(2)}) collective-permute-start(f32[40,128]{1,0:T(8,128)S(1)} %get-tuple-element.15), channel_id=1, source_target_pairs={{0,24},{8,16},{16,8},{24,0},{1,25},{9,17},{17,9},{25,1},{2,26},{10... | collective-permute-start | bytes 61448 | tf_op jit(solution)/shard_map/ppermute | solution.py:24
  20.1 4.1 %collective-permute-start.5 = (f32[40,128]{1,0:T(8,128)S(1)}, f32[40,128]{1,0:T(8,128)S(1)}, u32[]{:S(2)}, u32[]{:S(2)}) collective-permute-start(f32[40,128]{1,0:T(8,128)S(1)} %get-tuple-element.16), channel_id=1, source_target_pairs={{0,16},{8,24},{16,0},{24,8},{1,17},{9,25},{17,1},{25,9},{2,18},{10... | collective-permute-start | bytes 61448 | tf_op jit(solution)/shard_map/ppermute | solution.py:24
  25.0 16.5 %all-to-all-start = ((f32[8,40,128]{2,1,0:T(8,128)}), f32[8,40,128]{2,1,0:T(8,128)S(1)}, u32[]{:S(2)}, u32[]{:S(2)}) async-start(f32[8,40,128]{2,1,0:T(8,128)} %broadcast_in_dim.2), calls=%async_computation | async-start | bytes 327680 | tf_op jit(solution)/shard_map/all_to_all | solution.py:45
  41.4 4.2 %collective-permute-start.9 = (f32[40,128]{1,0:T(8,128)S(1)}, f32[40,128]{1,0:T(8,128)S(1)}, u32[]{:S(2)}, u32[]{:S(2)}) collective-permute-start(f32[40,128]{1,0:T(8,128)S(1)} %reduce_sum.9), channel_id=1, source_target_pairs={{0,24},{8,16},{16,8},{24,0},{1,25},{9,17},{17,9},{25,1},{2,26},{10... | collective-permute-start | bytes 61448 | tf_op jit(solution)/shard_map/ppermute | solution.py:24
  42.4 4.1 %collective-permute-start.8 = (f32[40,128]{1,0:T(8,128)S(1)}, f32[40,128]{1,0:T(8,128)S(1)}, u32[]{:S(2)}, u32[]{:S(2)}) collective-permute-start(f32[40,128]{1,0:T(8,128)S(1)} %reduce_sum.9), channel_id=1, source_target_pairs={{0,16},{8,24},{16,0},{24,8},{1,17},{9,25},{17,1},{25,9},{2,18},{10... | collective-permute-start | bytes 61448 | tf_op jit(solution)/shard_map/ppermute | solution.py:24
  43.7 2.8 %collective-permute-start.7 = (f32[40,128]{1,0:T(8,128)S(1)}, f32[40,128]{1,0:T(8,128)S(1)}, u32[]{:S(2)}, u32[]{:S(2)}) collective-permute-start(f32[40,128]{1,0:T(8,128)S(1)} %reduce_sum.9), channel_id=1, source_target_pairs={{0,8},{8,0},{16,24},{24,16},{1,9},{9,1},{17,25},{25,17},{2,10},{10... | collective-permute-start | bytes 61448 | tf_op jit(solution)/shard_map/ppermute | solution.py:24
  46.5 6.3 %collective-permute-start.12 = (f32[160,128]{1,0:T(8,128)S(1)}, f32[160,128]{1,0:T(8,128)S(1)}, u32[]{:S(2)}, u32[]{:S(2)}) collective-permute-start(f32[160,128]{1,0:T(8,128)S(1)} %pad_maximum_fusion), channel_id=1, source_target_pairs={{0,192},{64,128},{128,64},{192,0},{1,193},{65,129},{129,65},{193,1... | collective-permute-start | bytes 245768 | tf_op jit(solution)/shard_map/ppermute | solution.py:24
  47.5 5.3 %collective-permute-start.11 = (f32[160,128]{1,0:T(8,128)S(1)}, f32[160,128]{1,0:T(8,128)S(1)}, u32[]{:S(2)}, u32[]{:S(2)}) collective-permute-start(f32[160,128]{1,0:T(8,128)S(1)} %pad_maximum_fusion), channel_id=1, source_target_pairs={{0,128},{64,192},{128,0},{192,64},{1,129},{65,193},{129,1},{193,65... | collective-permute-start | bytes 245768 | tf_op jit(solution)/shard_map/ppermute | solution.py:24
  48.8 4.0 %collective-permute-start.10 = (f32[160,128]{1,0:T(8,128)S(1)}, f32[160,128]{1,0:T(8,128)S(1)}, u32[]{:S(2)}, u32[]{:S(2)}) collective-permute-start(f32[160,128]{1,0:T(8,128)S(1)} %pad_maximum_fusion), channel_id=1, source_target_pairs={{0,64},{64,0},{128,192},{192,128},{1,65},{65,1},{129,193},{193,129... | collective-permute-start | bytes 245768 | tf_op jit(solution)/shard_map/ppermute | solution.py:24
  52.9 12.1 %collective-permute-start.13 = (f32[640,128]{1,0:T(8,128)S(1)}, f32[640,128]{1,0:T(8,128)S(1)}, u32[]{:S(2)}, u32[]{:S(2)}) collective-permute-start(f32[640,128]{1,0:T(8,128)S(1)} %get-tuple-element.8), channel_id=1, source_target_pairs={{0,32},{32,0},{1,33},{33,1},{2,34},{34,2},{3,35},{35,3},{4,36},{36... | collective-permute-start | bytes 983048 | tf_op jit(solution)/shard_map/ppermute | solution.py:24
  65.0 2.2 %copy-start.1 = (f32[512,2048]{1,0:T(8,128)S(1)}, f32[512,2048]{1,0:T(8,128)}, u32[]{:S(2)}) copy-start(f32[512,2048]{1,0:T(8,128)} %x_hbm.1) | copy-start | bytes 12582916
  67.2 0.9 %copy-start.2 = (f32[64,512]{1,0:T(8,128)S(1)}, f32[64,512]{1,0:T(8,128)}, u32[]{:S(2)}) copy-start(f32[64,512]{1,0:T(8,128)} %start_rows.1.v_ref) | copy-start | bytes 393220

commit v3 on v2

--- a/solution.py
+++ b/solution.py
@@ -1,4 +1,6 @@
 import functools
+import itertools
+import math
 
 import jax
 import jax.numpy as jnp
@@ -10,25 +12,28 @@
 
 ITERS = 3
 AXES = ("y", "c", "x", "z")
+SHARED = ("c", "y", "x")
 HIGHEST = lax.Precision.HIGHEST
 EPSILON = 1e-06
 TILE = 128
 WIDE = 256
 ROWS = 8
+VMEM = 50 * 2**20
 F32 = jnp.float32
 BF16 = jnp.bfloat16
 NT = (((1,), (1,)), ((), ()))
 
 
-def partner(v, axis, k):
-    return lax.ppermute(v, axis, [(i, i ^ k) for i in range(lax.axis_size(axis))])
+def shifted(v, axis, k):
+    n = lax.axis_size(axis)
+    return lax.ppermute(v, axis, [(i, (i + k) % n) for i in range(n)])
 
 
 def share_of_sum(v, axis):
     n, me = lax.axis_size(axis), lax.axis_index(axis)
     rows = v.shape[0] // n
-    piece = lambda k: lax.dynamic_slice_in_dim(v, (me ^ k) * rows, rows, 0)
-    arrived = [partner(piece(k), axis, k) for k in range(1, n)]
+    piece = lambda k: lax.dynamic_slice_in_dim(v, lax.rem(me + k, n) * rows, rows, 0)
+    arrived = [shifted(piece(k), axis, k) for k in range(1, n)]
     total = piece(0)
     for part in arrived:
         total = total + part
@@ -36,7 +41,7 @@
 
 
 def joined(v, axis):
-    return jnp.concatenate([v] + [partner(v, axis, k) for k in range(1, lax.axis_size(axis))], axis=0)
+    return jnp.concatenate([v] + [shifted(v, axis, k) for k in range(1, lax.axis_size(axis))], axis=0)
 
 
 def summed(v, axis):
@@ -46,14 +51,13 @@
     return arrived.reshape(n, *v.shape).sum(axis=0)
 
 
-def sum_everywhere(v):
-    v = share_of_sum(v, "c")
-    v = share_of_sum(v, "y")
-    v = share_of_sum(v, "x")
-    v = summed(v, "z")
-    v = joined(v, "x")
-    v = joined(v, "y")
-    return joined(v, "c")
+def sum_everywhere(v, meanwhile):
+    for axis in SHARED:
+        v = share_of_sum(v, axis)
+    v, meanwhile = lax.optimization_barrier((summed(v, "z"), meanwhile))
+    for axis in reversed(SHARED):
+        v = joined(v, axis)
+    return v, meanwhile
 
 
 def two_parts(x):
@@ -117,7 +121,7 @@
         in_specs=[pl.BlockSpec((m, chunk), lambda i: (0, i))],
         out_specs=pl.BlockSpec((lines, TILE), lambda i: (0, 0)),
         scratch_shapes=[pltpu.VMEM((m, m), F32)],
-        compiler_params=pltpu.CompilerParams(vmem_limit_bytes=32 * 2**20),
+        compiler_params=pltpu.CompilerParams(vmem_limit_bytes=VMEM),
         cost_estimate=pl.CostEstimate(flops=6 * m * m * n, bytes_accessed=4 * m * n, transcendentals=0),
         name="gram",
     )(x)
@@ -159,11 +163,11 @@
 
 
 def start_kernel(s_ref, v_ref):
-    v_ref[...] = orthonormal(s_ref[...].T)
+    v_ref[...] = orthonormal(s_ref[...])
 
 
 def start_rows(s):
-    m, k = s.shape
+    k, m = s.shape
     return pl.pallas_call(
         start_kernel,
         out_shape=jax.ShapeDtypeStruct((k, m), F32),
@@ -183,17 +187,19 @@
     )
 
 
-def finish_kernel(pixel_total, chunk, me_ref, lines_ref, v_ref, x_hbm, out_hbm, x, out, ordered, g0, g1, g2, x_sem, out_sem):
+def finish_kernel(pixel_total, chunk, sizes, me_ref, lines_ref, v_ref, x_hbm, out_hbm, x, out, ordered, g0, g1, g2, x_sem, out_sem):
     m, n = x_hbm.shape
     k = v_ref.shape[0]
     tiles = m // TILE
     load = pltpu.make_async_copy(x_hbm, x, x_sem)
     load.start()
-    slots = 32
+    slots = math.prod(sizes)
     rows = lines_ref.shape[0] // slots
-    me = me_ref[0]
-    for slot in range(slots):
-        place = pl.multiple_of((me ^ slot) * rows, ROWS)
+    for slot, back in enumerate(itertools.product(*map(range, sizes))):
+        place = 0
+        for axis, (size, hops) in enumerate(zip(sizes, back)):
+            place = place * size + lax.rem(me_ref[axis] + (size - hops), size)
+        place = pl.multiple_of(place * rows, ROWS)
         ordered[pl.ds(place, rows), :] = lines_ref[slot * rows : (slot + 1) * rows, :]
 
     gram = (g0, g1, g2)
@@ -249,11 +255,11 @@
         pltpu.make_async_copy(out.at[:, here], out_hbm.at[:, here], out_sem.at[c]).wait()
 
 
-def corrected(lines, me, v, x, pixel_total, chunk=512):
+def corrected(lines, me, sizes, v, x, pixel_total, chunk=512):
     m, n = x.shape
     k = v.shape[0]
     return pl.pallas_call(
-        functools.partial(finish_kernel, pixel_total, chunk),
+        functools.partial(finish_kernel, pixel_total, chunk, sizes),
         out_shape=jax.ShapeDtypeStruct((m, n), F32),
         in_specs=[
             pl.BlockSpec(memory_space=pltpu.SMEM),
@@ -272,7 +278,7 @@
             pltpu.SemaphoreType.DMA,
             pltpu.SemaphoreType.DMA((n // chunk,)),
         ],
-        compiler_params=pltpu.CompilerParams(vmem_limit_bytes=48 * 2**20),
+        compiler_params=pltpu.CompilerParams(vmem_limit_bytes=VMEM),
         cost_estimate=pl.CostEstimate(flops=12 * m * k * n, bytes_accessed=8 * m * n, transcendentals=0),
         name="finish",
     )(me, lines, v, x)
@@ -280,10 +286,10 @@
 
 def on_device(phase_stack, start_basis):
     pixel_total = phase_stack.shape[1] * lax.axis_size(AXES)
-    v = start_rows(start_basis)
-    lines = sum_everywhere(upper_gram(phase_stack))
-    me = (lax.axis_index("c") * 4 + lax.axis_index("y")) * 4 + lax.axis_index("x")
-    return corrected(lines, me.astype(jnp.int32).reshape(1), v, phase_stack, pixel_total)
+    lines, v = sum_everywhere(upper_gram(phase_stack), start_rows(start_basis.T))
+    me = jnp.stack([lax.axis_index(axis) for axis in SHARED]).astype(jnp.int32)
+    sizes = tuple(lax.axis_size(axis) for axis in SHARED)
+    return corrected(lines, me, sizes, v, phase_stack, pixel_total)
 
 
 def solution(mesh):

time: 80.9 us -> 77.3 us (0.956)
  local copies, waits for them, and re-layouts: 6.95 us -> 1.74 us
  waiting for transfers between devices: 19.9 us -> 23.5 us
  starting transfers between devices: 33.3 us -> 29.7 us
  Pallas kernels: 20 us -> 21.6 us
    ppermute x14, waiting for transfers between devices: 12.5 us -> 19 us  [shifted(): return lax.ppermute(v, axis, [(i, (i + k) % n) for i in range(n)])]
    unnamed x15 -> x8, local copies, waits for them, and re-layouts: 6.16 us -> 0.95 us
    all_to_all x1, waiting for transfers between devices: 7.44 us -> 4.46 us  [summed(): arrived = lax.all_to_all(copies, axis, 0, 0, tiled=True)]
    ppermute x14, starting transfers between devices: 25.1 us -> 23.1 us  [shifted(): return lax.ppermute(v, axis, [(i, (i + k) % n) for i in range(n)])]
    all_to_all x1, starting transfers between devices: 8.19 us -> 6.6 us  [summed(): arrived = lax.all_to_all(copies, axis, 0, 0, tiled=True)]
    pallas_call x1, Pallas kernels: 3.72 us -> 5.12 us  [upper_gram(): pl.pallas_call(gram_kernel, out_shape=jax.ShapeDtypeStruct((lines, TILE),...]
  transfers between devices with their start and end apart: 15 -> 15, of which waited for: 10 -> 11; matrix products, arithmetic and copies ran while one was open for 1% -> 0% of each run, Pallas kernels for 5% -> 5%
where the time goes in v3:
time: 77.3 us; the launch traced here: 77 us
  starting transfers between devices  29.7 us (38%)
  waiting for transfers between devices  23.5 us (30%)
  Pallas kernels  21.6 us (28%)
  local copies, waits for them, and re-layouts  1.74 us (2%)
    ppermute x14, starting transfers between devices, shifted(): return lax.ppermute(v, axis, [(i, (i + k) % n) for i in range(n)])  23.1 us
    ppermute x14, waiting for transfers between devices, shifted(): return lax.ppermute(v, axis, [(i, (i + k) % n) for i in range(n)])  19 us
    pallas_call x1, Pallas kernels, corrected(): pl.pallas_call(functools.partial(finish_kernel, pixel_total, chunk, sizes...  12.7 us
    all_to_all x1, starting transfers between devices, summed(): arrived = lax.all_to_all(copies, axis, 0, 0, tiled=True)  6.6 us
    pallas_call x1, Pallas kernels, upper_gram(): pl.pallas_call(gram_kernel, out_shape=jax.ShapeDtypeStruct((lines, TILE),...  5.12 us
    all_to_all x1, waiting for transfers between devices, summed(): arrived = lax.all_to_all(copies, axis, 0, 0, tiled=True)  4.46 us
    pallas_call x1, Pallas kernels, start_rows(): pl.pallas_call(start_kernel, out_shape=jax.ShapeDtypeStruct((k, m), F32),...  3.83 us
  transfers between devices with their start and end apart: 15, of which 11 were waited for; matrix products, arithmetic and copies ran while one was open for 0% of the time, Pallas kernels for 5%

profile of v3, /device:TPU:1, one launch (start us, length us, event | category | flops | bytes accessed | tf_op | source)
XLA Modules:
  0.0 77.0 jit_solution(17832387568696480632)
XLA Ops:
  0.0 5.1 %gram.1 = f32[1280,128]{1,0:T(8,128)S(1)} custom-call(f32[512,2048]{1,0:T(8,128)} %x_hbm.1), custom_call_target="tpu_custom_call" | custom-call | flops 3221225472 | bytes 4194304 | tf_op jit(solution)/shard_map/gram/pallas_call | solution.py:117
  5.2 3.3 %collective-permute-start = (f32[640,128]{1,0:T(8,128)S(1)}, f32[640,128]{1,0:T(8,128)S(1)}, u32[]{:S(2)}, u32[]{:S(2)}) collective-permute-start(f32[640,128]{1,0:T(8,128)S(1)} %constant_dynamic-slice_fusion.6), channel_id=1, source_target_pairs={{0,32},{32,0},{1,33},{33,1},{2,34},{34,2},{3,35},{35,3},{4,36},{36... | collective-permute-start | bytes 983048 | tf_op jit(solution)/shard_map/ppermute | solution.py:29
  8.5 1.3 %collective-permute-done = f32[640,128]{1,0:T(8,128)S(1)} collective-permute-done((f32[640,128]{1,0:T(8,128)S(1)}, f32[640,128]{1,0:T(8,128)S(1)}, u32[]{:S(2)}, u32[]{:S(2)}) %collective-permute-start) | collective-permute-done | bytes 327712 | tf_op jit(solution)/shard_map/ppermute | solution.py:29
  9.8 0.1 collective-permute-start.1
  9.9 2.7 %collective-permute-start.3 = (f32[160,128]{1,0:T(8,128)S(1)}, f32[160,128]{1,0:T(8,128)S(1)}, u32[]{:S(2)}, u32[]{:S(2)}) collective-permute-start(f32[160,128]{1,0:T(8,128)S(1)} %get-tuple-element.10), channel_id=1, source_target_pairs={{0,192},{64,0},{128,64},{192,128},{1,193},{65,1},{129,65},{193,129... | collective-permute-start | bytes 245768 | tf_op jit(solution)/shard_map/ppermute | solution.py:29
  12.6 0.0 collective-permute-start.2
  12.6 2.2 %collective-permute-done.1 = f32[160,128]{1,0:T(8,128)S(1)} collective-permute-done((f32[160,128]{1,0:T(8,128)S(1)}, f32[160,128]{1,0:T(8,128)S(1)}, u32[]{:S(2)}, u32[]{:S(2)}) %collective-permute-start.1) | collective-permute-done | bytes 81952 | tf_op jit(solution)/shard_map/ppermute | solution.py:29
  14.8 1.3 %collective-permute-done.3 = f32[160,128]{1,0:T(8,128)S(1)} collective-permute-done((f32[160,128]{1,0:T(8,128)S(1)}, f32[160,128]{1,0:T(8,128)S(1)}, u32[]{:S(2)}, u32[]{:S(2)}) %collective-permute-start.3) | collective-permute-done | bytes 81952 | tf_op jit(solution)/shard_map/ppermute | solution.py:29
  16.0 1.3 %collective-permute-done.2 = f32[160,128]{1,0:T(8,128)S(1)} collective-permute-done((f32[160,128]{1,0:T(8,128)S(1)}, f32[160,128]{1,0:T(8,128)S(1)}, u32[]{:S(2)}, u32[]{:S(2)}) %collective-permute-start.2) | collective-permute-done | bytes 81952 | tf_op jit(solution)/shard_map/ppermute | solution.py:29
  17.4 0.1 collective-permute-start.4
  17.5 2.7 %collective-permute-start.6 = (f32[40,128]{1,0:T(8,128)S(1)}, f32[40,128]{1,0:T(8,128)S(1)}, u32[]{:S(2)}, u32[]{:S(2)}) collective-permute-start(f32[40,128]{1,0:T(8,128)S(1)} %get-tuple-element.19), channel_id=1, source_target_pairs={{0,24},{8,0},{16,8},{24,16},{1,25},{9,1},{17,9},{25,17},{2,26},{10... | collective-permute-start | bytes 61448 | tf_op jit(solution)/shard_map/ppermute | solution.py:29
  20.2 0.0 collective-permute-start.5
  20.2 1.2 %collective-permute-done.4 = f32[40,128]{1,0:T(8,128)S(1)} collective-permute-done((f32[40,128]{1,0:T(8,128)S(1)}, f32[40,128]{1,0:T(8,128)S(1)}, u32[]{:S(2)}, u32[]{:S(2)}) %collective-permute-start.4) | collective-permute-done | bytes 20512 | tf_op jit(solution)/shard_map/ppermute | solution.py:29
  21.3 0.0 collective-permute-done.6
  21.4 3.0 %collective-permute-done.5 = f32[40,128]{1,0:T(8,128)S(1)} collective-permute-done((f32[40,128]{1,0:T(8,128)S(1)}, f32[40,128]{1,0:T(8,128)S(1)}, u32[]{:S(2)}, u32[]{:S(2)}) %collective-permute-start.5) | collective-permute-done | bytes 20512 | tf_op jit(solution)/shard_map/ppermute | solution.py:29
  24.3 0.7 broadcast_in_dim.2
  25.0 6.6 %all-to-all-start = ((f32[8,40,128]{2,1,0:T(8,128)}), f32[8,40,128]{2,1,0:T(8,128)S(1)}, u32[]{:S(2)}, u32[]{:S(2)}) async-start(f32[8,40,128]{2,1,0:T(8,128)} %broadcast_in_dim.2), calls=%async_computation | async-start | bytes 327680 | tf_op jit(solution)/shard_map/all_to_all | solution.py:50
  31.6 3.8 %start_rows.1.v_ref = f32[64,512]{1,0:T(8,128)} custom-call(f32[64,512]{1,0:T(8,128)} %bitcast.4), custom_call_target="tpu_custom_call" | custom-call | flops 8000000000 | bytes 262144 | tf_op jit(solution)/shard_map/start_rows/pallas_call | solution.py:171
  35.4 4.5 %all-to-all-done = f32[8,40,128]{2,1,0:T(8,128)S(1)} async-done(((f32[8,40,128]{2,1,0:T(8,128)}), f32[8,40,128]{2,1,0:T(8,128)S(1)}, u32[]{:S(2)}, u32[]{:S(2)}) %all-to-all-start) | async-done | bytes 163872 | tf_op jit(solution)/shard_map/all_to_all | solution.py:50
  39.9 1.3 %collective-permute-start.9 = (f32[40,128]{1,0:T(8,128)S(1)}, f32[40,128]{1,0:T(8,128)S(1)}, u32[]{:S(2)}, u32[]{:S(2)}) collective-permute-start(f32[40,128]{1,0:T(8,128)S(1)} %reduce_sum.9), channel_id=1, source_target_pairs={{0,24},{8,0},{16,8},{24,16},{1,25},{9,1},{17,9},{25,17},{2,26},{10... | collective-permute-start | bytes 61448 | tf_op jit(solution)/shard_map/ppermute | solution.py:29
  41.3 0.5 collective-permute-start.8
  41.8 0.6 collective-permute-start.7
  42.4 3.2 %collective-permute-done.7 = f32[40,128]{1,0:T(8,128)S(1)} collective-permute-done((f32[40,128]{1,0:T(8,128)S(1)}, f32[40,128]{1,0:T(8,128)S(1)}, u32[]{:S(2)}, u32[]{:S(2)}) %collective-permute-start.7) | collective-permute-done | bytes 20512 | tf_op jit(solution)/shard_map/ppermute | solution.py:29
  45.6 0.0 collective-permute-done.8
  45.6 0.0 collective-permute-done.9
  45.7 0.8 %collective-permute-start.10 = (f32[160,128]{1,0:T(8,128)S(1)}, f32[160,128]{1,0:T(8,128)S(1)}, u32[]{:S(2)}, u32[]{:S(2)}) collective-permute-start(f32[160,128]{1,0:T(8,128)S(1)} %get-tuple-element.23), channel_id=1, source_target_pairs={{0,64},{64,128},{128,192},{192,0},{1,65},{65,129},{129,193},{193,1... | collective-permute-start | bytes 245768 | tf_op jit(solution)/shard_map/ppermute | solution.py:29
  46.5 1.9 %collective-permute-start.12 = (f32[160,128]{1,0:T(8,128)S(1)}, f32[160,128]{1,0:T(8,128)S(1)}, u32[]{:S(2)}, u32[]{:S(2)}) collective-permute-start(f32[160,128]{1,0:T(8,128)S(1)} %get-tuple-element.23), channel_id=1, source_target_pairs={{0,192},{64,0},{128,64},{192,128},{1,193},{65,1},{129,65},{193,129... | collective-permute-start | bytes 245768 | tf_op jit(solution)/shard_map/ppermute | solution.py:29
  48.4 0.3 collective-permute-start.11
  48.8 1.5 %collective-permute-done.10 = f32[160,128]{1,0:T(8,128)S(1)} collective-permute-done((f32[160,128]{1,0:T(8,128)S(1)}, f32[160,128]{1,0:T(8,128)S(1)}, u32[]{:S(2)}, u32[]{:S(2)}) %collective-permute-start.10) | collective-permute-done | bytes 81952 | tf_op jit(solution)/shard_map/ppermute | solution.py:29
  50.3 3.0 %collective-permute-done.11 = f32[160,128]{1,0:T(8,128)S(1)} collective-permute-done((f32[160,128]{1,0:T(8,128)S(1)}, f32[160,128]{1,0:T(8,128)S(1)}, u32[]{:S(2)}, u32[]{:S(2)}) %collective-permute-start.11) | collective-permute-done | bytes 81952 | tf_op jit(solution)/shard_map/ppermute | solution.py:29
  53.2 0.0 collective-permute-done.12
  53.3 8.8 %collective-permute-start.13 = (f32[640,128]{1,0:T(8,128)S(1)}, f32[640,128]{1,0:T(8,128)S(1)}, u32[]{:S(2)}, u32[]{:S(2)}) collective-permute-start(f32[640,128]{1,0:T(8,128)S(1)} %get-tuple-element.12), channel_id=1, source_target_pairs={{0,32},{32,0},{1,33},{33,1},{2,34},{34,2},{3,35},{35,3},{4,36},{36... | collective-permute-start | bytes 983048 | tf_op jit(solution)/shard_map/ppermute | solution.py:29
  62.0 0.1 pad_add_fusion.me_ref
  62.1 1.2 %collective-permute-done.13 = f32[640,128]{1,0:T(8,128)S(1)} collective-permute-done((f32[640,128]{1,0:T(8,128)S(1)}, f32[640,128]{1,0:T(8,128)S(1)}, u32[]{:S(2)}, u32[]{:S(2)}) %collective-permute-start.13) | collective-permute-done | bytes 327712 | tf_op jit(solution)/shard_map/ppermute | solution.py:29
  63.3 0.0 copy-start
  63.3 0.9 %copy-done = f32[64,512]{1,0:T(8,128)S(1)} copy-done((f32[64,512]{1,0:T(8,128)S(1)}, f32[64,512]{1,0:T(8,128)}, u32[]{:S(2)}) %copy-start) | copy-done | bytes 131096
  64.2 12.7 %finish.1 = f32[512,2048]{1,0:T(8,128)} custom-call(s32[3]{0:T(128)S(1)} %pad_add_fusion.me_ref, f32[1280,128]{1,0:T(8,128)S(1)} %constant_dynamic-update-slice_fusion.11.lines_ref, f32[64,512]{1,0:T(8,128)S(1)} %copy-done, f32[512,2048]{1,0:T(8,128)} %x_hbm.1), custom_call_target="tpu_custom_call" | custom-call | flops 805306368 | bytes 8388608 | tf_op jit(solution)/shard_map/finish/pallas_call | solution.py:261
  (15 shorter events, 0.2 us)
Async XLA Ops:
  5.2 4.6 %collective-permute-start = (f32[640,128]{1,0:T(8,128)S(1)}, f32[640,128]{1,0:T(8,128)S(1)}, u32[]{:S(2)}, u32[]{:S(2)}) collective-permute-start(f32[640,128]{1,0:T(8,128)S(1)} %constant_dynamic-slice_fusion.6), channel_id=1, source_target_pairs={{0,32},{32,0},{1,33},{33,1},{2,34},{34,2},{3,35},{35,3},{4,36},{36... | collective-permute-start | bytes 983048 | tf_op jit(solution)/shard_map/ppermute | solution.py:29
  9.8 4.9 %collective-permute-start.1 = (f32[160,128]{1,0:T(8,128)S(1)}, f32[160,128]{1,0:T(8,128)S(1)}, u32[]{:S(2)}, u32[]{:S(2)}) collective-permute-start(f32[160,128]{1,0:T(8,128)S(1)} %get-tuple-element.9), channel_id=1, source_target_pairs={{0,64},{64,128},{128,192},{192,0},{1,65},{65,129},{129,193},{193,1... | collective-permute-start | bytes 245768 | tf_op jit(solution)/shard_map/ppermute | solution.py:29
  9.9 6.1 %collective-permute-start.3 = (f32[160,128]{1,0:T(8,128)S(1)}, f32[160,128]{1,0:T(8,128)S(1)}, u32[]{:S(2)}, u32[]{:S(2)}) collective-permute-start(f32[160,128]{1,0:T(8,128)S(1)} %get-tuple-element.10), channel_id=1, source_target_pairs={{0,192},{64,0},{128,64},{192,128},{1,193},{65,1},{129,65},{193,129... | collective-permute-start | bytes 245768 | tf_op jit(solution)/shard_map/ppermute | solution.py:29
  12.6 4.8 %collective-permute-start.2 = (f32[160,128]{1,0:T(8,128)S(1)}, f32[160,128]{1,0:T(8,128)S(1)}, u32[]{:S(2)}, u32[]{:S(2)}) collective-permute-start(f32[160,128]{1,0:T(8,128)S(1)} %get-tuple-element.11), channel_id=1, source_target_pairs={{0,128},{64,192},{128,0},{192,64},{1,129},{65,193},{129,1},{193,65... | collective-permute-start | bytes 245768 | tf_op jit(solution)/shard_map/ppermute | solution.py:29
  17.4 3.9 %collective-permute-start.4 = (f32[40,128]{1,0:T(8,128)S(1)}, f32[40,128]{1,0:T(8,128)S(1)}, u32[]{:S(2)}, u32[]{:S(2)}) collective-permute-start(f32[40,128]{1,0:T(8,128)S(1)} %get-tuple-element.18), channel_id=1, source_target_pairs={{0,8},{8,16},{16,24},{24,0},{1,9},{9,17},{17,25},{25,1},{2,10},{10... | collective-permute-start | bytes 61448 | tf_op jit(solution)/shard_map/ppermute | solution.py:29
  17.5 3.8 %collective-permute-start.6 = (f32[40,128]{1,0:T(8,128)S(1)}, f32[40,128]{1,0:T(8,128)S(1)}, u32[]{:S(2)}, u32[]{:S(2)}) collective-permute-start(f32[40,128]{1,0:T(8,128)S(1)} %get-tuple-element.19), channel_id=1, source_target_pairs={{0,24},{8,0},{16,8},{24,16},{1,25},{9,1},{17,9},{25,17},{2,26},{10... | collective-permute-start | bytes 61448 | tf_op jit(solution)/shard_map/ppermute | solution.py:29
  20.2 4.1 %collective-permute-start.5 = (f32[40,128]{1,0:T(8,128)S(1)}, f32[40,128]{1,0:T(8,128)S(1)}, u32[]{:S(2)}, u32[]{:S(2)}) collective-permute-start(f32[40,128]{1,0:T(8,128)S(1)} %get-tuple-element.20), channel_id=1, source_target_pairs={{0,16},{8,24},{16,0},{24,8},{1,17},{9,25},{17,1},{25,9},{2,18},{10... | collective-permute-start | bytes 61448 | tf_op jit(solution)/shard_map/ppermute | solution.py:29
  25.0 14.9 %all-to-all-start = ((f32[8,40,128]{2,1,0:T(8,128)}), f32[8,40,128]{2,1,0:T(8,128)S(1)}, u32[]{:S(2)}, u32[]{:S(2)}) async-start(f32[8,40,128]{2,1,0:T(8,128)} %broadcast_in_dim.2), calls=%async_computation | async-start | bytes 327680 | tf_op jit(solution)/shard_map/all_to_all | solution.py:50
  39.9 5.7 %collective-permute-start.9 = (f32[40,128]{1,0:T(8,128)S(1)}, f32[40,128]{1,0:T(8,128)S(1)}, u32[]{:S(2)}, u32[]{:S(2)}) collective-permute-start(f32[40,128]{1,0:T(8,128)S(1)} %reduce_sum.9), channel_id=1, source_target_pairs={{0,24},{8,0},{16,8},{24,16},{1,25},{9,1},{17,9},{25,17},{2,26},{10... | collective-permute-start | bytes 61448 | tf_op jit(solution)/shard_map/ppermute | solution.py:29
  41.3 4.4 %collective-permute-start.8 = (f32[40,128]{1,0:T(8,128)S(1)}, f32[40,128]{1,0:T(8,128)S(1)}, u32[]{:S(2)}, u32[]{:S(2)}) collective-permute-start(f32[40,128]{1,0:T(8,128)S(1)} %reduce_sum.9), channel_id=1, source_target_pairs={{0,16},{8,24},{16,0},{24,8},{1,17},{9,25},{17,1},{25,9},{2,18},{10... | collective-permute-start | bytes 61448 | tf_op jit(solution)/shard_map/ppermute | solution.py:29
  41.8 3.8 %collective-permute-start.7 = (f32[40,128]{1,0:T(8,128)S(1)}, f32[40,128]{1,0:T(8,128)S(1)}, u32[]{:S(2)}, u32[]{:S(2)}) collective-permute-start(f32[40,128]{1,0:T(8,128)S(1)} %reduce_sum.9), channel_id=1, source_target_pairs={{0,8},{8,16},{16,24},{24,0},{1,9},{9,17},{17,25},{25,1},{2,10},{10... | collective-permute-start | bytes 61448 | tf_op jit(solution)/shard_map/ppermute | solution.py:29
  45.7 4.6 %collective-permute-start.10 = (f32[160,128]{1,0:T(8,128)S(1)}, f32[160,128]{1,0:T(8,128)S(1)}, u32[]{:S(2)}, u32[]{:S(2)}) collective-permute-start(f32[160,128]{1,0:T(8,128)S(1)} %get-tuple-element.23), channel_id=1, source_target_pairs={{0,64},{64,128},{128,192},{192,0},{1,65},{65,129},{129,193},{193,1... | collective-permute-start | bytes 245768 | tf_op jit(solution)/shard_map/ppermute | solution.py:29
  46.5 6.7 %collective-permute-start.12 = (f32[160,128]{1,0:T(8,128)S(1)}, f32[160,128]{1,0:T(8,128)S(1)}, u32[]{:S(2)}, u32[]{:S(2)}) collective-permute-start(f32[160,128]{1,0:T(8,128)S(1)} %get-tuple-element.23), channel_id=1, source_target_pairs={{0,192},{64,0},{128,64},{192,128},{1,193},{65,1},{129,65},{193,129... | collective-permute-start | bytes 245768 | tf_op jit(solution)/shard_map/ppermute | solution.py:29
  48.4 4.8 %collective-permute-start.11 = (f32[160,128]{1,0:T(8,128)S(1)}, f32[160,128]{1,0:T(8,128)S(1)}, u32[]{:S(2)}, u32[]{:S(2)}) collective-permute-start(f32[160,128]{1,0:T(8,128)S(1)} %get-tuple-element.23), channel_id=1, source_target_pairs={{0,128},{64,192},{128,0},{192,64},{1,129},{65,193},{129,1},{193,65... | collective-permute-start | bytes 245768 | tf_op jit(solution)/shard_map/ppermute | solution.py:29
  53.3 10.0 %collective-permute-start.13 = (f32[640,128]{1,0:T(8,128)S(1)}, f32[640,128]{1,0:T(8,128)S(1)}, u32[]{:S(2)}, u32[]{:S(2)}) collective-permute-start(f32[640,128]{1,0:T(8,128)S(1)} %get-tuple-element.12), channel_id=1, source_target_pairs={{0,32},{32,0},{1,33},{33,1},{2,34},{34,2},{3,35},{35,3},{4,36},{36... | collective-permute-start | bytes 983048 | tf_op jit(solution)/shard_map/ppermute | solution.py:29
  63.3 0.9 %copy-start = (f32[64,512]{1,0:T(8,128)S(1)}, f32[64,512]{1,0:T(8,128)}, u32[]{:S(2)}) copy-start(f32[64,512]{1,0:T(8,128)} %start_rows.1.v_ref) | copy-start | bytes 393220

commit v4 on v3

--- a/solution.py
+++ b/solution.py
@@ -24,13 +24,32 @@
 NT = (((1,), (1,)), ((), ()))
 
 
+def half():
+    return (lax.axis_index("c") + lax.axis_index("x") + lax.axis_index("y")) % 2
+
+
+def place_on(axis):
+    return half() if axis == "c" else lax.axis_index(axis)
+
+
 def shifted(v, axis, k):
-    n = lax.axis_size(axis)
-    return lax.ppermute(v, axis, [(i, (i + k) % n) for i in range(n)])
+    sizes = [lax.axis_size(a) for a in AXES]
+    along, core = AXES.index(axis), AXES.index("c")
+    pairs = []
+    for source, at in enumerate(itertools.product(*map(range, sizes))):
+        to = list(at)
+        to[along] = (to[along] + k) % sizes[along]
+        if along != core:
+            to[core] = (to[core] + k) % 2
+        target = 0
+        for size, i in zip(sizes, to):
+            target = target * size + i
+        pairs.append((source, target))
+    return lax.ppermute(v, AXES, pairs)
 
 
 def share_of_sum(v, axis):
-    n, me = lax.axis_size(axis), lax.axis_index(axis)
+    n, me = lax.axis_size(axis), place_on(axis)
     rows = v.shape[0] // n
     piece = lambda k: lax.dynamic_slice_in_dim(v, lax.rem(me + k, n) * rows, rows, 0)
     arrived = [shifted(piece(k), axis, k) for k in range(1, n)]
@@ -84,43 +103,45 @@
     return lax.broadcasted_iota(jnp.int32, shape, dim)
 
 
-def gram_kernel(x_ref, out_ref, total):
-    step = pl.program_id(0)
-    m = x_ref.shape[0]
-
-    @pl.when(step == 0)
-    def _():
-        total[...] = jnp.zeros_like(total)
-
-    hi, lo = two_parts(x_ref[...])
-    for j in range(m // WIDE):
-        rows, here = slice(0, (j + 1) * WIDE), slice(j * WIDE, (j + 1) * WIDE)
-        total[rows, here] += (
-            dot_nt(hi[rows], hi[here]) + dot_nt(lo[rows], hi[here]) + dot_nt(hi[rows], lo[here])
-        )
-
-    @pl.when(step == pl.num_programs(0) - 1)
-    def _():
-        place = 0
-        for i in range(m // TILE):
-            for j in range(i, m // TILE):
-                out_ref[place * TILE : (place + 1) * TILE, :] = total[
-                    i * TILE : (i + 1) * TILE, j * TILE : (j + 1) * TILE
-                ]
-                place += 1
-
-
-def upper_gram(x, chunk=512):
+def gram_kernel(x_hbm, out_ref, x, sem):
+    m, n = x_hbm.shape
+    bands = [slice(i, i + WIDE) for i in range(0, m, WIDE)]
+    loads = [pltpu.make_async_copy(x_hbm.at[b], x.at[b], sem.at[i]) for i, b in enumerate(bands)]
+    for load in loads:
+        load.start()
+    tiles = m // TILE
+    places = {}
+    for i in range(tiles):
+        for j in range(i, tiles):
+            places[i, j] = len(places)
+    step = WIDE // TILE
+    parts = []
+    for j, load in enumerate(loads):
+        load.wait()
+        parts.append(two_parts(x[bands[j]]))
+        hi, lo = parts[j]
+        for i in range(j + 1):
+            above_hi, above_lo = parts[i]
+            block = dot_nt(above_hi, hi) + (dot_nt(above_lo, hi) + dot_nt(above_hi, lo))
+            for s in range(step):
+                for t in range(step):
+                    place = places.get((i * step + s, j * step + t))
+                    if place is not None:
+                        out_ref[place * TILE : (place + 1) * TILE, :] = block[
+                            s * TILE : (s + 1) * TILE, t * TILE : (t + 1) * TILE
+                        ]
+
+
+def upper_gram(x):
     m, n = x.shape
     tiles = m // TILE
     lines = tiles * (tiles + 1) // 2 * TILE
     return pl.pallas_call(
         gram_kernel,
         out_shape=jax.ShapeDtypeStruct((lines, TILE), F32),
-        grid=(n // chunk,),
-        in_specs=[pl.BlockSpec((m, chunk), lambda i: (0, i))],
-        out_specs=pl.BlockSpec((lines, TILE), lambda i: (0, 0)),
-        scratch_shapes=[pltpu.VMEM((m, m), F32)],
+        in_specs=[pl.BlockSpec(memory_space=pl.ANY)],
+        out_specs=pl.BlockSpec(memory_space=pltpu.VMEM),
+        scratch_shapes=[pltpu.VMEM((m, n), F32), pltpu.SemaphoreType.DMA((m // WIDE,))],
         compiler_params=pltpu.CompilerParams(vmem_limit_bytes=VMEM),
         cost_estimate=pl.CostEstimate(flops=6 * m * m * n, bytes_accessed=4 * m * n, transcendentals=0),
         name="gram",
@@ -140,17 +161,27 @@
             for q in range(p, blocks)
             for i in range(ROWS)
         }
-        for i in range(ROWS):
-            inverse = 1.0 / column[p, i][i : i + 1, :]
-            pivot_row = line[p][i : i + 1, :] * inverse
-            ahead = {j: column[p, j][i : i + 1, :] * inverse for j in range(i + 1, ROWS)}
+        for i in range(0, ROWS, 2):
+            a, b_, c = column[p, i][i : i + 1, :], column[p, i + 1][i : i + 1, :], column[p, i + 1][i + 1 : i + 2, :]
+            first = 1.0 / a
+            second = a / (a * c - b_ * b_)
+            lower = b_ * first
+            others = range(i + 2, ROWS)
+            top = {j: column[p, j][i : i + 1, :] for j in others}
+            ahead = {j: top[j] * first for j in others}
+            then = {j: (column[p, j][i + 1 : i + 2, :] - lower * top[j]) * second for j in others}
+            top_row = line[p][i : i + 1, :]
+            first_row = top_row * first
+            next_row = (line[p][i + 1 : i + 2, :] - lower * top_row) * second
             for q in range(p, blocks):
                 factor = column[q, i]
+                following = column[q, i + 1] - factor * lower
                 if q == p:
                     factor = jnp.where(sub > i, factor, 0.0)
-                for j in range(i + 1, ROWS):
-                    column[q, j] = column[q, j] - factor * ahead[j]
-                line[q] = line[q] - factor * pivot_row
+                    following = jnp.where(sub > i + 1, following, 0.0)
+                for j in others:
+                    column[q, j] = column[q, j] - factor * ahead[j] - following * then[j]
+                line[q] = line[q] - factor * first_row - following * next_row
     both = jnp.concatenate(line, axis=0)
     pivots = jnp.sum(
         jnp.where(iota(both.shape, 0) == iota(both.shape, 1), both, 0.0), axis=1, keepdims=True
@@ -163,7 +194,9 @@
 
 
 def start_kernel(s_ref, v_ref):
-    v_ref[...] = orthonormal(s_ref[...])
+    s = s_ref[...]
+    size = jnp.max(jnp.max(jnp.abs(s), axis=0, keepdims=True), axis=1, keepdims=True)
+    v_ref[...] = orthonormal(s / size)
 
 
 def start_rows(s):
@@ -171,6 +204,7 @@
     return pl.pallas_call(
         start_kernel,
         out_shape=jax.ShapeDtypeStruct((k, m), F32),
+        compiler_params=pltpu.CompilerParams(vmem_limit_bytes=8 * 2**20),
         cost_estimate=pl.CostEstimate(flops=8 * 10**9, bytes_accessed=8 * m * k, transcendentals=0),
         name="start_rows",
     )(s)
@@ -219,13 +253,16 @@
                 for ref, part in zip(gram, three_parts(tile.T)):
                     ref[at_j, at_i] = part
 
+    diagonal = jnp.concatenate(diagonal, axis=1)
+    evened = m / jnp.sum(diagonal, axis=1, keepdims=True)
     v = v_ref[...]
     for sweep in range(ITERS):
-        v = orthonormal(times_gram(v, gram))
+        v = orthonormal(times_gram(v, gram) * evened)
+    load.wait()
     w = times_gram(v, gram)
     inner = dot_nt(w, v, HIGHEST)
     twice = jnp.dot(inner, v, precision=HIGHEST) - 2.0 * w
-    power = jnp.concatenate(diagonal, axis=1) + jnp.sum(v * twice, axis=0, keepdims=True)
+    power = diagonal + jnp.sum(v * twice, axis=0, keepdims=True)
     scale = lax.rsqrt(jnp.maximum(power, 0.0) + EPSILON)
     scale = jnp.concatenate(
         [
@@ -238,7 +275,6 @@
     spread = jnp.concatenate([q0, q1, q0], axis=1)
     v0, v1 = two_parts(v)
     v01 = jnp.concatenate([v0, v1], axis=0)
-    load.wait()
     for c in range(n // chunk):
         here = slice(c * chunk, (c + 1) * chunk)
         xc = x[:, here]
@@ -287,7 +323,7 @@
 def on_device(phase_stack, start_basis):
     pixel_total = phase_stack.shape[1] * lax.axis_size(AXES)
     lines, v = sum_everywhere(upper_gram(phase_stack), start_rows(start_basis.T))
-    me = jnp.stack([lax.axis_index(axis) for axis in SHARED]).astype(jnp.int32)
+    me = jnp.stack([place_on(axis) for axis in SHARED]).astype(jnp.int32)
     sizes = tuple(lax.axis_size(axis) for axis in SHARED)
     return corrected(lines, me, sizes, v, phase_stack, pixel_total)
 

time: 77.3 us -> 72.9 us (0.943)
  Pallas kernels: 21.6 us -> 18.2 us
  waiting for transfers between devices: 23.5 us -> 26.6 us
  starting transfers between devices: 29.7 us -> 26.6 us
  local copies, waits for them, and re-layouts: 1.74 us -> 0.84 us
    ppermute x14, starting transfers between devices: 23.1 us -> 19.4 us  [shifted(): return lax.ppermute(v, AXES, pairs)]
    all_to_all x1, waiting for transfers between devices: 4.46 us -> 6.1 us  [summed(): arrived = lax.all_to_all(copies, axis, 0, 0, tiled=True)]
    pallas_call x1, Pallas kernels: 3.83 us -> 2.19 us  [start_rows(): pl.pallas_call(start_kernel, out_shape=jax.ShapeDtypeStruct((k, m), F32),...]
    ppermute x14, waiting for transfers between devices: 19 us -> 20.5 us  [shifted(): return lax.ppermute(v, AXES, pairs)]
    pallas_call x1, Pallas kernels: 12.7 us -> 11.5 us  [corrected(): pl.pallas_call(functools.partial(finish_kernel, pixel_total, chunk, sizes...]
    unnamed x8, local copies, waits for them, and re-layouts: 0.95 us -> 0.05 us
  transfers between devices with their start and end apart: 15 -> 15, of which waited for: 11 -> 11; matrix products, arithmetic and copies ran while one was open for 0% -> 0% of each run, Pallas kernels for 5% -> 3%
where the time goes in v4:
time: 72.9 us; the launch traced here: 72.7 us
  starting transfers between devices  26.6 us (36%)
  waiting for transfers between devices  26.6 us (36%)
  Pallas kernels  18.2 us (25%)
  local copies, waits for them, and re-layouts  0.84 us (1%)
    ppermute x14, waiting for transfers between devices, shifted(): return lax.ppermute(v, AXES, pairs)  20.5 us
    ppermute x14, starting transfers between devices, shifted(): return lax.ppermute(v, AXES, pairs)  19.4 us
    pallas_call x1, Pallas kernels, corrected(): pl.pallas_call(functools.partial(finish_kernel, pixel_total, chunk, sizes...  11.5 us
    all_to_all x1, starting transfers between devices, summed(): arrived = lax.all_to_all(copies, axis, 0, 0, tiled=True)  7.24 us
    all_to_all x1, waiting for transfers between devices, summed(): arrived = lax.all_to_all(copies, axis, 0, 0, tiled=True)  6.1 us
    pallas_call x1, Pallas kernels, upper_gram(): pl.pallas_call(gram_kernel, out_shape=jax.ShapeDtypeStruct((lines, TILE),...  4.52 us
    pallas_call x1, Pallas kernels, start_rows(): pl.pallas_call(start_kernel, out_shape=jax.ShapeDtypeStruct((k, m), F32),...  2.19 us
  transfers between devices with their start and end apart: 15, of which 11 were waited for; matrix products, arithmetic and copies ran while one was open for 0% of the time, Pallas kernels for 3%

profile of v4, /device:TPU:1, one launch (start us, length us, event | category | flops | bytes accessed | tf_op | source)
XLA Modules:
  0.0 72.7 jit_solution(8331911236527176897)
XLA Ops:
  0.0 0.0 copy-start
  0.0 4.5 %gram.1 = f32[1280,128]{1,0:T(8,128)S(1)} custom-call(f32[512,2048]{1,0:T(8,128)} %x_hbm.3), custom_call_target="tpu_custom_call" | custom-call | flops 3221225472 | bytes 4194304 | tf_op jit(solution)/shard_map/gram/pallas_call | solution.py:139
  4.6 3.3 %collective-permute-start = (f32[640,128]{1,0:T(8,128)S(1)}, f32[640,128]{1,0:T(8,128)S(1)}, u32[]{:S(2)}, u32[]{:S(2)}) collective-permute-start(f32[640,128]{1,0:T(8,128)S(1)} %constant_dynamic-slice_fusion.6), channel_id=1, source_target_pairs={{0,32},{1,33},{2,34},{3,35},{4,36},{5,37},{6,38},{7,39},{8,40},{9,... | collective-permute-start | bytes 983048 | tf_op jit(solution)/shard_map/ppermute | solution.py:48
  7.9 1.3 %collective-permute-done = f32[640,128]{1,0:T(8,128)S(1)} collective-permute-done((f32[640,128]{1,0:T(8,128)S(1)}, f32[640,128]{1,0:T(8,128)S(1)}, u32[]{:S(2)}, u32[]{:S(2)}) %collective-permute-start) | collective-permute-done | bytes 327712 | tf_op jit(solution)/shard_map/ppermute | solution.py:48
  9.2 0.1 collective-permute-start.1
  9.3 3.0 %collective-permute-start.3 = (f32[160,128]{1,0:T(8,128)S(1)}, f32[160,128]{1,0:T(8,128)S(1)}, u32[]{:S(2)}, u32[]{:S(2)}) collective-permute-start(f32[160,128]{1,0:T(8,128)S(1)} %get-tuple-element.10), channel_id=1, source_target_pairs={{0,224},{1,225},{2,226},{3,227},{4,228},{5,229},{6,230},{7,231},{8... | collective-permute-start | bytes 245768 | tf_op jit(solution)/shard_map/ppermute | solution.py:48
  12.3 0.0 collective-permute-start.2
  12.3 2.7 %collective-permute-done.1 = f32[160,128]{1,0:T(8,128)S(1)} collective-permute-done((f32[160,128]{1,0:T(8,128)S(1)}, f32[160,128]{1,0:T(8,128)S(1)}, u32[]{:S(2)}, u32[]{:S(2)}) %collective-permute-start.1) | collective-permute-done | bytes 81952 | tf_op jit(solution)/shard_map/ppermute | solution.py:48
  15.0 0.9 %collective-permute-done.3 = f32[160,128]{1,0:T(8,128)S(1)} collective-permute-done((f32[160,128]{1,0:T(8,128)S(1)}, f32[160,128]{1,0:T(8,128)S(1)}, u32[]{:S(2)}, u32[]{:S(2)}) %collective-permute-start.3) | collective-permute-done | bytes 81952 | tf_op jit(solution)/shard_map/ppermute | solution.py:48
  15.8 1.6 %collective-permute-done.2 = f32[160,128]{1,0:T(8,128)S(1)} collective-permute-done((f32[160,128]{1,0:T(8,128)S(1)}, f32[160,128]{1,0:T(8,128)S(1)}, u32[]{:S(2)}, u32[]{:S(2)}) %collective-permute-start.2) | collective-permute-done | bytes 81952 | tf_op jit(solution)/shard_map/ppermute | solution.py:48
  17.5 0.7 %collective-permute-start.4 = (f32[40,128]{1,0:T(8,128)S(1)}, f32[40,128]{1,0:T(8,128)S(1)}, u32[]{:S(2)}, u32[]{:S(2)}) collective-permute-start(f32[40,128]{1,0:T(8,128)S(1)} %get-tuple-element.18), channel_id=1, source_target_pairs={{0,40},{1,41},{2,42},{3,43},{4,44},{5,45},{6,46},{7,47},{8,48},{9,... | collective-permute-start | bytes 61448 | tf_op jit(solution)/shard_map/ppermute | solution.py:48
  18.2 2.3 %collective-permute-start.6 = (f32[40,128]{1,0:T(8,128)S(1)}, f32[40,128]{1,0:T(8,128)S(1)}, u32[]{:S(2)}, u32[]{:S(2)}) collective-permute-start(f32[40,128]{1,0:T(8,128)S(1)} %get-tuple-element.19), channel_id=1, source_target_pairs={{0,56},{1,57},{2,58},{3,59},{4,60},{5,61},{6,62},{7,63},{8,32},{9,... | collective-permute-start | bytes 61448 | tf_op jit(solution)/shard_map/ppermute | solution.py:48
  20.5 0.1 collective-permute-start.5
  20.7 1.3 %collective-permute-done.4 = f32[40,128]{1,0:T(8,128)S(1)} collective-permute-done((f32[40,128]{1,0:T(8,128)S(1)}, f32[40,128]{1,0:T(8,128)S(1)}, u32[]{:S(2)}, u32[]{:S(2)}) %collective-permute-start.4) | collective-permute-done | bytes 20512 | tf_op jit(solution)/shard_map/ppermute | solution.py:48
  22.0 0.0 collective-permute-done.6
  22.0 2.7 %collective-permute-done.5 = f32[40,128]{1,0:T(8,128)S(1)} collective-permute-done((f32[40,128]{1,0:T(8,128)S(1)}, f32[40,128]{1,0:T(8,128)S(1)}, u32[]{:S(2)}, u32[]{:S(2)}) %collective-permute-start.5) | collective-permute-done | bytes 20512 | tf_op jit(solution)/shard_map/ppermute | solution.py:48
  24.7 0.7 broadcast_in_dim.2
  25.4 7.2 %all-to-all-start = ((f32[8,40,128]{2,1,0:T(8,128)}), f32[8,40,128]{2,1,0:T(8,128)S(1)}, u32[]{:S(2)}, u32[]{:S(2)}) async-start(f32[8,40,128]{2,1,0:T(8,128)} %broadcast_in_dim.2), calls=%async_computation | async-start | bytes 327680 | tf_op jit(solution)/shard_map/all_to_all | solution.py:69
  32.6 0.0 copy-done
  32.6 2.2 %start_rows.1.v_ref = f32[64,512]{1,0:T(8,128)S(1)} custom-call(f32[64,512]{1,0:T(8,128)S(1)} %bitcast.4), custom_call_target="tpu_custom_call" | custom-call | flops 8000000000 | bytes 262144 | tf_op jit(solution)/shard_map/start_rows/pallas_call | solution.py:204
  34.8 6.1 %all-to-all-done = f32[8,40,128]{2,1,0:T(8,128)S(1)} async-done(((f32[8,40,128]{2,1,0:T(8,128)}), f32[8,40,128]{2,1,0:T(8,128)S(1)}, u32[]{:S(2)}, u32[]{:S(2)}) %all-to-all-start) | async-done | bytes 163872 | tf_op jit(solution)/shard_map/all_to_all | solution.py:69
  40.9 4.3 %collective-permute-start.9 = (f32[40,128]{1,0:T(8,128)S(1)}, f32[40,128]{1,0:T(8,128)S(1)}, u32[]{:S(2)}, u32[]{:S(2)}) collective-permute-start(f32[40,128]{1,0:T(8,128)S(1)} %reduce_sum.9), channel_id=1, source_target_pairs={{0,56},{1,57},{2,58},{3,59},{4,60},{5,61},{6,62},{7,63},{8,32},{9,... | collective-permute-start | bytes 61448 | tf_op jit(solution)/shard_map/ppermute | solution.py:48
  45.2 0.5 collective-permute-start.8
  45.8 0.4 collective-permute-start.7
  46.2 4.0 %collective-permute-done.7 = f32[40,128]{1,0:T(8,128)S(1)} collective-permute-done((f32[40,128]{1,0:T(8,128)S(1)}, f32[40,128]{1,0:T(8,128)S(1)}, u32[]{:S(2)}, u32[]{:S(2)}) %collective-permute-start.7) | collective-permute-done | bytes 20512 | tf_op jit(solution)/shard_map/ppermute | solution.py:48
  50.2 0.0 collective-permute-done.8
  50.2 0.0 collective-permute-done.9
  50.2 1.0 %collective-permute-start.10 = (f32[160,128]{1,0:T(8,128)S(1)}, f32[160,128]{1,0:T(8,128)S(1)}, u32[]{:S(2)}, u32[]{:S(2)}) collective-permute-start(f32[160,128]{1,0:T(8,128)S(1)} %get-tuple-element.23), channel_id=1, source_target_pairs={{0,96},{1,97},{2,98},{3,99},{4,100},{5,101},{6,102},{7,103},{8,104... | collective-permute-start | bytes 245768 | tf_op jit(solution)/shard_map/ppermute | solution.py:48
  51.2 2.1 %collective-permute-start.12 = (f32[160,128]{1,0:T(8,128)S(1)}, f32[160,128]{1,0:T(8,128)S(1)}, u32[]{:S(2)}, u32[]{:S(2)}) collective-permute-start(f32[160,128]{1,0:T(8,128)S(1)} %get-tuple-element.23), channel_id=1, source_target_pairs={{0,224},{1,225},{2,226},{3,227},{4,228},{5,229},{6,230},{7,231},{8... | collective-permute-start | bytes 245768 | tf_op jit(solution)/shard_map/ppermute | solution.py:48
  53.3 0.4 collective-permute-start.11
  53.6 2.2 %collective-permute-done.10 = f32[160,128]{1,0:T(8,128)S(1)} collective-permute-done((f32[160,128]{1,0:T(8,128)S(1)}, f32[160,128]{1,0:T(8,128)S(1)}, u32[]{:S(2)}, u32[]{:S(2)}) %collective-permute-start.10) | collective-permute-done | bytes 81952 | tf_op jit(solution)/shard_map/ppermute | solution.py:48
  55.8 2.8 %collective-permute-done.11 = f32[160,128]{1,0:T(8,128)S(1)} collective-permute-done((f32[160,128]{1,0:T(8,128)S(1)}, f32[160,128]{1,0:T(8,128)S(1)}, u32[]{:S(2)}, u32[]{:S(2)}) %collective-permute-start.11) | collective-permute-done | bytes 81952 | tf_op jit(solution)/shard_map/ppermute | solution.py:48
  58.6 0.0 collective-permute-done.12
  58.6 1.1 %collective-permute-start.13 = (f32[640,128]{1,0:T(8,128)S(1)}, f32[640,128]{1,0:T(8,128)S(1)}, u32[]{:S(2)}, u32[]{:S(2)}) collective-permute-start(f32[640,128]{1,0:T(8,128)S(1)} %get-tuple-element.12), channel_id=1, source_target_pairs={{0,32},{1,33},{2,34},{3,35},{4,36},{5,37},{6,38},{7,39},{8,40},{9,... | collective-permute-start | bytes 983048 | tf_op jit(solution)/shard_map/ppermute | solution.py:48
  59.8 0.1 pad_add_fusion.me_ref
  59.8 1.2 %collective-permute-done.13 = f32[640,128]{1,0:T(8,128)S(1)} collective-permute-done((f32[640,128]{1,0:T(8,128)S(1)}, f32[640,128]{1,0:T(8,128)S(1)}, u32[]{:S(2)}, u32[]{:S(2)}) %collective-permute-start.13) | collective-permute-done | bytes 327712 | tf_op jit(solution)/shard_map/ppermute | solution.py:48
  61.0 11.5 %finish.1 = f32[512,2048]{1,0:T(8,128)} custom-call(s32[3]{0:T(128)S(1)} %pad_add_fusion.me_ref, f32[1280,128]{1,0:T(8,128)S(1)} %constant_dynamic-update-slice_fusion.11.lines_ref, f32[64,512]{1,0:T(8,128)S(1)} %start_rows.1.v_ref, f32[512,2048]{1,0:T(8,128)} %x_hbm.3), custom_call_target="tpu_custom_call" | custom-call | flops 805306368 | bytes 8388608 | tf_op jit(solution)/shard_map/finish/pallas_call | solution.py:297
  (15 shorter events, 0.2 us)
Async XLA Ops:
  0.0 32.6 %copy-start = (f32[512,64]{0,1:T(8,128)S(1)}, f32[512,64]{0,1:T(8,128)}, u32[]{:S(2)}) copy-start(f32[512,64]{0,1:T(8,128)} %param.3) | copy-start | bytes 393220
  4.6 4.6 %collective-permute-start = (f32[640,128]{1,0:T(8,128)S(1)}, f32[640,128]{1,0:T(8,128)S(1)}, u32[]{:S(2)}, u32[]{:S(2)}) collective-permute-start(f32[640,128]{1,0:T(8,128)S(1)} %constant_dynamic-slice_fusion.6), channel_id=1, source_target_pairs={{0,32},{1,33},{2,34},{3,35},{4,36},{5,37},{6,38},{7,39},{8,40},{9,... | collective-permute-start | bytes 983048 | tf_op jit(solution)/shard_map/ppermute | solution.py:48
  9.2 5.7 %collective-permute-start.1 = (f32[160,128]{1,0:T(8,128)S(1)}, f32[160,128]{1,0:T(8,128)S(1)}, u32[]{:S(2)}, u32[]{:S(2)}) collective-permute-start(f32[160,128]{1,0:T(8,128)S(1)} %get-tuple-element.9), channel_id=1, source_target_pairs={{0,96},{1,97},{2,98},{3,99},{4,100},{5,101},{6,102},{7,103},{8,104... | collective-permute-start | bytes 245768 | tf_op jit(solution)/shard_map/ppermute | solution.py:48
  9.3 6.5 %collective-permute-start.3 = (f32[160,128]{1,0:T(8,128)S(1)}, f32[160,128]{1,0:T(8,128)S(1)}, u32[]{:S(2)}, u32[]{:S(2)}) collective-permute-start(f32[160,128]{1,0:T(8,128)S(1)} %get-tuple-element.10), channel_id=1, source_target_pairs={{0,224},{1,225},{2,226},{3,227},{4,228},{5,229},{6,230},{7,231},{8... | collective-permute-start | bytes 245768 | tf_op jit(solution)/shard_map/ppermute | solution.py:48
  12.3 5.2 %collective-permute-start.2 = (f32[160,128]{1,0:T(8,128)S(1)}, f32[160,128]{1,0:T(8,128)S(1)}, u32[]{:S(2)}, u32[]{:S(2)}) collective-permute-start(f32[160,128]{1,0:T(8,128)S(1)} %get-tuple-element.11), channel_id=1, source_target_pairs={{0,128},{1,129},{2,130},{3,131},{4,132},{5,133},{6,134},{7,135},{8... | collective-permute-start | bytes 245768 | tf_op jit(solution)/shard_map/ppermute | solution.py:48
  17.5 4.5 %collective-permute-start.4 = (f32[40,128]{1,0:T(8,128)S(1)}, f32[40,128]{1,0:T(8,128)S(1)}, u32[]{:S(2)}, u32[]{:S(2)}) collective-permute-start(f32[40,128]{1,0:T(8,128)S(1)} %get-tuple-element.18), channel_id=1, source_target_pairs={{0,40},{1,41},{2,42},{3,43},{4,44},{5,45},{6,46},{7,47},{8,48},{9,... | collective-permute-start | bytes 61448 | tf_op jit(solution)/shard_map/ppermute | solution.py:48
  18.2 3.8 %collective-permute-start.6 = (f32[40,128]{1,0:T(8,128)S(1)}, f32[40,128]{1,0:T(8,128)S(1)}, u32[]{:S(2)}, u32[]{:S(2)}) collective-permute-start(f32[40,128]{1,0:T(8,128)S(1)} %get-tuple-element.19), channel_id=1, source_target_pairs={{0,56},{1,57},{2,58},{3,59},{4,60},{5,61},{6,62},{7,63},{8,32},{9,... | collective-permute-start | bytes 61448 | tf_op jit(solution)/shard_map/ppermute | solution.py:48
  20.5 4.1 %collective-permute-start.5 = (f32[40,128]{1,0:T(8,128)S(1)}, f32[40,128]{1,0:T(8,128)S(1)}, u32[]{:S(2)}, u32[]{:S(2)}) collective-permute-start(f32[40,128]{1,0:T(8,128)S(1)} %get-tuple-element.20), channel_id=1, source_target_pairs={{0,16},{1,17},{2,18},{3,19},{4,20},{5,21},{6,22},{7,23},{8,24},{9,... | collective-permute-start | bytes 61448 | tf_op jit(solution)/shard_map/ppermute | solution.py:48
  25.4 15.5 %all-to-all-start = ((f32[8,40,128]{2,1,0:T(8,128)}), f32[8,40,128]{2,1,0:T(8,128)S(1)}, u32[]{:S(2)}, u32[]{:S(2)}) async-start(f32[8,40,128]{2,1,0:T(8,128)} %broadcast_in_dim.2), calls=%async_computation | async-start | bytes 327680 | tf_op jit(solution)/shard_map/all_to_all | solution.py:69
  40.9 9.3 %collective-permute-start.9 = (f32[40,128]{1,0:T(8,128)S(1)}, f32[40,128]{1,0:T(8,128)S(1)}, u32[]{:S(2)}, u32[]{:S(2)}) collective-permute-start(f32[40,128]{1,0:T(8,128)S(1)} %reduce_sum.9), channel_id=1, source_target_pairs={{0,56},{1,57},{2,58},{3,59},{4,60},{5,61},{6,62},{7,63},{8,32},{9,... | collective-permute-start | bytes 61448 | tf_op jit(solution)/shard_map/ppermute | solution.py:48
  45.2 5.0 %collective-permute-start.8 = (f32[40,128]{1,0:T(8,128)S(1)}, f32[40,128]{1,0:T(8,128)S(1)}, u32[]{:S(2)}, u32[]{:S(2)}) collective-permute-start(f32[40,128]{1,0:T(8,128)S(1)} %reduce_sum.9), channel_id=1, source_target_pairs={{0,16},{1,17},{2,18},{3,19},{4,20},{5,21},{6,22},{7,23},{8,24},{9,... | collective-permute-start | bytes 61448 | tf_op jit(solution)/shard_map/ppermute | solution.py:48
  45.8 4.4 %collective-permute-start.7 = (f32[40,128]{1,0:T(8,128)S(1)}, f32[40,128]{1,0:T(8,128)S(1)}, u32[]{:S(2)}, u32[]{:S(2)}) collective-permute-start(f32[40,128]{1,0:T(8,128)S(1)} %reduce_sum.9), channel_id=1, source_target_pairs={{0,40},{1,41},{2,42},{3,43},{4,44},{5,45},{6,46},{7,47},{8,48},{9,... | collective-permute-start | bytes 61448 | tf_op jit(solution)/shard_map/ppermute | solution.py:48
  50.2 5.6 %collective-permute-start.10 = (f32[160,128]{1,0:T(8,128)S(1)}, f32[160,128]{1,0:T(8,128)S(1)}, u32[]{:S(2)}, u32[]{:S(2)}) collective-permute-start(f32[160,128]{1,0:T(8,128)S(1)} %get-tuple-element.23), channel_id=1, source_target_pairs={{0,96},{1,97},{2,98},{3,99},{4,100},{5,101},{6,102},{7,103},{8,104... | collective-permute-start | bytes 245768 | tf_op jit(solution)/shard_map/ppermute | solution.py:48
  51.2 7.4 %collective-permute-start.12 = (f32[160,128]{1,0:T(8,128)S(1)}, f32[160,128]{1,0:T(8,128)S(1)}, u32[]{:S(2)}, u32[]{:S(2)}) collective-permute-start(f32[160,128]{1,0:T(8,128)S(1)} %get-tuple-element.23), channel_id=1, source_target_pairs={{0,224},{1,225},{2,226},{3,227},{4,228},{5,229},{6,230},{7,231},{8... | collective-permute-start | bytes 245768 | tf_op jit(solution)/shard_map/ppermute | solution.py:48
  53.3 5.3 %collective-permute-start.11 = (f32[160,128]{1,0:T(8,128)S(1)}, f32[160,128]{1,0:T(8,128)S(1)}, u32[]{:S(2)}, u32[]{:S(2)}) collective-permute-start(f32[160,128]{1,0:T(8,128)S(1)} %get-tuple-element.23), channel_id=1, source_target_pairs={{0,128},{1,129},{2,130},{3,131},{4,132},{5,133},{6,134},{7,135},{8... | collective-permute-start | bytes 245768 | tf_op jit(solution)/shard_map/ppermute | solution.py:48
  58.6 2.4 %collective-permute-start.13 = (f32[640,128]{1,0:T(8,128)S(1)}, f32[640,128]{1,0:T(8,128)S(1)}, u32[]{:S(2)}, u32[]{:S(2)}) collective-permute-start(f32[640,128]{1,0:T(8,128)S(1)} %get-tuple-element.12), channel_id=1, source_target_pairs={{0,32},{1,33},{2,34},{3,35},{4,36},{5,37},{6,38},{7,39},{8,40},{9,... | collective-permute-start | bytes 983048 | tf_op jit(solution)/shard_map/ppermute | solution.py:48

commit v5 on v4

--- a/solution.py
+++ b/solution.py
@@ -48,11 +48,15 @@
     return lax.ppermute(v, AXES, pairs)
 
 
+def steps(n):
+    return sorted(range(1, n), key=lambda k: -min(k, n - k))
+
+
 def share_of_sum(v, axis):
     n, me = lax.axis_size(axis), place_on(axis)
     rows = v.shape[0] // n
     piece = lambda k: lax.dynamic_slice_in_dim(v, lax.rem(me + k, n) * rows, rows, 0)
-    arrived = [shifted(piece(k), axis, k) for k in range(1, n)]
+    arrived = [shifted(piece(k), axis, k) for k in steps(n)]
     total = piece(0)
     for part in arrived:
         total = total + part
@@ -60,7 +64,7 @@
 
 
 def joined(v, axis):
-    return jnp.concatenate([v] + [shifted(v, axis, k) for k in range(1, lax.axis_size(axis))], axis=0)
+    return jnp.concatenate([v] + [shifted(v, axis, k) for k in steps(lax.axis_size(axis))], axis=0)
 
 
 def summed(v, axis):
@@ -122,7 +126,11 @@
         hi, lo = parts[j]
         for i in range(j + 1):
             above_hi, above_lo = parts[i]
-            block = dot_nt(above_hi, hi) + (dot_nt(above_lo, hi) + dot_nt(above_hi, lo))
+            if i < j:
+                block = dot_nt(above_hi, hi) + (dot_nt(above_lo, hi) + dot_nt(above_hi, lo))
+            else:
+                mixed = dot_nt(hi, lo)
+                block = dot_nt(hi, hi) + ((mixed + mixed.T) + dot_nt(lo, lo))
             for s in range(step):
                 for t in range(step):
                     place = places.get((i * step + s, j * step + t))
@@ -155,30 +163,34 @@
     both = jnp.concatenate([b, eye], axis=1)
     line = [both[ROWS * q : ROWS * (q + 1), :] for q in range(blocks)]
     sub = iota((ROWS, 2 * k), 0)
-    for p in range(blocks):
+    span = 16
+    per = span // ROWS
+    for p in range(0, blocks, per):
         column = {
             (q, i): jnp.broadcast_to(line[q][:, ROWS * p + i : ROWS * p + i + 1], (ROWS, 2 * k))
             for q in range(p, blocks)
-            for i in range(ROWS)
+            for i in range(span)
         }
-        for i in range(0, ROWS, 2):
-            a, b_, c = column[p, i][i : i + 1, :], column[p, i + 1][i : i + 1, :], column[p, i + 1][i + 1 : i + 2, :]
-            first = 1.0 / a
-            second = a / (a * c - b_ * b_)
+        at = lambda i, j: column[p + i // ROWS, j][i % ROWS : i % ROWS + 1, :]
+        for i in range(0, span, 2):
+            a, b_, c = at(i, i), at(i, i + 1), at(i + 1, i + 1)
+            first = pl.reciprocal(a)
+            second = a * pl.reciprocal(a * c - b_ * b_)
             lower = b_ * first
-            others = range(i + 2, ROWS)
-            top = {j: column[p, j][i : i + 1, :] for j in others}
+            others = range(i + 2, span)
+            top = {j: at(i, j) for j in others}
             ahead = {j: top[j] * first for j in others}
-            then = {j: (column[p, j][i + 1 : i + 2, :] - lower * top[j]) * second for j in others}
-            top_row = line[p][i : i + 1, :]
+            then = {j: (at(i + 1, j) - lower * top[j]) * second for j in others}
+            home, row = p + i // ROWS, i % ROWS
+            top_row = line[home][row : row + 1, :]
             first_row = top_row * first
-            next_row = (line[p][i + 1 : i + 2, :] - lower * top_row) * second
-            for q in range(p, blocks):
+            next_row = (line[home][row + 1 : row + 2, :] - lower * top_row) * second
+            for q in range(home, blocks):
                 factor = column[q, i]
                 following = column[q, i + 1] - factor * lower
-                if q == p:
-                    factor = jnp.where(sub > i, factor, 0.0)
-                    following = jnp.where(sub > i + 1, following, 0.0)
+                if q == home:
+                    factor = jnp.where(sub > row, factor, 0.0)
+                    following = jnp.where(sub > row + 1, following, 0.0)
                 for j in others:
                     column[q, j] = column[q, j] - factor * ahead[j] - following * then[j]
                 line[q] = line[q] - factor * first_row - following * next_row
@@ -221,7 +233,7 @@
     )
 
 
-def finish_kernel(pixel_total, chunk, sizes, me_ref, lines_ref, v_ref, x_hbm, out_hbm, x, out, ordered, g0, g1, g2, x_sem, out_sem):
+def finish_kernel(pixel_total, chunk, sizes, me_ref, lines_ref, v_ref, x_hbm, out_hbm, x, out, ordered, g0, g1, g2, x0_ref, x1_ref, x_sem, out_sem):
     m, n = x_hbm.shape
     k = v_ref.shape[0]
     tiles = m // TILE
@@ -229,7 +241,7 @@
     load.start()
     slots = math.prod(sizes)
     rows = lines_ref.shape[0] // slots
-    for slot, back in enumerate(itertools.product(*map(range, sizes))):
+    for slot, back in enumerate(itertools.product(*([0, *steps(size)] for size in sizes))):
         place = 0
         for axis, (size, hops) in enumerate(zip(sizes, back)):
             place = place * size + lax.rem(me_ref[axis] + (size - hops), size)
@@ -257,8 +269,10 @@
     evened = m / jnp.sum(diagonal, axis=1, keepdims=True)
     v = v_ref[...]
     for sweep in range(ITERS):
+        if sweep == ITERS - 1:
+            load.wait()
+            x0_ref[...], x1_ref[...] = two_parts(x[...])
         v = orthonormal(times_gram(v, gram) * evened)
-    load.wait()
     w = times_gram(v, gram)
     inner = dot_nt(w, v, HIGHEST)
     twice = jnp.dot(inner, v, precision=HIGHEST) - 2.0 * w
@@ -275,19 +289,19 @@
     spread = jnp.concatenate([q0, q1, q0], axis=1)
     v0, v1 = two_parts(v)
     v01 = jnp.concatenate([v0, v1], axis=0)
-    for c in range(n // chunk):
-        here = slice(c * chunk, (c + 1) * chunk)
+    cuts = [*range(0, n, chunk), n - chunk // 2, n]
+    bands = [slice(a, b) for a, b in zip(cuts, cuts[1:])]
+    for c, here in enumerate(bands):
         xc = x[:, here]
-        x0, x1 = two_parts(xc)
+        x0, x1 = x0_ref[:, here], x1_ref[:, here]
         both = dot(v01, x0)
         l0, l1 = two_parts(both[:k] + (both[k:] + dot(v0, x1)))
         common = dot(spread, jnp.concatenate([l0, l0, l1], axis=0))
-        for t in range(chunk // TILE):
+        for t in range((here.stop - here.start) // TILE):
             at = slice(t * TILE, (t + 1) * TILE)
-            out[:, c * chunk + t * TILE : c * chunk + (t + 1) * TILE] = (xc[:, at] - common[:, at]) * scale
+            out[:, here.start + t * TILE : here.start + (t + 1) * TILE] = (xc[:, at] - common[:, at]) * scale
         pltpu.make_async_copy(out.at[:, here], out_hbm.at[:, here], out_sem.at[c]).start()
-    for c in range(n // chunk):
-        here = slice(c * chunk, (c + 1) * chunk)
+    for c, here in enumerate(bands):
         pltpu.make_async_copy(out.at[:, here], out_hbm.at[:, here], out_sem.at[c]).wait()
 
 
@@ -311,8 +325,10 @@
             pltpu.VMEM((m, m), BF16),
             pltpu.VMEM((m, m), BF16),
             pltpu.VMEM((m, m), BF16),
+            pltpu.VMEM((m, n), BF16),
+            pltpu.VMEM((m, n), BF16),
             pltpu.SemaphoreType.DMA,
-            pltpu.SemaphoreType.DMA((n // chunk,)),
+            pltpu.SemaphoreType.DMA((n // chunk + 1,)),
         ],
         compiler_params=pltpu.CompilerParams(vmem_limit_bytes=VMEM),
         cost_estimate=pl.CostEstimate(flops=12 * m * k * n, bytes_accessed=8 * m * n, transcendentals=0),

time: 72.9 us -> 73.3 us (level)
  starting transfers between devices: 26.6 us -> 28.1 us
    ppermute x14, waiting for transfers between devices: 20.5 us -> 19.3 us  [shifted(): return lax.ppermute(v, AXES, pairs)]
    all_to_all x1, starting transfers between devices: 7.24 us -> 8.18 us  [summed(): arrived = lax.all_to_all(copies, axis, 0, 0, tiled=True)]
where the time goes in v5:
time: 73.3 us; the launch traced here: 73.1 us
  starting transfers between devices  28.1 us (38%)
  waiting for transfers between devices  25.9 us (35%)
  Pallas kernels  17.8 us (24%)
  local copies, waits for them, and re-layouts  0.84 us (1%)
    ppermute x14, starting transfers between devices, shifted(): return lax.ppermute(v, AXES, pairs)  20 us
    ppermute x14, waiting for transfers between devices, shifted(): return lax.ppermute(v, AXES, pairs)  19.3 us
    pallas_call x1, Pallas kernels, corrected(): pl.pallas_call(functools.partial(finish_kernel, pixel_total, chunk, sizes...  11.3 us
    all_to_all x1, starting transfers between devices, summed(): arrived = lax.all_to_all(copies, axis, 0, 0, tiled=True)  8.18 us
    all_to_all x1, waiting for transfers between devices, summed(): arrived = lax.all_to_all(copies, axis, 0, 0, tiled=True)  6.61 us
    pallas_call x1, Pallas kernels, upper_gram(): pl.pallas_call(gram_kernel, out_shape=jax.ShapeDtypeStruct((lines, TILE),...  4.52 us
    pallas_call x1, Pallas kernels, start_rows(): pl.pallas_call(start_kernel, out_shape=jax.ShapeDtypeStruct((k, m), F32),...  2.02 us
  transfers between devices with their start and end apart: 15, of which 11 were waited for; matrix products, arithmetic and copies ran while one was open for 0% of the time, Pallas kernels for 3%

profile of v5, /device:TPU:1, one launch (start us, length us, event | category | flops | bytes accessed | tf_op | source)
XLA Modules:
  0.0 73.1 jit_solution(10278982416740372816)
XLA Ops:
  0.0 0.0 copy-start
  0.0 4.5 %gram.1 = f32[1280,128]{1,0:T(8,128)S(1)} custom-call(f32[512,2048]{1,0:T(8,128)} %x_hbm.3), custom_call_target="tpu_custom_call" | custom-call | flops 3221225472 | bytes 4194304 | tf_op jit(solution)/shard_map/gram/pallas_call | solution.py:147
  4.6 3.3 %collective-permute-start = (f32[640,128]{1,0:T(8,128)S(1)}, f32[640,128]{1,0:T(8,128)S(1)}, u32[]{:S(2)}, u32[]{:S(2)}) collective-permute-start(f32[640,128]{1,0:T(8,128)S(1)} %constant_dynamic-slice_fusion.6), channel_id=1, source_target_pairs={{0,32},{1,33},{2,34},{3,35},{4,36},{5,37},{6,38},{7,39},{8,40},{9,... | collective-permute-start | bytes 983048 | tf_op jit(solution)/shard_map/ppermute | solution.py:48
  7.9 1.3 %collective-permute-done = f32[640,128]{1,0:T(8,128)S(1)} collective-permute-done((f32[640,128]{1,0:T(8,128)S(1)}, f32[640,128]{1,0:T(8,128)S(1)}, u32[]{:S(2)}, u32[]{:S(2)}) %collective-permute-start) | collective-permute-done | bytes 327712 | tf_op jit(solution)/shard_map/ppermute | solution.py:48
  9.2 1.3 %collective-permute-start.1 = (f32[160,128]{1,0:T(8,128)S(1)}, f32[160,128]{1,0:T(8,128)S(1)}, u32[]{:S(2)}, u32[]{:S(2)}) collective-permute-start(f32[160,128]{1,0:T(8,128)S(1)} %get-tuple-element.9), channel_id=1, source_target_pairs={{0,128},{1,129},{2,130},{3,131},{4,132},{5,133},{6,134},{7,135},{8... | collective-permute-start | bytes 245768 | tf_op jit(solution)/shard_map/ppermute | solution.py:48
  10.5 1.3 %collective-permute-start.3 = (f32[160,128]{1,0:T(8,128)S(1)}, f32[160,128]{1,0:T(8,128)S(1)}, u32[]{:S(2)}, u32[]{:S(2)}) collective-permute-start(f32[160,128]{1,0:T(8,128)S(1)} %get-tuple-element.10), channel_id=1, source_target_pairs={{0,224},{1,225},{2,226},{3,227},{4,228},{5,229},{6,230},{7,231},{8... | collective-permute-start | bytes 245768 | tf_op jit(solution)/shard_map/ppermute | solution.py:48
  11.8 0.4 collective-permute-start.2
  12.2 2.2 %collective-permute-done.1 = f32[160,128]{1,0:T(8,128)S(1)} collective-permute-done((f32[160,128]{1,0:T(8,128)S(1)}, f32[160,128]{1,0:T(8,128)S(1)}, u32[]{:S(2)}, u32[]{:S(2)}) %collective-permute-start.1) | collective-permute-done | bytes 81952 | tf_op jit(solution)/shard_map/ppermute | solution.py:48
  14.5 1.2 %collective-permute-done.3 = f32[160,128]{1,0:T(8,128)S(1)} collective-permute-done((f32[160,128]{1,0:T(8,128)S(1)}, f32[160,128]{1,0:T(8,128)S(1)}, u32[]{:S(2)}, u32[]{:S(2)}) %collective-permute-start.3) | collective-permute-done | bytes 81952 | tf_op jit(solution)/shard_map/ppermute | solution.py:48
  15.7 1.3 %collective-permute-done.2 = f32[160,128]{1,0:T(8,128)S(1)} collective-permute-done((f32[160,128]{1,0:T(8,128)S(1)}, f32[160,128]{1,0:T(8,128)S(1)}, u32[]{:S(2)}, u32[]{:S(2)}) %collective-permute-start.2) | collective-permute-done | bytes 81952 | tf_op jit(solution)/shard_map/ppermute | solution.py:48
  17.0 2.8 %collective-permute-start.4 = (f32[40,128]{1,0:T(8,128)S(1)}, f32[40,128]{1,0:T(8,128)S(1)}, u32[]{:S(2)}, u32[]{:S(2)}) collective-permute-start(f32[40,128]{1,0:T(8,128)S(1)} %get-tuple-element.18), channel_id=1, source_target_pairs={{0,16},{1,17},{2,18},{3,19},{4,20},{5,21},{6,22},{7,23},{8,24},{9,... | collective-permute-start | bytes 61448 | tf_op jit(solution)/shard_map/ppermute | solution.py:48
  19.8 0.9 %collective-permute-start.6 = (f32[40,128]{1,0:T(8,128)S(1)}, f32[40,128]{1,0:T(8,128)S(1)}, u32[]{:S(2)}, u32[]{:S(2)}) collective-permute-start(f32[40,128]{1,0:T(8,128)S(1)} %get-tuple-element.19), channel_id=1, source_target_pairs={{0,56},{1,57},{2,58},{3,59},{4,60},{5,61},{6,62},{7,63},{8,32},{9,... | collective-permute-start | bytes 61448 | tf_op jit(solution)/shard_map/ppermute | solution.py:48
  20.7 0.8 %collective-permute-start.5 = (f32[40,128]{1,0:T(8,128)S(1)}, f32[40,128]{1,0:T(8,128)S(1)}, u32[]{:S(2)}, u32[]{:S(2)}) collective-permute-start(f32[40,128]{1,0:T(8,128)S(1)} %get-tuple-element.20), channel_id=1, source_target_pairs={{0,40},{1,41},{2,42},{3,43},{4,44},{5,45},{6,46},{7,47},{8,48},{9,... | collective-permute-start | bytes 61448 | tf_op jit(solution)/shard_map/ppermute | solution.py:48
  21.5 0.0 collective-permute-done.4
  21.6 1.5 %collective-permute-done.6 = f32[40,128]{1,0:T(8,128)S(1)} collective-permute-done((f32[40,128]{1,0:T(8,128)S(1)}, f32[40,128]{1,0:T(8,128)S(1)}, u32[]{:S(2)}, u32[]{:S(2)}) %collective-permute-start.6) | collective-permute-done | bytes 20512 | tf_op jit(solution)/shard_map/ppermute | solution.py:48
  23.0 2.1 %collective-permute-done.5 = f32[40,128]{1,0:T(8,128)S(1)} collective-permute-done((f32[40,128]{1,0:T(8,128)S(1)}, f32[40,128]{1,0:T(8,128)S(1)}, u32[]{:S(2)}, u32[]{:S(2)}) %collective-permute-start.5) | collective-permute-done | bytes 20512 | tf_op jit(solution)/shard_map/ppermute | solution.py:48
  25.2 0.7 broadcast_in_dim.2
  25.8 8.2 %all-to-all-start = ((f32[8,40,128]{2,1,0:T(8,128)}), f32[8,40,128]{2,1,0:T(8,128)S(1)}, u32[]{:S(2)}, u32[]{:S(2)}) async-start(f32[8,40,128]{2,1,0:T(8,128)} %broadcast_in_dim.2), calls=%async_computation | async-start | bytes 327680 | tf_op jit(solution)/shard_map/all_to_all | solution.py:73
  34.0 0.0 copy-done
  34.0 2.0 %start_rows.1.v_ref = f32[64,512]{1,0:T(8,128)S(1)} custom-call(f32[64,512]{1,0:T(8,128)S(1)} %bitcast.4), custom_call_target="tpu_custom_call" | custom-call | flops 8000000000 | bytes 262144 | tf_op jit(solution)/shard_map/start_rows/pallas_call | solution.py:216
  36.0 6.6 %all-to-all-done = f32[8,40,128]{2,1,0:T(8,128)S(1)} async-done(((f32[8,40,128]{2,1,0:T(8,128)}), f32[8,40,128]{2,1,0:T(8,128)S(1)}, u32[]{:S(2)}, u32[]{:S(2)}) %all-to-all-start) | async-done | bytes 163872 | tf_op jit(solution)/shard_map/all_to_all | solution.py:73
  42.7 2.0 %collective-permute-start.9 = (f32[40,128]{1,0:T(8,128)S(1)}, f32[40,128]{1,0:T(8,128)S(1)}, u32[]{:S(2)}, u32[]{:S(2)}) collective-permute-start(f32[40,128]{1,0:T(8,128)S(1)} %reduce_sum.9), channel_id=1, source_target_pairs={{0,56},{1,57},{2,58},{3,59},{4,60},{5,61},{6,62},{7,63},{8,32},{9,... | collective-permute-start | bytes 61448 | tf_op jit(solution)/shard_map/ppermute | solution.py:48
  44.7 0.0 collective-permute-start.8
  44.7 1.3 %collective-permute-start.7 = (f32[40,128]{1,0:T(8,128)S(1)}, f32[40,128]{1,0:T(8,128)S(1)}, u32[]{:S(2)}, u32[]{:S(2)}) collective-permute-start(f32[40,128]{1,0:T(8,128)S(1)} %reduce_sum.9), channel_id=1, source_target_pairs={{0,16},{1,17},{2,18},{3,19},{4,20},{5,21},{6,22},{7,23},{8,24},{9,... | collective-permute-start | bytes 61448 | tf_op jit(solution)/shard_map/ppermute | solution.py:48
  45.9 2.9 %collective-permute-done.7 = f32[40,128]{1,0:T(8,128)S(1)} collective-permute-done((f32[40,128]{1,0:T(8,128)S(1)}, f32[40,128]{1,0:T(8,128)S(1)}, u32[]{:S(2)}, u32[]{:S(2)}) %collective-permute-start.7) | collective-permute-done | bytes 20512 | tf_op jit(solution)/shard_map/ppermute | solution.py:48
  48.9 0.2 collective-permute-done.8
  49.1 0.0 collective-permute-done.9
  49.1 3.0 %collective-permute-start.10 = (f32[160,128]{1,0:T(8,128)S(1)}, f32[160,128]{1,0:T(8,128)S(1)}, u32[]{:S(2)}, u32[]{:S(2)}) collective-permute-start(f32[160,128]{1,0:T(8,128)S(1)} %get-tuple-element.23), channel_id=1, source_target_pairs={{0,128},{1,129},{2,130},{3,131},{4,132},{5,133},{6,134},{7,135},{8... | collective-permute-start | bytes 245768 | tf_op jit(solution)/shard_map/ppermute | solution.py:48
  52.1 2.7 %collective-permute-start.12 = (f32[160,128]{1,0:T(8,128)S(1)}, f32[160,128]{1,0:T(8,128)S(1)}, u32[]{:S(2)}, u32[]{:S(2)}) collective-permute-start(f32[160,128]{1,0:T(8,128)S(1)} %get-tuple-element.23), channel_id=1, source_target_pairs={{0,224},{1,225},{2,226},{3,227},{4,228},{5,229},{6,230},{7,231},{8... | collective-permute-start | bytes 245768 | tf_op jit(solution)/shard_map/ppermute | solution.py:48
  54.8 0.0 collective-permute-start.11
  54.8 0.0 collective-permute-done.10
  54.8 5.1 %collective-permute-done.11 = f32[160,128]{1,0:T(8,128)S(1)} collective-permute-done((f32[160,128]{1,0:T(8,128)S(1)}, f32[160,128]{1,0:T(8,128)S(1)}, u32[]{:S(2)}, u32[]{:S(2)}) %collective-permute-start.11) | collective-permute-done | bytes 81952 | tf_op jit(solution)/shard_map/ppermute | solution.py:48
  59.9 0.0 collective-permute-done.12
  59.9 0.1 collective-permute-start.13
  60.0 0.1 pad_add_fusion.me_ref
  60.1 1.5 %collective-permute-done.13 = f32[640,128]{1,0:T(8,128)S(1)} collective-permute-done((f32[640,128]{1,0:T(8,128)S(1)}, f32[640,128]{1,0:T(8,128)S(1)}, u32[]{:S(2)}, u32[]{:S(2)}) %collective-permute-start.13) | collective-permute-done | bytes 327712 | tf_op jit(solution)/shard_map/ppermute | solution.py:48
  61.7 11.3 %finish.1 = f32[512,2048]{1,0:T(8,128)} custom-call(s32[3]{0:T(128)S(1)} %pad_add_fusion.me_ref, f32[1280,128]{1,0:T(8,128)S(1)} %constant_dynamic-update-slice_fusion.11.lines_ref, f32[64,512]{1,0:T(8,128)S(1)} %start_rows.1.v_ref, f32[512,2048]{1,0:T(8,128)} %x_hbm.3), custom_call_target="tpu_custom_call" | custom-call | flops 805306368 | bytes 8388608 | tf_op jit(solution)/shard_map/finish/pallas_call | solution.py:311
  (15 shorter events, 0.2 us)
Async XLA Ops:
  0.0 34.0 %copy-start = (f32[512,64]{0,1:T(8,128)S(1)}, f32[512,64]{0,1:T(8,128)}, u32[]{:S(2)}) copy-start(f32[512,64]{0,1:T(8,128)} %param.3) | copy-start | bytes 393220
  4.6 4.6 %collective-permute-start = (f32[640,128]{1,0:T(8,128)S(1)}, f32[640,128]{1,0:T(8,128)S(1)}, u32[]{:S(2)}, u32[]{:S(2)}) collective-permute-start(f32[640,128]{1,0:T(8,128)S(1)} %constant_dynamic-slice_fusion.6), channel_id=1, source_target_pairs={{0,32},{1,33},{2,34},{3,35},{4,36},{5,37},{6,38},{7,39},{8,40},{9,... | collective-permute-start | bytes 983048 | tf_op jit(solution)/shard_map/ppermute | solution.py:48
  9.2 5.2 %collective-permute-start.1 = (f32[160,128]{1,0:T(8,128)S(1)}, f32[160,128]{1,0:T(8,128)S(1)}, u32[]{:S(2)}, u32[]{:S(2)}) collective-permute-start(f32[160,128]{1,0:T(8,128)S(1)} %get-tuple-element.9), channel_id=1, source_target_pairs={{0,128},{1,129},{2,130},{3,131},{4,132},{5,133},{6,134},{7,135},{8... | collective-permute-start | bytes 245768 | tf_op jit(solution)/shard_map/ppermute | solution.py:48
  10.5 5.2 %collective-permute-start.3 = (f32[160,128]{1,0:T(8,128)S(1)}, f32[160,128]{1,0:T(8,128)S(1)}, u32[]{:S(2)}, u32[]{:S(2)}) collective-permute-start(f32[160,128]{1,0:T(8,128)S(1)} %get-tuple-element.10), channel_id=1, source_target_pairs={{0,224},{1,225},{2,226},{3,227},{4,228},{5,229},{6,230},{7,231},{8... | collective-permute-start | bytes 245768 | tf_op jit(solution)/shard_map/ppermute | solution.py:48
  11.8 5.1 %collective-permute-start.2 = (f32[160,128]{1,0:T(8,128)S(1)}, f32[160,128]{1,0:T(8,128)S(1)}, u32[]{:S(2)}, u32[]{:S(2)}) collective-permute-start(f32[160,128]{1,0:T(8,128)S(1)} %get-tuple-element.11), channel_id=1, source_target_pairs={{0,96},{1,97},{2,98},{3,99},{4,100},{5,101},{6,102},{7,103},{8,104... | collective-permute-start | bytes 245768 | tf_op jit(solution)/shard_map/ppermute | solution.py:48
  17.0 4.6 %collective-permute-start.4 = (f32[40,128]{1,0:T(8,128)S(1)}, f32[40,128]{1,0:T(8,128)S(1)}, u32[]{:S(2)}, u32[]{:S(2)}) collective-permute-start(f32[40,128]{1,0:T(8,128)S(1)} %get-tuple-element.18), channel_id=1, source_target_pairs={{0,16},{1,17},{2,18},{3,19},{4,20},{5,21},{6,22},{7,23},{8,24},{9,... | collective-permute-start | bytes 61448 | tf_op jit(solution)/shard_map/ppermute | solution.py:48
  19.8 3.2 %collective-permute-start.6 = (f32[40,128]{1,0:T(8,128)S(1)}, f32[40,128]{1,0:T(8,128)S(1)}, u32[]{:S(2)}, u32[]{:S(2)}) collective-permute-start(f32[40,128]{1,0:T(8,128)S(1)} %get-tuple-element.19), channel_id=1, source_target_pairs={{0,56},{1,57},{2,58},{3,59},{4,60},{5,61},{6,62},{7,63},{8,32},{9,... | collective-permute-start | bytes 61448 | tf_op jit(solution)/shard_map/ppermute | solution.py:48
  20.7 4.4 %collective-permute-start.5 = (f32[40,128]{1,0:T(8,128)S(1)}, f32[40,128]{1,0:T(8,128)S(1)}, u32[]{:S(2)}, u32[]{:S(2)}) collective-permute-start(f32[40,128]{1,0:T(8,128)S(1)} %get-tuple-element.20), channel_id=1, source_target_pairs={{0,40},{1,41},{2,42},{3,43},{4,44},{5,45},{6,46},{7,47},{8,48},{9,... | collective-permute-start | bytes 61448 | tf_op jit(solution)/shard_map/ppermute | solution.py:48
  25.8 16.8 %all-to-all-start = ((f32[8,40,128]{2,1,0:T(8,128)}), f32[8,40,128]{2,1,0:T(8,128)S(1)}, u32[]{:S(2)}, u32[]{:S(2)}) async-start(f32[8,40,128]{2,1,0:T(8,128)} %broadcast_in_dim.2), calls=%async_computation | async-start | bytes 327680 | tf_op jit(solution)/shard_map/all_to_all | solution.py:73
  42.7 6.4 %collective-permute-start.9 = (f32[40,128]{1,0:T(8,128)S(1)}, f32[40,128]{1,0:T(8,128)S(1)}, u32[]{:S(2)}, u32[]{:S(2)}) collective-permute-start(f32[40,128]{1,0:T(8,128)S(1)} %reduce_sum.9), channel_id=1, source_target_pairs={{0,56},{1,57},{2,58},{3,59},{4,60},{5,61},{6,62},{7,63},{8,32},{9,... | collective-permute-start | bytes 61448 | tf_op jit(solution)/shard_map/ppermute | solution.py:48
  44.7 4.4 %collective-permute-start.8 = (f32[40,128]{1,0:T(8,128)S(1)}, f32[40,128]{1,0:T(8,128)S(1)}, u32[]{:S(2)}, u32[]{:S(2)}) collective-permute-start(f32[40,128]{1,0:T(8,128)S(1)} %reduce_sum.9), channel_id=1, source_target_pairs={{0,40},{1,41},{2,42},{3,43},{4,44},{5,45},{6,46},{7,47},{8,48},{9,... | collective-permute-start | bytes 61448 | tf_op jit(solution)/shard_map/ppermute | solution.py:48
  44.7 4.2 %collective-permute-start.7 = (f32[40,128]{1,0:T(8,128)S(1)}, f32[40,128]{1,0:T(8,128)S(1)}, u32[]{:S(2)}, u32[]{:S(2)}) collective-permute-start(f32[40,128]{1,0:T(8,128)S(1)} %reduce_sum.9), channel_id=1, source_target_pairs={{0,16},{1,17},{2,18},{3,19},{4,20},{5,21},{6,22},{7,23},{8,24},{9,... | collective-permute-start | bytes 61448 | tf_op jit(solution)/shard_map/ppermute | solution.py:48
  49.1 5.7 %collective-permute-start.10 = (f32[160,128]{1,0:T(8,128)S(1)}, f32[160,128]{1,0:T(8,128)S(1)}, u32[]{:S(2)}, u32[]{:S(2)}) collective-permute-start(f32[160,128]{1,0:T(8,128)S(1)} %get-tuple-element.23), channel_id=1, source_target_pairs={{0,128},{1,129},{2,130},{3,131},{4,132},{5,133},{6,134},{7,135},{8... | collective-permute-start | bytes 245768 | tf_op jit(solution)/shard_map/ppermute | solution.py:48
  52.1 7.8 %collective-permute-start.12 = (f32[160,128]{1,0:T(8,128)S(1)}, f32[160,128]{1,0:T(8,128)S(1)}, u32[]{:S(2)}, u32[]{:S(2)}) collective-permute-start(f32[160,128]{1,0:T(8,128)S(1)} %get-tuple-element.23), channel_id=1, source_target_pairs={{0,224},{1,225},{2,226},{3,227},{4,228},{5,229},{6,230},{7,231},{8... | collective-permute-start | bytes 245768 | tf_op jit(solution)/shard_map/ppermute | solution.py:48
  54.8 5.1 %collective-permute-start.11 = (f32[160,128]{1,0:T(8,128)S(1)}, f32[160,128]{1,0:T(8,128)S(1)}, u32[]{:S(2)}, u32[]{:S(2)}) collective-permute-start(f32[160,128]{1,0:T(8,128)S(1)} %get-tuple-element.23), channel_id=1, source_target_pairs={{0,96},{1,97},{2,98},{3,99},{4,100},{5,101},{6,102},{7,103},{8,104... | collective-permute-start | bytes 245768 | tf_op jit(solution)/shard_map/ppermute | solution.py:48
  59.9 1.7 %collective-permute-start.13 = (f32[640,128]{1,0:T(8,128)S(1)}, f32[640,128]{1,0:T(8,128)S(1)}, u32[]{:S(2)}, u32[]{:S(2)}) collective-permute-start(f32[640,128]{1,0:T(8,128)S(1)} %get-tuple-element.12), channel_id=1, source_target_pairs={{0,32},{1,33},{2,34},{3,35},{4,36},{5,37},{6,38},{7,39},{8,40},{9,... | collective-permute-start | bytes 983048 | tf_op jit(solution)/shard_map/ppermute | solution.py:48

commit v6 on v5

--- a/solution.py
+++ b/solution.py
@@ -25,7 +25,7 @@
 
 
 def half():
-    return (lax.axis_index("c") + lax.axis_index("x") + lax.axis_index("y")) % 2
+    return sum(lax.axis_index(axis) for axis in AXES) % 2
 
 
 def place_on(axis):
@@ -68,10 +68,12 @@
 
 
 def summed(v, axis):
-    n = lax.axis_size(axis)
-    copies = jnp.broadcast_to(v[None], (n, *v.shape)).reshape(n * v.shape[0], *v.shape[1:])
-    arrived = lax.all_to_all(copies, axis, 0, 0, tiled=True)
-    return arrived.reshape(n, *v.shape).sum(axis=0)
+    pairs = lax.axis_size(axis) // 2
+    v = v + shifted(v, axis, pairs)
+    arrived = [shifted(v, axis, k if 2 * k <= pairs else k - pairs) for k in steps(pairs)]
+    for part in arrived:
+        v = v + part
+    return v
 
 
 def sum_everywhere(v, meanwhile):

time: 73.3 us -> 72.8 us (level)
  starting transfers between devices: 28.1 us -> 30.1 us
  waiting for transfers between devices: 25.9 us -> 24.1 us
    ppermute x14 -> x18, starting transfers between devices: 20 us -> 30.1 us  [shifted(): return lax.ppermute(v, AXES, pairs)]
    all_to_all x1 -> x0, starting transfers between devices: 8.18 us -> none  [summed(): arrived = lax.all_to_all(copies, axis, 0, 0, tiled=True)]
    all_to_all x1 -> x0, waiting for transfers between devices: 6.61 us -> none  [summed(): arrived = lax.all_to_all(copies, axis, 0, 0, tiled=True)]
    ppermute x14 -> x18, waiting for transfers between devices: 19.3 us -> 24.1 us  [shifted(): return lax.ppermute(v, AXES, pairs)]
  transfers between devices with their start and end apart: 15 -> 18, of which waited for: 11 -> 13; matrix products, arithmetic and copies ran while one was open for 0% -> 0% of each run, Pallas kernels for 3% -> 3%
where the time goes in v6:
time: 72.8 us; the launch traced here: 72.7 us
  starting transfers between devices  30.1 us (41%)
  waiting for transfers between devices  24.1 us (33%)
  Pallas kernels  17.8 us (24%)
    ppermute x18, starting transfers between devices, shifted(): return lax.ppermute(v, AXES, pairs)  30.1 us
    ppermute x18, waiting for transfers between devices, shifted(): return lax.ppermute(v, AXES, pairs)  24.1 us
    pallas_call x1, Pallas kernels, corrected(): pl.pallas_call(functools.partial(finish_kernel, pixel_total, chunk, sizes...  11.3 us
    pallas_call x1, Pallas kernels, upper_gram(): pl.pallas_call(gram_kernel, out_shape=jax.ShapeDtypeStruct((lines, TILE),...  4.52 us
    pallas_call x1, Pallas kernels, start_rows(): pl.pallas_call(start_kernel, out_shape=jax.ShapeDtypeStruct((k, m), F32),...  2.02 us
  transfers between devices with their start and end apart: 18, of which 13 were waited for; matrix products, arithmetic and copies ran while one was open for 0% of the time, Pallas kernels for 3%

profile of v6, /device:TPU:1, one launch (start us, length us, event | category | flops | bytes accessed | tf_op | source)
XLA Modules:
  0.0 72.7 jit_solution(5945180024020530491)
XLA Ops:
  0.0 0.0 copy-start
  0.0 4.5 %gram.1 = f32[1280,128]{1,0:T(8,128)S(1)} custom-call(f32[512,2048]{1,0:T(8,128)} %x_hbm.3), custom_call_target="tpu_custom_call" | custom-call | flops 3221225472 | bytes 4194304 | tf_op jit(solution)/shard_map/gram/pallas_call | solution.py:149
  4.6 3.3 %collective-permute-start = (f32[640,128]{1,0:T(8,128)S(1)}, f32[640,128]{1,0:T(8,128)S(1)}, u32[]{:S(2)}, u32[]{:S(2)}) collective-permute-start(f32[640,128]{1,0:T(8,128)S(1)} %constant_dynamic-slice_fusion.6), channel_id=1, source_target_pairs={{0,32},{1,33},{2,34},{3,35},{4,36},{5,37},{6,38},{7,39},{8,40},{9,... | collective-permute-start | bytes 983048 | tf_op jit(solution)/shard_map/ppermute | solution.py:48
  7.9 1.3 %collective-permute-done = f32[640,128]{1,0:T(8,128)S(1)} collective-permute-done((f32[640,128]{1,0:T(8,128)S(1)}, f32[640,128]{1,0:T(8,128)S(1)}, u32[]{:S(2)}, u32[]{:S(2)}) %collective-permute-start) | collective-permute-done | bytes 327712 | tf_op jit(solution)/shard_map/ppermute | solution.py:48
  9.2 1.3 %collective-permute-start.1 = (f32[160,128]{1,0:T(8,128)S(1)}, f32[160,128]{1,0:T(8,128)S(1)}, u32[]{:S(2)}, u32[]{:S(2)}) collective-permute-start(f32[160,128]{1,0:T(8,128)S(1)} %get-tuple-element.9), channel_id=1, source_target_pairs={{0,128},{1,129},{2,130},{3,131},{4,132},{5,133},{6,134},{7,135},{8... | collective-permute-start | bytes 245768 | tf_op jit(solution)/shard_map/ppermute | solution.py:48
  10.5 1.3 %collective-permute-start.3 = (f32[160,128]{1,0:T(8,128)S(1)}, f32[160,128]{1,0:T(8,128)S(1)}, u32[]{:S(2)}, u32[]{:S(2)}) collective-permute-start(f32[160,128]{1,0:T(8,128)S(1)} %get-tuple-element.10), channel_id=1, source_target_pairs={{0,224},{1,225},{2,226},{3,227},{4,228},{5,229},{6,230},{7,231},{8... | collective-permute-start | bytes 245768 | tf_op jit(solution)/shard_map/ppermute | solution.py:48
  11.8 0.4 collective-permute-start.2
  12.2 2.2 %collective-permute-done.1 = f32[160,128]{1,0:T(8,128)S(1)} collective-permute-done((f32[160,128]{1,0:T(8,128)S(1)}, f32[160,128]{1,0:T(8,128)S(1)}, u32[]{:S(2)}, u32[]{:S(2)}) %collective-permute-start.1) | collective-permute-done | bytes 81952 | tf_op jit(solution)/shard_map/ppermute | solution.py:48
  14.5 1.2 %collective-permute-done.3 = f32[160,128]{1,0:T(8,128)S(1)} collective-permute-done((f32[160,128]{1,0:T(8,128)S(1)}, f32[160,128]{1,0:T(8,128)S(1)}, u32[]{:S(2)}, u32[]{:S(2)}) %collective-permute-start.3) | collective-permute-done | bytes 81952 | tf_op jit(solution)/shard_map/ppermute | solution.py:48
  15.7 1.3 %collective-permute-done.2 = f32[160,128]{1,0:T(8,128)S(1)} collective-permute-done((f32[160,128]{1,0:T(8,128)S(1)}, f32[160,128]{1,0:T(8,128)S(1)}, u32[]{:S(2)}, u32[]{:S(2)}) %collective-permute-start.2) | collective-permute-done | bytes 81952 | tf_op jit(solution)/shard_map/ppermute | solution.py:48
  17.0 2.8 %collective-permute-start.4 = (f32[40,128]{1,0:T(8,128)S(1)}, f32[40,128]{1,0:T(8,128)S(1)}, u32[]{:S(2)}, u32[]{:S(2)}) collective-permute-start(f32[40,128]{1,0:T(8,128)S(1)} %get-tuple-element.18), channel_id=1, source_target_pairs={{0,16},{1,17},{2,18},{3,19},{4,20},{5,21},{6,22},{7,23},{8,24},{9,... | collective-permute-start | bytes 61448 | tf_op jit(solution)/shard_map/ppermute | solution.py:48
  19.8 0.9 %collective-permute-start.6 = (f32[40,128]{1,0:T(8,128)S(1)}, f32[40,128]{1,0:T(8,128)S(1)}, u32[]{:S(2)}, u32[]{:S(2)}) collective-permute-start(f32[40,128]{1,0:T(8,128)S(1)} %get-tuple-element.19), channel_id=1, source_target_pairs={{0,56},{1,57},{2,58},{3,59},{4,60},{5,61},{6,62},{7,63},{8,32},{9,... | collective-permute-start | bytes 61448 | tf_op jit(solution)/shard_map/ppermute | solution.py:48
  20.7 0.8 %collective-permute-start.5 = (f32[40,128]{1,0:T(8,128)S(1)}, f32[40,128]{1,0:T(8,128)S(1)}, u32[]{:S(2)}, u32[]{:S(2)}) collective-permute-start(f32[40,128]{1,0:T(8,128)S(1)} %get-tuple-element.20), channel_id=1, source_target_pairs={{0,40},{1,41},{2,42},{3,43},{4,44},{5,45},{6,46},{7,47},{8,48},{9,... | collective-permute-start | bytes 61448 | tf_op jit(solution)/shard_map/ppermute | solution.py:48
  21.5 0.0 collective-permute-done.4
  21.6 1.5 %collective-permute-done.6 = f32[40,128]{1,0:T(8,128)S(1)} collective-permute-done((f32[40,128]{1,0:T(8,128)S(1)}, f32[40,128]{1,0:T(8,128)S(1)}, u32[]{:S(2)}, u32[]{:S(2)}) %collective-permute-start.6) | collective-permute-done | bytes 20512 | tf_op jit(solution)/shard_map/ppermute | solution.py:48
  23.0 2.1 %collective-permute-done.5 = f32[40,128]{1,0:T(8,128)S(1)} collective-permute-done((f32[40,128]{1,0:T(8,128)S(1)}, f32[40,128]{1,0:T(8,128)S(1)}, u32[]{:S(2)}, u32[]{:S(2)}) %collective-permute-start.5) | collective-permute-done | bytes 20512 | tf_op jit(solution)/shard_map/ppermute | solution.py:48
  25.2 7.0 %collective-permute-start.7 = (f32[40,128]{1,0:T(8,128)S(1)}, f32[40,128]{1,0:T(8,128)S(1)}, u32[]{:S(2)}, u32[]{:S(2)}) collective-permute-start(f32[40,128]{1,0:T(8,128)S(1)} %add_add_fusion.2), channel_id=1, source_target_pairs={{0,4},{1,5},{2,6},{3,7},{4,0},{5,1},{6,2},{7,3},{8,12},{9,13},{10,... | collective-permute-start | bytes 61448 | tf_op jit(solution)/shard_map/ppermute | solution.py:48
  32.1 1.2 %collective-permute-done.7 = f32[40,128]{1,0:T(8,128)S(1)} collective-permute-done((f32[40,128]{1,0:T(8,128)S(1)}, f32[40,128]{1,0:T(8,128)S(1)}, u32[]{:S(2)}, u32[]{:S(2)}) %collective-permute-start.7) | collective-permute-done | bytes 20512 | tf_op jit(solution)/shard_map/ppermute | solution.py:48
  33.3 5.4 %collective-permute-start.10 = (f32[40,128]{1,0:T(8,128)S(1)}, f32[40,128]{1,0:T(8,128)S(1)}, u32[]{:S(2)}, u32[]{:S(2)}) collective-permute-start(f32[40,128]{1,0:T(8,128)S(1)} %add.129), channel_id=1, source_target_pairs={{0,39},{1,32},{2,33},{3,34},{4,35},{5,36},{6,37},{7,38},{8,47},{9,... | collective-permute-start | bytes 61448 | tf_op jit(solution)/shard_map/ppermute | solution.py:48
  38.7 0.0 collective-permute-start.9
  38.7 0.0 collective-permute-start.8
  38.7 0.0 copy-done
  38.7 2.0 %start_rows.1.v_ref = f32[64,512]{1,0:T(8,128)S(1)} custom-call(f32[64,512]{1,0:T(8,128)S(1)} %bitcast.4), custom_call_target="tpu_custom_call" | custom-call | flops 8000000000 | bytes 262144 | tf_op jit(solution)/shard_map/start_rows/pallas_call | solution.py:218
  40.8 0.0 collective-permute-done.10
  40.8 2.6 %collective-permute-done.9 = f32[40,128]{1,0:T(8,128)S(1)} collective-permute-done((f32[40,128]{1,0:T(8,128)S(1)}, f32[40,128]{1,0:T(8,128)S(1)}, u32[]{:S(2)}, u32[]{:S(2)}) %collective-permute-start.9) | collective-permute-done | bytes 20512 | tf_op jit(solution)/shard_map/ppermute | solution.py:48
  43.4 0.1 collective-permute-done.8
  43.5 0.3 collective-permute-start.13
  43.8 1.7 %collective-permute-start.12 = (f32[40,128]{1,0:T(8,128)S(1)}, f32[40,128]{1,0:T(8,128)S(1)}, u32[]{:S(2)}, u32[]{:S(2)}) collective-permute-start(f32[40,128]{1,0:T(8,128)S(1)} %add_add_fusion.1), channel_id=1, source_target_pairs={{0,40},{1,41},{2,42},{3,43},{4,44},{5,45},{6,46},{7,47},{8,48},{9,... | collective-permute-start | bytes 61448 | tf_op jit(solution)/shard_map/ppermute | solution.py:48
  45.5 0.0 collective-permute-start.11
  45.6 4.1 %collective-permute-done.11 = f32[40,128]{1,0:T(8,128)S(1)} collective-permute-done((f32[40,128]{1,0:T(8,128)S(1)}, f32[40,128]{1,0:T(8,128)S(1)}, u32[]{:S(2)}, u32[]{:S(2)}) %collective-permute-start.11) | collective-permute-done | bytes 20512 | tf_op jit(solution)/shard_map/ppermute | solution.py:48
  49.7 0.0 collective-permute-done.12
  49.7 0.0 collective-permute-done.13
  49.7 1.8 %collective-permute-start.14 = (f32[160,128]{1,0:T(8,128)S(1)}, f32[160,128]{1,0:T(8,128)S(1)}, u32[]{:S(2)}, u32[]{:S(2)}) collective-permute-start(f32[160,128]{1,0:T(8,128)S(1)} %get-tuple-element.23), channel_id=1, source_target_pairs={{0,128},{1,129},{2,130},{3,131},{4,132},{5,133},{6,134},{7,135},{8... | collective-permute-start | bytes 245768 | tf_op jit(solution)/shard_map/ppermute | solution.py:48
  51.5 2.7 %collective-permute-start.16 = (f32[160,128]{1,0:T(8,128)S(1)}, f32[160,128]{1,0:T(8,128)S(1)}, u32[]{:S(2)}, u32[]{:S(2)}) collective-permute-start(f32[160,128]{1,0:T(8,128)S(1)} %get-tuple-element.23), channel_id=1, source_target_pairs={{0,224},{1,225},{2,226},{3,227},{4,228},{5,229},{6,230},{7,231},{8... | collective-permute-start | bytes 245768 | tf_op jit(solution)/shard_map/ppermute | solution.py:48
  54.2 0.0 collective-permute-start.15
  54.2 0.4 collective-permute-done.14
  54.6 4.6 %collective-permute-done.15 = f32[160,128]{1,0:T(8,128)S(1)} collective-permute-done((f32[160,128]{1,0:T(8,128)S(1)}, f32[160,128]{1,0:T(8,128)S(1)}, u32[]{:S(2)}, u32[]{:S(2)}) %collective-permute-start.15) | collective-permute-done | bytes 81952 | tf_op jit(solution)/shard_map/ppermute | solution.py:48
  59.3 0.0 collective-permute-done.16
  59.3 0.3 collective-permute-start.17
  59.6 0.1 pad_add_fusion.me_ref
  59.7 1.5 %collective-permute-done.17 = f32[640,128]{1,0:T(8,128)S(1)} collective-permute-done((f32[640,128]{1,0:T(8,128)S(1)}, f32[640,128]{1,0:T(8,128)S(1)}, u32[]{:S(2)}, u32[]{:S(2)}) %collective-permute-start.17) | collective-permute-done | bytes 327712 | tf_op jit(solution)/shard_map/ppermute | solution.py:48
  61.3 11.3 %finish.1 = f32[512,2048]{1,0:T(8,128)} custom-call(s32[3]{0:T(128)S(1)} %pad_add_fusion.me_ref, f32[1280,128]{1,0:T(8,128)S(1)} %constant_dynamic-update-slice_fusion.11.lines_ref, f32[64,512]{1,0:T(8,128)S(1)} %start_rows.1.v_ref, f32[512,2048]{1,0:T(8,128)} %x_hbm.3), custom_call_target="tpu_custom_call" | custom-call | flops 805306368 | bytes 8388608 | tf_op jit(solution)/shard_map/finish/pallas_call | solution.py:313
  (16 shorter events, 0.2 us)
Async XLA Ops:
  0.0 38.7 %copy-start = (f32[512,64]{0,1:T(8,128)S(1)}, f32[512,64]{0,1:T(8,128)}, u32[]{:S(2)}) copy-start(f32[512,64]{0,1:T(8,128)} %param.3) | copy-start | bytes 393220
  4.6 4.6 %collective-permute-start = (f32[640,128]{1,0:T(8,128)S(1)}, f32[640,128]{1,0:T(8,128)S(1)}, u32[]{:S(2)}, u32[]{:S(2)}) collective-permute-start(f32[640,128]{1,0:T(8,128)S(1)} %constant_dynamic-slice_fusion.6), channel_id=1, source_target_pairs={{0,32},{1,33},{2,34},{3,35},{4,36},{5,37},{6,38},{7,39},{8,40},{9,... | collective-permute-start | bytes 983048 | tf_op jit(solution)/shard_map/ppermute | solution.py:48
  9.2 5.2 %collective-permute-start.1 = (f32[160,128]{1,0:T(8,128)S(1)}, f32[160,128]{1,0:T(8,128)S(1)}, u32[]{:S(2)}, u32[]{:S(2)}) collective-permute-start(f32[160,128]{1,0:T(8,128)S(1)} %get-tuple-element.9), channel_id=1, source_target_pairs={{0,128},{1,129},{2,130},{3,131},{4,132},{5,133},{6,134},{7,135},{8... | collective-permute-start | bytes 245768 | tf_op jit(solution)/shard_map/ppermute | solution.py:48
  10.5 5.2 %collective-permute-start.3 = (f32[160,128]{1,0:T(8,128)S(1)}, f32[160,128]{1,0:T(8,128)S(1)}, u32[]{:S(2)}, u32[]{:S(2)}) collective-permute-start(f32[160,128]{1,0:T(8,128)S(1)} %get-tuple-element.10), channel_id=1, source_target_pairs={{0,224},{1,225},{2,226},{3,227},{4,228},{5,229},{6,230},{7,231},{8... | collective-permute-start | bytes 245768 | tf_op jit(solution)/shard_map/ppermute | solution.py:48
  11.8 5.1 %collective-permute-start.2 = (f32[160,128]{1,0:T(8,128)S(1)}, f32[160,128]{1,0:T(8,128)S(1)}, u32[]{:S(2)}, u32[]{:S(2)}) collective-permute-start(f32[160,128]{1,0:T(8,128)S(1)} %get-tuple-element.11), channel_id=1, source_target_pairs={{0,96},{1,97},{2,98},{3,99},{4,100},{5,101},{6,102},{7,103},{8,104... | collective-permute-start | bytes 245768 | tf_op jit(solution)/shard_map/ppermute | solution.py:48
  17.0 4.6 %collective-permute-start.4 = (f32[40,128]{1,0:T(8,128)S(1)}, f32[40,128]{1,0:T(8,128)S(1)}, u32[]{:S(2)}, u32[]{:S(2)}) collective-permute-start(f32[40,128]{1,0:T(8,128)S(1)} %get-tuple-element.18), channel_id=1, source_target_pairs={{0,16},{1,17},{2,18},{3,19},{4,20},{5,21},{6,22},{7,23},{8,24},{9,... | collective-permute-start | bytes 61448 | tf_op jit(solution)/shard_map/ppermute | solution.py:48
  19.8 3.2 %collective-permute-start.6 = (f32[40,128]{1,0:T(8,128)S(1)}, f32[40,128]{1,0:T(8,128)S(1)}, u32[]{:S(2)}, u32[]{:S(2)}) collective-permute-start(f32[40,128]{1,0:T(8,128)S(1)} %get-tuple-element.19), channel_id=1, source_target_pairs={{0,56},{1,57},{2,58},{3,59},{4,60},{5,61},{6,62},{7,63},{8,32},{9,... | collective-permute-start | bytes 61448 | tf_op jit(solution)/shard_map/ppermute | solution.py:48
  20.7 4.4 %collective-permute-start.5 = (f32[40,128]{1,0:T(8,128)S(1)}, f32[40,128]{1,0:T(8,128)S(1)}, u32[]{:S(2)}, u32[]{:S(2)}) collective-permute-start(f32[40,128]{1,0:T(8,128)S(1)} %get-tuple-element.20), channel_id=1, source_target_pairs={{0,40},{1,41},{2,42},{3,43},{4,44},{5,45},{6,46},{7,47},{8,48},{9,... | collective-permute-start | bytes 61448 | tf_op jit(solution)/shard_map/ppermute | solution.py:48
  25.2 8.2 %collective-permute-start.7 = (f32[40,128]{1,0:T(8,128)S(1)}, f32[40,128]{1,0:T(8,128)S(1)}, u32[]{:S(2)}, u32[]{:S(2)}) collective-permute-start(f32[40,128]{1,0:T(8,128)S(1)} %add_add_fusion.2), channel_id=1, source_target_pairs={{0,4},{1,5},{2,6},{3,7},{4,0},{5,1},{6,2},{7,3},{8,12},{9,13},{10,... | collective-permute-start | bytes 61448 | tf_op jit(solution)/shard_map/ppermute | solution.py:48
  33.3 7.5 %collective-permute-start.10 = (f32[40,128]{1,0:T(8,128)S(1)}, f32[40,128]{1,0:T(8,128)S(1)}, u32[]{:S(2)}, u32[]{:S(2)}) collective-permute-start(f32[40,128]{1,0:T(8,128)S(1)} %add.129), channel_id=1, source_target_pairs={{0,39},{1,32},{2,33},{3,34},{4,35},{5,36},{6,37},{7,38},{8,47},{9,... | collective-permute-start | bytes 61448 | tf_op jit(solution)/shard_map/ppermute | solution.py:48
  38.7 4.7 %collective-permute-start.9 = (f32[40,128]{1,0:T(8,128)S(1)}, f32[40,128]{1,0:T(8,128)S(1)}, u32[]{:S(2)}, u32[]{:S(2)}) collective-permute-start(f32[40,128]{1,0:T(8,128)S(1)} %add.129), channel_id=1, source_target_pairs={{0,33},{1,34},{2,35},{3,36},{4,37},{5,38},{6,39},{7,32},{8,41},{9,... | collective-permute-start | bytes 61448 | tf_op jit(solution)/shard_map/ppermute | solution.py:48
  38.7 4.8 %collective-permute-start.8 = (f32[40,128]{1,0:T(8,128)S(1)}, f32[40,128]{1,0:T(8,128)S(1)}, u32[]{:S(2)}, u32[]{:S(2)}) collective-permute-start(f32[40,128]{1,0:T(8,128)S(1)} %add.129), channel_id=1, source_target_pairs={{0,2},{1,3},{2,4},{3,5},{4,6},{5,7},{6,0},{7,1},{8,10},{9,11},{10,... | collective-permute-start | bytes 61448 | tf_op jit(solution)/shard_map/ppermute | solution.py:48
  43.5 6.2 %collective-permute-start.13 = (f32[40,128]{1,0:T(8,128)S(1)}, f32[40,128]{1,0:T(8,128)S(1)}, u32[]{:S(2)}, u32[]{:S(2)}) collective-permute-start(f32[40,128]{1,0:T(8,128)S(1)} %add_add_fusion.1), channel_id=1, source_target_pairs={{0,56},{1,57},{2,58},{3,59},{4,60},{5,61},{6,62},{7,63},{8,32},{9,... | collective-permute-start | bytes 61448 | tf_op jit(solution)/shard_map/ppermute | solution.py:48
  43.8 5.9 %collective-permute-start.12 = (f32[40,128]{1,0:T(8,128)S(1)}, f32[40,128]{1,0:T(8,128)S(1)}, u32[]{:S(2)}, u32[]{:S(2)}) collective-permute-start(f32[40,128]{1,0:T(8,128)S(1)} %add_add_fusion.1), channel_id=1, source_target_pairs={{0,40},{1,41},{2,42},{3,43},{4,44},{5,45},{6,46},{7,47},{8,48},{9,... | collective-permute-start | bytes 61448 | tf_op jit(solution)/shard_map/ppermute | solution.py:48
  45.5 4.1 %collective-permute-start.11 = (f32[40,128]{1,0:T(8,128)S(1)}, f32[40,128]{1,0:T(8,128)S(1)}, u32[]{:S(2)}, u32[]{:S(2)}) collective-permute-start(f32[40,128]{1,0:T(8,128)S(1)} %add_add_fusion.1), channel_id=1, source_target_pairs={{0,16},{1,17},{2,18},{3,19},{4,20},{5,21},{6,22},{7,23},{8,24},{9,... | collective-permute-start | bytes 61448 | tf_op jit(solution)/shard_map/ppermute | solution.py:48
  49.7 4.9 %collective-permute-start.14 = (f32[160,128]{1,0:T(8,128)S(1)}, f32[160,128]{1,0:T(8,128)S(1)}, u32[]{:S(2)}, u32[]{:S(2)}) collective-permute-start(f32[160,128]{1,0:T(8,128)S(1)} %get-tuple-element.23), channel_id=1, source_target_pairs={{0,128},{1,129},{2,130},{3,131},{4,132},{5,133},{6,134},{7,135},{8... | collective-permute-start | bytes 245768 | tf_op jit(solution)/shard_map/ppermute | solution.py:48
  51.5 7.8 %collective-permute-start.16 = (f32[160,128]{1,0:T(8,128)S(1)}, f32[160,128]{1,0:T(8,128)S(1)}, u32[]{:S(2)}, u32[]{:S(2)}) collective-permute-start(f32[160,128]{1,0:T(8,128)S(1)} %get-tuple-element.23), channel_id=1, source_target_pairs={{0,224},{1,225},{2,226},{3,227},{4,228},{5,229},{6,230},{7,231},{8... | collective-permute-start | bytes 245768 | tf_op jit(solution)/shard_map/ppermute | solution.py:48
  54.2 5.1 %collective-permute-start.15 = (f32[160,128]{1,0:T(8,128)S(1)}, f32[160,128]{1,0:T(8,128)S(1)}, u32[]{:S(2)}, u32[]{:S(2)}) collective-permute-start(f32[160,128]{1,0:T(8,128)S(1)} %get-tuple-element.23), channel_id=1, source_target_pairs={{0,96},{1,97},{2,98},{3,99},{4,100},{5,101},{6,102},{7,103},{8,104... | collective-permute-start | bytes 245768 | tf_op jit(solution)/shard_map/ppermute | solution.py:48
  59.3 1.9 %collective-permute-start.17 = (f32[640,128]{1,0:T(8,128)S(1)}, f32[640,128]{1,0:T(8,128)S(1)}, u32[]{:S(2)}, u32[]{:S(2)}) collective-permute-start(f32[640,128]{1,0:T(8,128)S(1)} %get-tuple-element.12), channel_id=1, source_target_pairs={{0,32},{1,33},{2,34},{3,35},{4,36},{5,37},{6,38},{7,39},{8,40},{9,... | collective-permute-start | bytes 983048 | tf_op jit(solution)/shard_map/ppermute | solution.py:48

commit v7 on v6

--- a/solution.py
+++ b/solution.py
@@ -32,20 +32,25 @@
     return half() if axis == "c" else lax.axis_index(axis)
 
 
-def shifted(v, axis, k):
+def moved(v, axis, to_place):
     sizes = [lax.axis_size(a) for a in AXES]
     along, core = AXES.index(axis), AXES.index("c")
     pairs = []
     for source, at in enumerate(itertools.product(*map(range, sizes))):
         to = list(at)
-        to[along] = (to[along] + k) % sizes[along]
+        step = to_place(at[along]) - at[along]
+        to[along] = (at[along] + step) % sizes[along]
         if along != core:
-            to[core] = (to[core] + k) % 2
+            to[core] = (at[core] + step) % 2
         target = 0
         for size, i in zip(sizes, to):
             target = target * size + i
         pairs.append((source, target))
     return lax.ppermute(v, AXES, pairs)
+
+
+def shifted(v, axis, k):
+    return moved(v, axis, lambda i: i + k)
 
 
 def steps(n):
@@ -68,9 +73,10 @@
 
 
 def summed(v, axis):
-    pairs = lax.axis_size(axis) // 2
-    v = v + shifted(v, axis, pairs)
-    arrived = [shifted(v, axis, k if 2 * k <= pairs else k - pairs) for k in steps(pairs)]
+    if lax.axis_size(axis) != 8:
+        return lax.psum(v, axis)
+    v = v + moved(v, axis, lambda i: i ^ 1)
+    arrived = [moved(v, axis, lambda i, k=k: i + k if i % 2 else i - k) for k in (3, 2, 1)]
     for part in arrived:
         v = v + part
     return v

time: 72.8 us -> 71.2 us (0.978)
  starting transfers between devices: 30.1 us -> 27.6 us
  waiting for transfers between devices: 24.1 us -> 25 us
    ppermute x18, starting transfers between devices: 30.1 us -> 27.6 us  [moved(): return lax.ppermute(v, AXES, pairs)]
    ppermute x18, waiting for transfers between devices: 24.1 us -> 25 us  [moved(): return lax.ppermute(v, AXES, pairs)]
  transfers between devices with their start and end apart: 18 -> 18, of which waited for: 13 -> 12; matrix products, arithmetic and copies ran while one was open for 0% -> 0% of each run, Pallas kernels for 3% -> 3%
where the time goes in v7:
time: 71.2 us; the launch traced here: 71.1 us
  starting transfers between devices  27.6 us (39%)
  waiting for transfers between devices  25 us (35%)
  Pallas kernels  17.8 us (25%)
    ppermute x18, starting transfers between devices, moved(): return lax.ppermute(v, AXES, pairs)  27.6 us
    ppermute x18, waiting for transfers between devices, moved(): return lax.ppermute(v, AXES, pairs)  25 us
    pallas_call x1, Pallas kernels, corrected(): pl.pallas_call(functools.partial(finish_kernel, pixel_total, chunk, sizes...  11.3 us
    pallas_call x1, Pallas kernels, upper_gram(): pl.pallas_call(gram_kernel, out_shape=jax.ShapeDtypeStruct((lines, TILE),...  4.52 us
    pallas_call x1, Pallas kernels, start_rows(): pl.pallas_call(start_kernel, out_shape=jax.ShapeDtypeStruct((k, m), F32),...  2.02 us
  transfers between devices with their start and end apart: 18, of which 12 were waited for; matrix products, arithmetic and copies ran while one was open for 0% of the time, Pallas kernels for 3%

profile of v7, /device:TPU:1, one launch (start us, length us, event | category | flops | bytes accessed | tf_op | source)
XLA Modules:
  0.0 71.1 jit_solution(7329813117212294754)
XLA Ops:
  0.0 0.0 copy-start
  0.0 4.5 %gram.1 = f32[1280,128]{1,0:T(8,128)S(1)} custom-call(f32[512,2048]{1,0:T(8,128)} %x_hbm.3), custom_call_target="tpu_custom_call" | custom-call | flops 3221225472 | bytes 4194304 | tf_op jit(solution)/shard_map/gram/pallas_call | solution.py:155
  4.6 3.3 %collective-permute-start = (f32[640,128]{1,0:T(8,128)S(1)}, f32[640,128]{1,0:T(8,128)S(1)}, u32[]{:S(2)}, u32[]{:S(2)}) collective-permute-start(f32[640,128]{1,0:T(8,128)S(1)} %constant_dynamic-slice_fusion.6), channel_id=1, source_target_pairs={{0,32},{1,33},{2,34},{3,35},{4,36},{5,37},{6,38},{7,39},{8,40},{9,... | collective-permute-start | bytes 983048 | tf_op jit(solution)/shard_map/ppermute | solution.py:49
  7.9 1.3 %collective-permute-done = f32[640,128]{1,0:T(8,128)S(1)} collective-permute-done((f32[640,128]{1,0:T(8,128)S(1)}, f32[640,128]{1,0:T(8,128)S(1)}, u32[]{:S(2)}, u32[]{:S(2)}) %collective-permute-start) | collective-permute-done | bytes 327712 | tf_op jit(solution)/shard_map/ppermute | solution.py:49
  9.2 1.3 %collective-permute-start.1 = (f32[160,128]{1,0:T(8,128)S(1)}, f32[160,128]{1,0:T(8,128)S(1)}, u32[]{:S(2)}, u32[]{:S(2)}) collective-permute-start(f32[160,128]{1,0:T(8,128)S(1)} %get-tuple-element.9), channel_id=1, source_target_pairs={{0,128},{1,129},{2,130},{3,131},{4,132},{5,133},{6,134},{7,135},{8... | collective-permute-start | bytes 245768 | tf_op jit(solution)/shard_map/ppermute | solution.py:49
  10.5 1.3 %collective-permute-start.3 = (f32[160,128]{1,0:T(8,128)S(1)}, f32[160,128]{1,0:T(8,128)S(1)}, u32[]{:S(2)}, u32[]{:S(2)}) collective-permute-start(f32[160,128]{1,0:T(8,128)S(1)} %get-tuple-element.10), channel_id=1, source_target_pairs={{0,224},{1,225},{2,226},{3,227},{4,228},{5,229},{6,230},{7,231},{8... | collective-permute-start | bytes 245768 | tf_op jit(solution)/shard_map/ppermute | solution.py:49
  11.8 0.4 collective-permute-start.2
  12.2 2.2 %collective-permute-done.1 = f32[160,128]{1,0:T(8,128)S(1)} collective-permute-done((f32[160,128]{1,0:T(8,128)S(1)}, f32[160,128]{1,0:T(8,128)S(1)}, u32[]{:S(2)}, u32[]{:S(2)}) %collective-permute-start.1) | collective-permute-done | bytes 81952 | tf_op jit(solution)/shard_map/ppermute | solution.py:49
  14.5 1.2 %collective-permute-done.3 = f32[160,128]{1,0:T(8,128)S(1)} collective-permute-done((f32[160,128]{1,0:T(8,128)S(1)}, f32[160,128]{1,0:T(8,128)S(1)}, u32[]{:S(2)}, u32[]{:S(2)}) %collective-permute-start.3) | collective-permute-done | bytes 81952 | tf_op jit(solution)/shard_map/ppermute | solution.py:49
  15.7 1.3 %collective-permute-done.2 = f32[160,128]{1,0:T(8,128)S(1)} collective-permute-done((f32[160,128]{1,0:T(8,128)S(1)}, f32[160,128]{1,0:T(8,128)S(1)}, u32[]{:S(2)}, u32[]{:S(2)}) %collective-permute-start.2) | collective-permute-done | bytes 81952 | tf_op jit(solution)/shard_map/ppermute | solution.py:49
  17.0 2.8 %collective-permute-start.4 = (f32[40,128]{1,0:T(8,128)S(1)}, f32[40,128]{1,0:T(8,128)S(1)}, u32[]{:S(2)}, u32[]{:S(2)}) collective-permute-start(f32[40,128]{1,0:T(8,128)S(1)} %get-tuple-element.18), channel_id=1, source_target_pairs={{0,16},{1,17},{2,18},{3,19},{4,20},{5,21},{6,22},{7,23},{8,24},{9,... | collective-permute-start | bytes 61448 | tf_op jit(solution)/shard_map/ppermute | solution.py:49
  19.8 0.9 %collective-permute-start.6 = (f32[40,128]{1,0:T(8,128)S(1)}, f32[40,128]{1,0:T(8,128)S(1)}, u32[]{:S(2)}, u32[]{:S(2)}) collective-permute-start(f32[40,128]{1,0:T(8,128)S(1)} %get-tuple-element.19), channel_id=1, source_target_pairs={{0,56},{1,57},{2,58},{3,59},{4,60},{5,61},{6,62},{7,63},{8,32},{9,... | collective-permute-start | bytes 61448 | tf_op jit(solution)/shard_map/ppermute | solution.py:49
  20.7 0.8 %collective-permute-start.5 = (f32[40,128]{1,0:T(8,128)S(1)}, f32[40,128]{1,0:T(8,128)S(1)}, u32[]{:S(2)}, u32[]{:S(2)}) collective-permute-start(f32[40,128]{1,0:T(8,128)S(1)} %get-tuple-element.20), channel_id=1, source_target_pairs={{0,40},{1,41},{2,42},{3,43},{4,44},{5,45},{6,46},{7,47},{8,48},{9,... | collective-permute-start | bytes 61448 | tf_op jit(solution)/shard_map/ppermute | solution.py:49
  21.5 0.0 collective-permute-done.4
  21.6 1.5 %collective-permute-done.6 = f32[40,128]{1,0:T(8,128)S(1)} collective-permute-done((f32[40,128]{1,0:T(8,128)S(1)}, f32[40,128]{1,0:T(8,128)S(1)}, u32[]{:S(2)}, u32[]{:S(2)}) %collective-permute-start.6) | collective-permute-done | bytes 20512 | tf_op jit(solution)/shard_map/ppermute | solution.py:49
  23.0 2.1 %collective-permute-done.5 = f32[40,128]{1,0:T(8,128)S(1)} collective-permute-done((f32[40,128]{1,0:T(8,128)S(1)}, f32[40,128]{1,0:T(8,128)S(1)}, u32[]{:S(2)}, u32[]{:S(2)}) %collective-permute-start.5) | collective-permute-done | bytes 20512 | tf_op jit(solution)/shard_map/ppermute | solution.py:49
  25.2 1.9 %collective-permute-start.7 = (f32[40,128]{1,0:T(8,128)S(1)}, f32[40,128]{1,0:T(8,128)S(1)}, u32[]{:S(2)}, u32[]{:S(2)}) collective-permute-start(f32[40,128]{1,0:T(8,128)S(1)} %add_add_fusion.2), channel_id=1, source_target_pairs={{0,33},{1,32},{2,35},{3,34},{4,37},{5,36},{6,39},{7,38},{8,41},{9,... | collective-permute-start | bytes 61448 | tf_op jit(solution)/shard_map/ppermute | solution.py:49
  27.1 1.5 %collective-permute-done.7 = f32[40,128]{1,0:T(8,128)S(1)} collective-permute-done((f32[40,128]{1,0:T(8,128)S(1)}, f32[40,128]{1,0:T(8,128)S(1)}, u32[]{:S(2)}, u32[]{:S(2)}) %collective-permute-start.7) | collective-permute-done | bytes 20512 | tf_op jit(solution)/shard_map/ppermute | solution.py:49
  28.6 5.7 %collective-permute-start.10 = (f32[40,128]{1,0:T(8,128)S(1)}, f32[40,128]{1,0:T(8,128)S(1)}, u32[]{:S(2)}, u32[]{:S(2)}) collective-permute-start(f32[40,128]{1,0:T(8,128)S(1)} %add.129), channel_id=1, source_target_pairs={{0,39},{1,34},{2,33},{3,36},{4,35},{5,38},{6,37},{7,32},{8,47},{9,... | collective-permute-start | bytes 61448 | tf_op jit(solution)/shard_map/ppermute | solution.py:49
  34.2 1.2 %collective-permute-start.9 = (f32[40,128]{1,0:T(8,128)S(1)}, f32[40,128]{1,0:T(8,128)S(1)}, u32[]{:S(2)}, u32[]{:S(2)}) collective-permute-start(f32[40,128]{1,0:T(8,128)S(1)} %add.129), channel_id=1, source_target_pairs={{0,6},{1,3},{2,0},{3,5},{4,2},{5,7},{6,4},{7,1},{8,14},{9,11},{10,... | collective-permute-start | bytes 61448 | tf_op jit(solution)/shard_map/ppermute | solution.py:49
  35.4 1.3 %collective-permute-start.8 = (f32[40,128]{1,0:T(8,128)S(1)}, f32[40,128]{1,0:T(8,128)S(1)}, u32[]{:S(2)}, u32[]{:S(2)}) collective-permute-start(f32[40,128]{1,0:T(8,128)S(1)} %add.129), channel_id=1, source_target_pairs={{0,37},{1,36},{2,39},{3,38},{4,33},{5,32},{6,35},{7,34},{8,45},{9,... | collective-permute-start | bytes 61448 | tf_op jit(solution)/shard_map/ppermute | solution.py:49
  36.7 0.0 copy-done
  36.7 2.0 %start_rows.1.v_ref = f32[64,512]{1,0:T(8,128)S(1)} custom-call(f32[64,512]{1,0:T(8,128)S(1)} %bitcast.4), custom_call_target="tpu_custom_call" | custom-call | flops 8000000000 | bytes 262144 | tf_op jit(solution)/shard_map/start_rows/pallas_call | solution.py:224
  38.7 0.0 collective-permute-done.10
  38.7 0.0 collective-permute-done.9
  38.7 3.3 %collective-permute-done.8 = f32[40,128]{1,0:T(8,128)S(1)} collective-permute-done((f32[40,128]{1,0:T(8,128)S(1)}, f32[40,128]{1,0:T(8,128)S(1)}, u32[]{:S(2)}, u32[]{:S(2)}) %collective-permute-start.8) | collective-permute-done | bytes 20512 | tf_op jit(solution)/shard_map/ppermute | solution.py:49
  42.1 0.7 %collective-permute-start.13 = (f32[40,128]{1,0:T(8,128)S(1)}, f32[40,128]{1,0:T(8,128)S(1)}, u32[]{:S(2)}, u32[]{:S(2)}) collective-permute-start(f32[40,128]{1,0:T(8,128)S(1)} %add_add_fusion.1), channel_id=1, source_target_pairs={{0,56},{1,57},{2,58},{3,59},{4,60},{5,61},{6,62},{7,63},{8,32},{9,... | collective-permute-start | bytes 61448 | tf_op jit(solution)/shard_map/ppermute | solution.py:49
  42.8 1.3 %collective-permute-start.12 = (f32[40,128]{1,0:T(8,128)S(1)}, f32[40,128]{1,0:T(8,128)S(1)}, u32[]{:S(2)}, u32[]{:S(2)}) collective-permute-start(f32[40,128]{1,0:T(8,128)S(1)} %add_add_fusion.1), channel_id=1, source_target_pairs={{0,40},{1,41},{2,42},{3,43},{4,44},{5,45},{6,46},{7,47},{8,48},{9,... | collective-permute-start | bytes 61448 | tf_op jit(solution)/shard_map/ppermute | solution.py:49
  44.1 0.0 collective-permute-start.11
  44.1 4.1 %collective-permute-done.11 = f32[40,128]{1,0:T(8,128)S(1)} collective-permute-done((f32[40,128]{1,0:T(8,128)S(1)}, f32[40,128]{1,0:T(8,128)S(1)}, u32[]{:S(2)}, u32[]{:S(2)}) %collective-permute-start.11) | collective-permute-done | bytes 20512 | tf_op jit(solution)/shard_map/ppermute | solution.py:49
  48.2 0.0 collective-permute-done.12
  48.2 0.0 collective-permute-done.13
  48.3 0.9 %collective-permute-start.14 = (f32[160,128]{1,0:T(8,128)S(1)}, f32[160,128]{1,0:T(8,128)S(1)}, u32[]{:S(2)}, u32[]{:S(2)}) collective-permute-start(f32[160,128]{1,0:T(8,128)S(1)} %get-tuple-element.23), channel_id=1, source_target_pairs={{0,128},{1,129},{2,130},{3,131},{4,132},{5,133},{6,134},{7,135},{8... | collective-permute-start | bytes 245768 | tf_op jit(solution)/shard_map/ppermute | solution.py:49
  49.2 3.6 %collective-permute-start.16 = (f32[160,128]{1,0:T(8,128)S(1)}, f32[160,128]{1,0:T(8,128)S(1)}, u32[]{:S(2)}, u32[]{:S(2)}) collective-permute-start(f32[160,128]{1,0:T(8,128)S(1)} %get-tuple-element.23), channel_id=1, source_target_pairs={{0,224},{1,225},{2,226},{3,227},{4,228},{5,229},{6,230},{7,231},{8... | collective-permute-start | bytes 245768 | tf_op jit(solution)/shard_map/ppermute | solution.py:49
  52.7 0.0 collective-permute-start.15
  52.8 0.4 collective-permute-done.14
  53.2 4.7 %collective-permute-done.15 = f32[160,128]{1,0:T(8,128)S(1)} collective-permute-done((f32[160,128]{1,0:T(8,128)S(1)}, f32[160,128]{1,0:T(8,128)S(1)}, u32[]{:S(2)}, u32[]{:S(2)}) %collective-permute-start.15) | collective-permute-done | bytes 81952 | tf_op jit(solution)/shard_map/ppermute | solution.py:49
  57.8 0.0 collective-permute-done.16
  57.9 0.1 collective-permute-start.17
  58.0 0.1 pad_add_fusion.me_ref
  58.1 1.5 %collective-permute-done.17 = f32[640,128]{1,0:T(8,128)S(1)} collective-permute-done((f32[640,128]{1,0:T(8,128)S(1)}, f32[640,128]{1,0:T(8,128)S(1)}, u32[]{:S(2)}, u32[]{:S(2)}) %collective-permute-start.17) | collective-permute-done | bytes 327712 | tf_op jit(solution)/shard_map/ppermute | solution.py:49
  59.6 11.3 %finish.1 = f32[512,2048]{1,0:T(8,128)} custom-call(s32[3]{0:T(128)S(1)} %pad_add_fusion.me_ref, f32[1280,128]{1,0:T(8,128)S(1)} %constant_dynamic-update-slice_fusion.11.lines_ref, f32[64,512]{1,0:T(8,128)S(1)} %start_rows.1.v_ref, f32[512,2048]{1,0:T(8,128)} %x_hbm.3), custom_call_target="tpu_custom_call" | custom-call | flops 805306368 | bytes 8388608 | tf_op jit(solution)/shard_map/finish/pallas_call | solution.py:319
  (16 shorter events, 0.2 us)
Async XLA Ops:
  0.0 36.7 %copy-start = (f32[512,64]{0,1:T(8,128)S(1)}, f32[512,64]{0,1:T(8,128)}, u32[]{:S(2)}) copy-start(f32[512,64]{0,1:T(8,128)} %param.3) | copy-start | bytes 393220
  4.6 4.6 %collective-permute-start = (f32[640,128]{1,0:T(8,128)S(1)}, f32[640,128]{1,0:T(8,128)S(1)}, u32[]{:S(2)}, u32[]{:S(2)}) collective-permute-start(f32[640,128]{1,0:T(8,128)S(1)} %constant_dynamic-slice_fusion.6), channel_id=1, source_target_pairs={{0,32},{1,33},{2,34},{3,35},{4,36},{5,37},{6,38},{7,39},{8,40},{9,... | collective-permute-start | bytes 983048 | tf_op jit(solution)/shard_map/ppermute | solution.py:49
  9.2 5.2 %collective-permute-start.1 = (f32[160,128]{1,0:T(8,128)S(1)}, f32[160,128]{1,0:T(8,128)S(1)}, u32[]{:S(2)}, u32[]{:S(2)}) collective-permute-start(f32[160,128]{1,0:T(8,128)S(1)} %get-tuple-element.9), channel_id=1, source_target_pairs={{0,128},{1,129},{2,130},{3,131},{4,132},{5,133},{6,134},{7,135},{8... | collective-permute-start | bytes 245768 | tf_op jit(solution)/shard_map/ppermute | solution.py:49
  10.5 5.2 %collective-permute-start.3 = (f32[160,128]{1,0:T(8,128)S(1)}, f32[160,128]{1,0:T(8,128)S(1)}, u32[]{:S(2)}, u32[]{:S(2)}) collective-permute-start(f32[160,128]{1,0:T(8,128)S(1)} %get-tuple-element.10), channel_id=1, source_target_pairs={{0,224},{1,225},{2,226},{3,227},{4,228},{5,229},{6,230},{7,231},{8... | collective-permute-start | bytes 245768 | tf_op jit(solution)/shard_map/ppermute | solution.py:49
  11.8 5.1 %collective-permute-start.2 = (f32[160,128]{1,0:T(8,128)S(1)}, f32[160,128]{1,0:T(8,128)S(1)}, u32[]{:S(2)}, u32[]{:S(2)}) collective-permute-start(f32[160,128]{1,0:T(8,128)S(1)} %get-tuple-element.11), channel_id=1, source_target_pairs={{0,96},{1,97},{2,98},{3,99},{4,100},{5,101},{6,102},{7,103},{8,104... | collective-permute-start | bytes 245768 | tf_op jit(solution)/shard_map/ppermute | solution.py:49
  17.0 4.6 %collective-permute-start.4 = (f32[40,128]{1,0:T(8,128)S(1)}, f32[40,128]{1,0:T(8,128)S(1)}, u32[]{:S(2)}, u32[]{:S(2)}) collective-permute-start(f32[40,128]{1,0:T(8,128)S(1)} %get-tuple-element.18), channel_id=1, source_target_pairs={{0,16},{1,17},{2,18},{3,19},{4,20},{5,21},{6,22},{7,23},{8,24},{9,... | collective-permute-start | bytes 61448 | tf_op jit(solution)/shard_map/ppermute | solution.py:49
  19.8 3.2 %collective-permute-start.6 = (f32[40,128]{1,0:T(8,128)S(1)}, f32[40,128]{1,0:T(8,128)S(1)}, u32[]{:S(2)}, u32[]{:S(2)}) collective-permute-start(f32[40,128]{1,0:T(8,128)S(1)} %get-tuple-element.19), channel_id=1, source_target_pairs={{0,56},{1,57},{2,58},{3,59},{4,60},{5,61},{6,62},{7,63},{8,32},{9,... | collective-permute-start | bytes 61448 | tf_op jit(solution)/shard_map/ppermute | solution.py:49
  20.7 4.4 %collective-permute-start.5 = (f32[40,128]{1,0:T(8,128)S(1)}, f32[40,128]{1,0:T(8,128)S(1)}, u32[]{:S(2)}, u32[]{:S(2)}) collective-permute-start(f32[40,128]{1,0:T(8,128)S(1)} %get-tuple-element.20), channel_id=1, source_target_pairs={{0,40},{1,41},{2,42},{3,43},{4,44},{5,45},{6,46},{7,47},{8,48},{9,... | collective-permute-start | bytes 61448 | tf_op jit(solution)/shard_map/ppermute | solution.py:49
  25.2 3.4 %collective-permute-start.7 = (f32[40,128]{1,0:T(8,128)S(1)}, f32[40,128]{1,0:T(8,128)S(1)}, u32[]{:S(2)}, u32[]{:S(2)}) collective-permute-start(f32[40,128]{1,0:T(8,128)S(1)} %add_add_fusion.2), channel_id=1, source_target_pairs={{0,33},{1,32},{2,35},{3,34},{4,37},{5,36},{6,39},{7,38},{8,41},{9,... | collective-permute-start | bytes 61448 | tf_op jit(solution)/shard_map/ppermute | solution.py:49
  28.6 10.2 %collective-permute-start.10 = (f32[40,128]{1,0:T(8,128)S(1)}, f32[40,128]{1,0:T(8,128)S(1)}, u32[]{:S(2)}, u32[]{:S(2)}) collective-permute-start(f32[40,128]{1,0:T(8,128)S(1)} %add.129), channel_id=1, source_target_pairs={{0,39},{1,34},{2,33},{3,36},{4,35},{5,38},{6,37},{7,32},{8,47},{9,... | collective-permute-start | bytes 61448 | tf_op jit(solution)/shard_map/ppermute | solution.py:49
  34.2 4.5 %collective-permute-start.9 = (f32[40,128]{1,0:T(8,128)S(1)}, f32[40,128]{1,0:T(8,128)S(1)}, u32[]{:S(2)}, u32[]{:S(2)}) collective-permute-start(f32[40,128]{1,0:T(8,128)S(1)} %add.129), channel_id=1, source_target_pairs={{0,6},{1,3},{2,0},{3,5},{4,2},{5,7},{6,4},{7,1},{8,14},{9,11},{10,... | collective-permute-start | bytes 61448 | tf_op jit(solution)/shard_map/ppermute | solution.py:49
  35.4 6.6 %collective-permute-start.8 = (f32[40,128]{1,0:T(8,128)S(1)}, f32[40,128]{1,0:T(8,128)S(1)}, u32[]{:S(2)}, u32[]{:S(2)}) collective-permute-start(f32[40,128]{1,0:T(8,128)S(1)} %add.129), channel_id=1, source_target_pairs={{0,37},{1,36},{2,39},{3,38},{4,33},{5,32},{6,35},{7,34},{8,45},{9,... | collective-permute-start | bytes 61448 | tf_op jit(solution)/shard_map/ppermute | solution.py:49
  42.1 6.2 %collective-permute-start.13 = (f32[40,128]{1,0:T(8,128)S(1)}, f32[40,128]{1,0:T(8,128)S(1)}, u32[]{:S(2)}, u32[]{:S(2)}) collective-permute-start(f32[40,128]{1,0:T(8,128)S(1)} %add_add_fusion.1), channel_id=1, source_target_pairs={{0,56},{1,57},{2,58},{3,59},{4,60},{5,61},{6,62},{7,63},{8,32},{9,... | collective-permute-start | bytes 61448 | tf_op jit(solution)/shard_map/ppermute | solution.py:49
  42.8 5.4 %collective-permute-start.12 = (f32[40,128]{1,0:T(8,128)S(1)}, f32[40,128]{1,0:T(8,128)S(1)}, u32[]{:S(2)}, u32[]{:S(2)}) collective-permute-start(f32[40,128]{1,0:T(8,128)S(1)} %add_add_fusion.1), channel_id=1, source_target_pairs={{0,40},{1,41},{2,42},{3,43},{4,44},{5,45},{6,46},{7,47},{8,48},{9,... | collective-permute-start | bytes 61448 | tf_op jit(solution)/shard_map/ppermute | solution.py:49
  44.1 4.1 %collective-permute-start.11 = (f32[40,128]{1,0:T(8,128)S(1)}, f32[40,128]{1,0:T(8,128)S(1)}, u32[]{:S(2)}, u32[]{:S(2)}) collective-permute-start(f32[40,128]{1,0:T(8,128)S(1)} %add_add_fusion.1), channel_id=1, source_target_pairs={{0,16},{1,17},{2,18},{3,19},{4,20},{5,21},{6,22},{7,23},{8,24},{9,... | collective-permute-start | bytes 61448 | tf_op jit(solution)/shard_map/ppermute | solution.py:49
  48.3 4.9 %collective-permute-start.14 = (f32[160,128]{1,0:T(8,128)S(1)}, f32[160,128]{1,0:T(8,128)S(1)}, u32[]{:S(2)}, u32[]{:S(2)}) collective-permute-start(f32[160,128]{1,0:T(8,128)S(1)} %get-tuple-element.23), channel_id=1, source_target_pairs={{0,128},{1,129},{2,130},{3,131},{4,132},{5,133},{6,134},{7,135},{8... | collective-permute-start | bytes 245768 | tf_op jit(solution)/shard_map/ppermute | solution.py:49
  49.2 8.7 %collective-permute-start.16 = (f32[160,128]{1,0:T(8,128)S(1)}, f32[160,128]{1,0:T(8,128)S(1)}, u32[]{:S(2)}, u32[]{:S(2)}) collective-permute-start(f32[160,128]{1,0:T(8,128)S(1)} %get-tuple-element.23), channel_id=1, source_target_pairs={{0,224},{1,225},{2,226},{3,227},{4,228},{5,229},{6,230},{7,231},{8... | collective-permute-start | bytes 245768 | tf_op jit(solution)/shard_map/ppermute | solution.py:49
  52.7 5.1 %collective-permute-start.15 = (f32[160,128]{1,0:T(8,128)S(1)}, f32[160,128]{1,0:T(8,128)S(1)}, u32[]{:S(2)}, u32[]{:S(2)}) collective-permute-start(f32[160,128]{1,0:T(8,128)S(1)} %get-tuple-element.23), channel_id=1, source_target_pairs={{0,96},{1,97},{2,98},{3,99},{4,100},{5,101},{6,102},{7,103},{8,104... | collective-permute-start | bytes 245768 | tf_op jit(solution)/shard_map/ppermute | solution.py:49
  57.9 1.7 %collective-permute-start.17 = (f32[640,128]{1,0:T(8,128)S(1)}, f32[640,128]{1,0:T(8,128)S(1)}, u32[]{:S(2)}, u32[]{:S(2)}) collective-permute-start(f32[640,128]{1,0:T(8,128)S(1)} %get-tuple-element.12), channel_id=1, source_target_pairs={{0,32},{1,33},{2,34},{3,35},{4,36},{5,37},{6,38},{7,39},{8,40},{9,... | collective-permute-start | bytes 983048 | tf_op jit(solution)/shard_map/ppermute | solution.py:49

commit v8 on v7

--- a/solution.py
+++ b/solution.py
@@ -57,6 +57,11 @@
     return sorted(range(1, n), key=lambda k: -min(k, n - k))
 
 
+def slots_of(axis):
+    ways = steps(lax.axis_size(axis))
+    return (0, *(ways[::-1] if axis == "x" else ways))
+
+
 def share_of_sum(v, axis):
     n, me = lax.axis_size(axis), place_on(axis)
     rows = v.shape[0] // n
@@ -69,14 +74,14 @@
 
 
 def joined(v, axis):
-    return jnp.concatenate([v] + [shifted(v, axis, k) for k in steps(lax.axis_size(axis))], axis=0)
+    return jnp.concatenate([v] + [shifted(v, axis, k) for k in slots_of(axis)[1:]], axis=0)
 
 
 def summed(v, axis):
     if lax.axis_size(axis) != 8:
         return lax.psum(v, axis)
     v = v + moved(v, axis, lambda i: i ^ 1)
-    arrived = [moved(v, axis, lambda i, k=k: i + k if i % 2 else i - k) for k in (3, 2, 1)]
+    arrived = [moved(v, axis, lambda i, k=k: i + k if i % 2 else i - k) for k in (1, 2, 3)]
     for part in arrived:
         v = v + part
     return v
@@ -241,15 +246,16 @@
     )
 
 
-def finish_kernel(pixel_total, chunk, sizes, me_ref, lines_ref, v_ref, x_hbm, out_hbm, x, out, ordered, g0, g1, g2, x0_ref, x1_ref, x_sem, out_sem):
+def finish_kernel(pixel_total, chunk, orders, me_ref, lines_ref, v_ref, x_hbm, out_hbm, x, out, ordered, g0, g1, g2, x0_ref, x1_ref, x_sem, out_sem):
     m, n = x_hbm.shape
     k = v_ref.shape[0]
     tiles = m // TILE
     load = pltpu.make_async_copy(x_hbm, x, x_sem)
     load.start()
+    sizes = [len(order) for order in orders]
     slots = math.prod(sizes)
     rows = lines_ref.shape[0] // slots
-    for slot, back in enumerate(itertools.product(*([0, *steps(size)] for size in sizes))):
+    for slot, back in enumerate(itertools.product(*orders)):
         place = 0
         for axis, (size, hops) in enumerate(zip(sizes, back)):
             place = place * size + lax.rem(me_ref[axis] + (size - hops), size)
@@ -313,11 +319,11 @@
         pltpu.make_async_copy(out.at[:, here], out_hbm.at[:, here], out_sem.at[c]).wait()
 
 
-def corrected(lines, me, sizes, v, x, pixel_total, chunk=512):
+def corrected(lines, me, orders, v, x, pixel_total, chunk=512):
     m, n = x.shape
     k = v.shape[0]
     return pl.pallas_call(
-        functools.partial(finish_kernel, pixel_total, chunk, sizes),
+        functools.partial(finish_kernel, pixel_total, chunk, orders),
         out_shape=jax.ShapeDtypeStruct((m, n), F32),
         in_specs=[
             pl.BlockSpec(memory_space=pltpu.SMEM),
@@ -348,8 +354,8 @@
     pixel_total = phase_stack.shape[1] * lax.axis_size(AXES)
     lines, v = sum_everywhere(upper_gram(phase_stack), start_rows(start_basis.T))
     me = jnp.stack([place_on(axis) for axis in SHARED]).astype(jnp.int32)
-    sizes = tuple(lax.axis_size(axis) for axis in SHARED)
-    return corrected(lines, me, sizes, v, phase_stack, pixel_total)
+    orders = tuple(slots_of(axis) for axis in SHARED)
+    return corrected(lines, me, orders, v, phase_stack, pixel_total)
 
 
 def solution(mesh):

time: 71.2 us -> 67.2 us (0.944)
  waiting for transfers between devices: 25 us -> 19.1 us
  starting transfers between devices: 27.6 us -> 29.6 us
    ppermute x18, waiting for transfers between devices: 25 us -> 19.1 us  [moved(): return lax.ppermute(v, AXES, pairs)]
    ppermute x18, starting transfers between devices: 27.6 us -> 29.6 us  [moved(): return lax.ppermute(v, AXES, pairs)]
where the time goes in v8:
time: 67.2 us; the launch traced here: 67.1 us
  starting transfers between devices  29.6 us (44%)
  waiting for transfers between devices  19.1 us (28%)
  Pallas kernels  17.8 us (26%)
    ppermute x18, starting transfers between devices, moved(): return lax.ppermute(v, AXES, pairs)  29.6 us
    ppermute x18, waiting for transfers between devices, moved(): return lax.ppermute(v, AXES, pairs)  19.1 us
    pallas_call x1, Pallas kernels, corrected(): pl.pallas_call(functools.partial(finish_kernel, pixel_total, chunk, order...  11.3 us
    pallas_call x1, Pallas kernels, upper_gram(): pl.pallas_call(gram_kernel, out_shape=jax.ShapeDtypeStruct((lines, TILE),...  4.52 us
    pallas_call x1, Pallas kernels, start_rows(): pl.pallas_call(start_kernel, out_shape=jax.ShapeDtypeStruct((k, m), F32),...  2.02 us
  transfers between devices with their start and end apart: 18, of which 12 were waited for; matrix products, arithmetic and copies ran while one was open for 0% of the time, Pallas kernels for 3%

profile of v8, /device:TPU:1, one launch (start us, length us, event | category | flops | bytes accessed | tf_op | source)
XLA Modules:
  0.0 67.1 jit_solution(10609738789700330394)
XLA Ops:
  0.0 0.0 copy-start
  0.0 4.5 %gram.1 = f32[1280,128]{1,0:T(8,128)S(1)} custom-call(f32[512,2048]{1,0:T(8,128)} %x_hbm.3), custom_call_target="tpu_custom_call" | custom-call | flops 3221225472 | bytes 4194304 | tf_op jit(solution)/shard_map/gram/pallas_call | solution.py:160
  4.6 3.3 %collective-permute-start = (f32[640,128]{1,0:T(8,128)S(1)}, f32[640,128]{1,0:T(8,128)S(1)}, u32[]{:S(2)}, u32[]{:S(2)}) collective-permute-start(f32[640,128]{1,0:T(8,128)S(1)} %constant_dynamic-slice_fusion.6), channel_id=1, source_target_pairs={{0,32},{1,33},{2,34},{3,35},{4,36},{5,37},{6,38},{7,39},{8,40},{9,... | collective-permute-start | bytes 983048 | tf_op jit(solution)/shard_map/ppermute | solution.py:49
  7.9 1.3 %collective-permute-done = f32[640,128]{1,0:T(8,128)S(1)} collective-permute-done((f32[640,128]{1,0:T(8,128)S(1)}, f32[640,128]{1,0:T(8,128)S(1)}, u32[]{:S(2)}, u32[]{:S(2)}) %collective-permute-start) | collective-permute-done | bytes 327712 | tf_op jit(solution)/shard_map/ppermute | solution.py:49
  9.2 1.3 %collective-permute-start.1 = (f32[160,128]{1,0:T(8,128)S(1)}, f32[160,128]{1,0:T(8,128)S(1)}, u32[]{:S(2)}, u32[]{:S(2)}) collective-permute-start(f32[160,128]{1,0:T(8,128)S(1)} %get-tuple-element.9), channel_id=1, source_target_pairs={{0,128},{1,129},{2,130},{3,131},{4,132},{5,133},{6,134},{7,135},{8... | collective-permute-start | bytes 245768 | tf_op jit(solution)/shard_map/ppermute | solution.py:49
  10.5 1.3 %collective-permute-start.3 = (f32[160,128]{1,0:T(8,128)S(1)}, f32[160,128]{1,0:T(8,128)S(1)}, u32[]{:S(2)}, u32[]{:S(2)}) collective-permute-start(f32[160,128]{1,0:T(8,128)S(1)} %get-tuple-element.10), channel_id=1, source_target_pairs={{0,224},{1,225},{2,226},{3,227},{4,228},{5,229},{6,230},{7,231},{8... | collective-permute-start | bytes 245768 | tf_op jit(solution)/shard_map/ppermute | solution.py:49
  11.8 0.4 collective-permute-start.2
  12.2 2.2 %collective-permute-done.1 = f32[160,128]{1,0:T(8,128)S(1)} collective-permute-done((f32[160,128]{1,0:T(8,128)S(1)}, f32[160,128]{1,0:T(8,128)S(1)}, u32[]{:S(2)}, u32[]{:S(2)}) %collective-permute-start.1) | collective-permute-done | bytes 81952 | tf_op jit(solution)/shard_map/ppermute | solution.py:49
  14.5 1.2 %collective-permute-done.3 = f32[160,128]{1,0:T(8,128)S(1)} collective-permute-done((f32[160,128]{1,0:T(8,128)S(1)}, f32[160,128]{1,0:T(8,128)S(1)}, u32[]{:S(2)}, u32[]{:S(2)}) %collective-permute-start.3) | collective-permute-done | bytes 81952 | tf_op jit(solution)/shard_map/ppermute | solution.py:49
  15.7 1.3 %collective-permute-done.2 = f32[160,128]{1,0:T(8,128)S(1)} collective-permute-done((f32[160,128]{1,0:T(8,128)S(1)}, f32[160,128]{1,0:T(8,128)S(1)}, u32[]{:S(2)}, u32[]{:S(2)}) %collective-permute-start.2) | collective-permute-done | bytes 81952 | tf_op jit(solution)/shard_map/ppermute | solution.py:49
  17.0 2.8 %collective-permute-start.4 = (f32[40,128]{1,0:T(8,128)S(1)}, f32[40,128]{1,0:T(8,128)S(1)}, u32[]{:S(2)}, u32[]{:S(2)}) collective-permute-start(f32[40,128]{1,0:T(8,128)S(1)} %get-tuple-element.18), channel_id=1, source_target_pairs={{0,16},{1,17},{2,18},{3,19},{4,20},{5,21},{6,22},{7,23},{8,24},{9,... | collective-permute-start | bytes 61448 | tf_op jit(solution)/shard_map/ppermute | solution.py:49
  19.8 0.9 %collective-permute-start.6 = (f32[40,128]{1,0:T(8,128)S(1)}, f32[40,128]{1,0:T(8,128)S(1)}, u32[]{:S(2)}, u32[]{:S(2)}) collective-permute-start(f32[40,128]{1,0:T(8,128)S(1)} %get-tuple-element.19), channel_id=1, source_target_pairs={{0,56},{1,57},{2,58},{3,59},{4,60},{5,61},{6,62},{7,63},{8,32},{9,... | collective-permute-start | bytes 61448 | tf_op jit(solution)/shard_map/ppermute | solution.py:49
  20.7 0.8 %collective-permute-start.5 = (f32[40,128]{1,0:T(8,128)S(1)}, f32[40,128]{1,0:T(8,128)S(1)}, u32[]{:S(2)}, u32[]{:S(2)}) collective-permute-start(f32[40,128]{1,0:T(8,128)S(1)} %get-tuple-element.20), channel_id=1, source_target_pairs={{0,40},{1,41},{2,42},{3,43},{4,44},{5,45},{6,46},{7,47},{8,48},{9,... | collective-permute-start | bytes 61448 | tf_op jit(solution)/shard_map/ppermute | solution.py:49
  21.5 0.0 collective-permute-done.4
  21.6 1.5 %collective-permute-done.6 = f32[40,128]{1,0:T(8,128)S(1)} collective-permute-done((f32[40,128]{1,0:T(8,128)S(1)}, f32[40,128]{1,0:T(8,128)S(1)}, u32[]{:S(2)}, u32[]{:S(2)}) %collective-permute-start.6) | collective-permute-done | bytes 20512 | tf_op jit(solution)/shard_map/ppermute | solution.py:49
  23.0 2.1 %collective-permute-done.5 = f32[40,128]{1,0:T(8,128)S(1)} collective-permute-done((f32[40,128]{1,0:T(8,128)S(1)}, f32[40,128]{1,0:T(8,128)S(1)}, u32[]{:S(2)}, u32[]{:S(2)}) %collective-permute-start.5) | collective-permute-done | bytes 20512 | tf_op jit(solution)/shard_map/ppermute | solution.py:49
  25.2 1.9 %collective-permute-start.7 = (f32[40,128]{1,0:T(8,128)S(1)}, f32[40,128]{1,0:T(8,128)S(1)}, u32[]{:S(2)}, u32[]{:S(2)}) collective-permute-start(f32[40,128]{1,0:T(8,128)S(1)} %add_add_fusion.2), channel_id=1, source_target_pairs={{0,33},{1,32},{2,35},{3,34},{4,37},{5,36},{6,39},{7,38},{8,41},{9,... | collective-permute-start | bytes 61448 | tf_op jit(solution)/shard_map/ppermute | solution.py:49
  27.1 1.5 %collective-permute-done.7 = f32[40,128]{1,0:T(8,128)S(1)} collective-permute-done((f32[40,128]{1,0:T(8,128)S(1)}, f32[40,128]{1,0:T(8,128)S(1)}, u32[]{:S(2)}, u32[]{:S(2)}) %collective-permute-start.7) | collective-permute-done | bytes 20512 | tf_op jit(solution)/shard_map/ppermute | solution.py:49
  28.6 6.6 %collective-permute-start.10 = (f32[40,128]{1,0:T(8,128)S(1)}, f32[40,128]{1,0:T(8,128)S(1)}, u32[]{:S(2)}, u32[]{:S(2)}) collective-permute-start(f32[40,128]{1,0:T(8,128)S(1)} %add.129), channel_id=1, source_target_pairs={{0,37},{1,36},{2,39},{3,38},{4,33},{5,32},{6,35},{7,34},{8,45},{9,... | collective-permute-start | bytes 61448 | tf_op jit(solution)/shard_map/ppermute | solution.py:49
  35.1 0.3 collective-permute-start.9
  35.4 3.2 %collective-permute-start.8 = (f32[40,128]{1,0:T(8,128)S(1)}, f32[40,128]{1,0:T(8,128)S(1)}, u32[]{:S(2)}, u32[]{:S(2)}) collective-permute-start(f32[40,128]{1,0:T(8,128)S(1)} %add.129), channel_id=1, source_target_pairs={{0,39},{1,34},{2,33},{3,36},{4,35},{5,38},{6,37},{7,32},{8,47},{9,... | collective-permute-start | bytes 61448 | tf_op jit(solution)/shard_map/ppermute | solution.py:49
  38.6 0.0 copy-done
  38.6 2.0 %start_rows.1.v_ref = f32[64,512]{1,0:T(8,128)S(1)} custom-call(f32[64,512]{1,0:T(8,128)S(1)} %bitcast.4), custom_call_target="tpu_custom_call" | custom-call | flops 8000000000 | bytes 262144 | tf_op jit(solution)/shard_map/start_rows/pallas_call | solution.py:229
  40.6 0.0 collective-permute-done.10
  40.6 0.0 collective-permute-done.9
  40.6 0.0 collective-permute-done.8
  40.7 0.1 collective-permute-start.13
  40.8 0.6 collective-permute-start.12
  41.4 2.6 %collective-permute-start.11 = (f32[40,128]{1,0:T(8,128)S(1)}, f32[40,128]{1,0:T(8,128)S(1)}, u32[]{:S(2)}, u32[]{:S(2)}) collective-permute-start(f32[40,128]{1,0:T(8,128)S(1)} %add_add_fusion.1), channel_id=1, source_target_pairs={{0,56},{1,57},{2,58},{3,59},{4,60},{5,61},{6,62},{7,63},{8,32},{9,... | collective-permute-start | bytes 61448 | tf_op jit(solution)/shard_map/ppermute | solution.py:49
  44.0 1.5 %collective-permute-done.11 = f32[40,128]{1,0:T(8,128)S(1)} collective-permute-done((f32[40,128]{1,0:T(8,128)S(1)}, f32[40,128]{1,0:T(8,128)S(1)}, u32[]{:S(2)}, u32[]{:S(2)}) %collective-permute-start.11) | collective-permute-done | bytes 20512 | tf_op jit(solution)/shard_map/ppermute | solution.py:49
  45.5 0.3 collective-permute-done.12
  45.7 0.0 collective-permute-done.13
  45.7 1.6 %collective-permute-start.14 = (f32[160,128]{1,0:T(8,128)S(1)}, f32[160,128]{1,0:T(8,128)S(1)}, u32[]{:S(2)}, u32[]{:S(2)}) collective-permute-start(f32[160,128]{1,0:T(8,128)S(1)} %get-tuple-element.23), channel_id=1, source_target_pairs={{0,128},{1,129},{2,130},{3,131},{4,132},{5,133},{6,134},{7,135},{8... | collective-permute-start | bytes 245768 | tf_op jit(solution)/shard_map/ppermute | solution.py:49
  47.3 1.3 %collective-permute-start.16 = (f32[160,128]{1,0:T(8,128)S(1)}, f32[160,128]{1,0:T(8,128)S(1)}, u32[]{:S(2)}, u32[]{:S(2)}) collective-permute-start(f32[160,128]{1,0:T(8,128)S(1)} %get-tuple-element.23), channel_id=1, source_target_pairs={{0,224},{1,225},{2,226},{3,227},{4,228},{5,229},{6,230},{7,231},{8... | collective-permute-start | bytes 245768 | tf_op jit(solution)/shard_map/ppermute | solution.py:49
  48.7 0.4 collective-permute-start.15
  49.1 2.0 %collective-permute-done.14 = f32[160,128]{1,0:T(8,128)S(1)} collective-permute-done((f32[160,128]{1,0:T(8,128)S(1)}, f32[160,128]{1,0:T(8,128)S(1)}, u32[]{:S(2)}, u32[]{:S(2)}) %collective-permute-start.14) | collective-permute-done | bytes 81952 | tf_op jit(solution)/shard_map/ppermute | solution.py:49
  51.1 2.8 %collective-permute-done.15 = f32[160,128]{1,0:T(8,128)S(1)} collective-permute-done((f32[160,128]{1,0:T(8,128)S(1)}, f32[160,128]{1,0:T(8,128)S(1)}, u32[]{:S(2)}, u32[]{:S(2)}) %collective-permute-start.15) | collective-permute-done | bytes 81952 | tf_op jit(solution)/shard_map/ppermute | solution.py:49
  53.9 0.0 collective-permute-done.16
  53.9 0.1 collective-permute-start.17
  54.0 0.1 pad_add_fusion.me_ref
  54.1 1.5 %collective-permute-done.17 = f32[640,128]{1,0:T(8,128)S(1)} collective-permute-done((f32[640,128]{1,0:T(8,128)S(1)}, f32[640,128]{1,0:T(8,128)S(1)}, u32[]{:S(2)}, u32[]{:S(2)}) %collective-permute-start.17) | collective-permute-done | bytes 327712 | tf_op jit(solution)/shard_map/ppermute | solution.py:49
  55.7 11.3 %finish.1 = f32[512,2048]{1,0:T(8,128)} custom-call(s32[3]{0:T(128)S(1)} %pad_add_fusion.me_ref, f32[1280,128]{1,0:T(8,128)S(1)} %constant_dynamic-update-slice_fusion.11.lines_ref, f32[64,512]{1,0:T(8,128)S(1)} %start_rows.1.v_ref, f32[512,2048]{1,0:T(8,128)} %x_hbm.3), custom_call_target="tpu_custom_call" | custom-call | flops 805306368 | bytes 8388608 | tf_op jit(solution)/shard_map/finish/pallas_call | solution.py:325
  (16 shorter events, 0.2 us)
Async XLA Ops:
  0.0 38.6 %copy-start = (f32[512,64]{0,1:T(8,128)S(1)}, f32[512,64]{0,1:T(8,128)}, u32[]{:S(2)}) copy-start(f32[512,64]{0,1:T(8,128)} %param.3) | copy-start | bytes 393220
  4.6 4.6 %collective-permute-start = (f32[640,128]{1,0:T(8,128)S(1)}, f32[640,128]{1,0:T(8,128)S(1)}, u32[]{:S(2)}, u32[]{:S(2)}) collective-permute-start(f32[640,128]{1,0:T(8,128)S(1)} %constant_dynamic-slice_fusion.6), channel_id=1, source_target_pairs={{0,32},{1,33},{2,34},{3,35},{4,36},{5,37},{6,38},{7,39},{8,40},{9,... | collective-permute-start | bytes 983048 | tf_op jit(solution)/shard_map/ppermute | solution.py:49
  9.2 5.2 %collective-permute-start.1 = (f32[160,128]{1,0:T(8,128)S(1)}, f32[160,128]{1,0:T(8,128)S(1)}, u32[]{:S(2)}, u32[]{:S(2)}) collective-permute-start(f32[160,128]{1,0:T(8,128)S(1)} %get-tuple-element.9), channel_id=1, source_target_pairs={{0,128},{1,129},{2,130},{3,131},{4,132},{5,133},{6,134},{7,135},{8... | collective-permute-start | bytes 245768 | tf_op jit(solution)/shard_map/ppermute | solution.py:49
  10.5 5.2 %collective-permute-start.3 = (f32[160,128]{1,0:T(8,128)S(1)}, f32[160,128]{1,0:T(8,128)S(1)}, u32[]{:S(2)}, u32[]{:S(2)}) collective-permute-start(f32[160,128]{1,0:T(8,128)S(1)} %get-tuple-element.10), channel_id=1, source_target_pairs={{0,224},{1,225},{2,226},{3,227},{4,228},{5,229},{6,230},{7,231},{8... | collective-permute-start | bytes 245768 | tf_op jit(solution)/shard_map/ppermute | solution.py:49
  11.8 5.1 %collective-permute-start.2 = (f32[160,128]{1,0:T(8,128)S(1)}, f32[160,128]{1,0:T(8,128)S(1)}, u32[]{:S(2)}, u32[]{:S(2)}) collective-permute-start(f32[160,128]{1,0:T(8,128)S(1)} %get-tuple-element.11), channel_id=1, source_target_pairs={{0,96},{1,97},{2,98},{3,99},{4,100},{5,101},{6,102},{7,103},{8,104... | collective-permute-start | bytes 245768 | tf_op jit(solution)/shard_map/ppermute | solution.py:49
  17.0 4.6 %collective-permute-start.4 = (f32[40,128]{1,0:T(8,128)S(1)}, f32[40,128]{1,0:T(8,128)S(1)}, u32[]{:S(2)}, u32[]{:S(2)}) collective-permute-start(f32[40,128]{1,0:T(8,128)S(1)} %get-tuple-element.18), channel_id=1, source_target_pairs={{0,16},{1,17},{2,18},{3,19},{4,20},{5,21},{6,22},{7,23},{8,24},{9,... | collective-permute-start | bytes 61448 | tf_op jit(solution)/shard_map/ppermute | solution.py:49
  19.8 3.2 %collective-permute-start.6 = (f32[40,128]{1,0:T(8,128)S(1)}, f32[40,128]{1,0:T(8,128)S(1)}, u32[]{:S(2)}, u32[]{:S(2)}) collective-permute-start(f32[40,128]{1,0:T(8,128)S(1)} %get-tuple-element.19), channel_id=1, source_target_pairs={{0,56},{1,57},{2,58},{3,59},{4,60},{5,61},{6,62},{7,63},{8,32},{9,... | collective-permute-start | bytes 61448 | tf_op jit(solution)/shard_map/ppermute | solution.py:49
  20.7 4.4 %collective-permute-start.5 = (f32[40,128]{1,0:T(8,128)S(1)}, f32[40,128]{1,0:T(8,128)S(1)}, u32[]{:S(2)}, u32[]{:S(2)}) collective-permute-start(f32[40,128]{1,0:T(8,128)S(1)} %get-tuple-element.20), channel_id=1, source_target_pairs={{0,40},{1,41},{2,42},{3,43},{4,44},{5,45},{6,46},{7,47},{8,48},{9,... | collective-permute-start | bytes 61448 | tf_op jit(solution)/shard_map/ppermute | solution.py:49
  25.2 3.4 %collective-permute-start.7 = (f32[40,128]{1,0:T(8,128)S(1)}, f32[40,128]{1,0:T(8,128)S(1)}, u32[]{:S(2)}, u32[]{:S(2)}) collective-permute-start(f32[40,128]{1,0:T(8,128)S(1)} %add_add_fusion.2), channel_id=1, source_target_pairs={{0,33},{1,32},{2,35},{3,34},{4,37},{5,36},{6,39},{7,38},{8,41},{9,... | collective-permute-start | bytes 61448 | tf_op jit(solution)/shard_map/ppermute | solution.py:49
  28.6 12.1 %collective-permute-start.10 = (f32[40,128]{1,0:T(8,128)S(1)}, f32[40,128]{1,0:T(8,128)S(1)}, u32[]{:S(2)}, u32[]{:S(2)}) collective-permute-start(f32[40,128]{1,0:T(8,128)S(1)} %add.129), channel_id=1, source_target_pairs={{0,37},{1,36},{2,39},{3,38},{4,33},{5,32},{6,35},{7,34},{8,45},{9,... | collective-permute-start | bytes 61448 | tf_op jit(solution)/shard_map/ppermute | solution.py:49
  35.1 5.5 %collective-permute-start.9 = (f32[40,128]{1,0:T(8,128)S(1)}, f32[40,128]{1,0:T(8,128)S(1)}, u32[]{:S(2)}, u32[]{:S(2)}) collective-permute-start(f32[40,128]{1,0:T(8,128)S(1)} %add.129), channel_id=1, source_target_pairs={{0,6},{1,3},{2,0},{3,5},{4,2},{5,7},{6,4},{7,1},{8,14},{9,11},{10,... | collective-permute-start | bytes 61448 | tf_op jit(solution)/shard_map/ppermute | solution.py:49
  35.4 5.2 %collective-permute-start.8 = (f32[40,128]{1,0:T(8,128)S(1)}, f32[40,128]{1,0:T(8,128)S(1)}, u32[]{:S(2)}, u32[]{:S(2)}) collective-permute-start(f32[40,128]{1,0:T(8,128)S(1)} %add.129), channel_id=1, source_target_pairs={{0,39},{1,34},{2,33},{3,36},{4,35},{5,38},{6,37},{7,32},{8,47},{9,... | collective-permute-start | bytes 61448 | tf_op jit(solution)/shard_map/ppermute | solution.py:49
  40.7 5.1 %collective-permute-start.13 = (f32[40,128]{1,0:T(8,128)S(1)}, f32[40,128]{1,0:T(8,128)S(1)}, u32[]{:S(2)}, u32[]{:S(2)}) collective-permute-start(f32[40,128]{1,0:T(8,128)S(1)} %add_add_fusion.1), channel_id=1, source_target_pairs={{0,16},{1,17},{2,18},{3,19},{4,20},{5,21},{6,22},{7,23},{8,24},{9,... | collective-permute-start | bytes 61448 | tf_op jit(solution)/shard_map/ppermute | solution.py:49
  40.8 4.9 %collective-permute-start.12 = (f32[40,128]{1,0:T(8,128)S(1)}, f32[40,128]{1,0:T(8,128)S(1)}, u32[]{:S(2)}, u32[]{:S(2)}) collective-permute-start(f32[40,128]{1,0:T(8,128)S(1)} %add_add_fusion.1), channel_id=1, source_target_pairs={{0,40},{1,41},{2,42},{3,43},{4,44},{5,45},{6,46},{7,47},{8,48},{9,... | collective-permute-start | bytes 61448 | tf_op jit(solution)/shard_map/ppermute | solution.py:49
  41.4 4.1 %collective-permute-start.11 = (f32[40,128]{1,0:T(8,128)S(1)}, f32[40,128]{1,0:T(8,128)S(1)}, u32[]{:S(2)}, u32[]{:S(2)}) collective-permute-start(f32[40,128]{1,0:T(8,128)S(1)} %add_add_fusion.1), channel_id=1, source_target_pairs={{0,56},{1,57},{2,58},{3,59},{4,60},{5,61},{6,62},{7,63},{8,32},{9,... | collective-permute-start | bytes 61448 | tf_op jit(solution)/shard_map/ppermute | solution.py:49
  45.7 5.3 %collective-permute-start.14 = (f32[160,128]{1,0:T(8,128)S(1)}, f32[160,128]{1,0:T(8,128)S(1)}, u32[]{:S(2)}, u32[]{:S(2)}) collective-permute-start(f32[160,128]{1,0:T(8,128)S(1)} %get-tuple-element.23), channel_id=1, source_target_pairs={{0,128},{1,129},{2,130},{3,131},{4,132},{5,133},{6,134},{7,135},{8... | collective-permute-start | bytes 245768 | tf_op jit(solution)/shard_map/ppermute | solution.py:49
  47.3 6.6 %collective-permute-start.16 = (f32[160,128]{1,0:T(8,128)S(1)}, f32[160,128]{1,0:T(8,128)S(1)}, u32[]{:S(2)}, u32[]{:S(2)}) collective-permute-start(f32[160,128]{1,0:T(8,128)S(1)} %get-tuple-element.23), channel_id=1, source_target_pairs={{0,224},{1,225},{2,226},{3,227},{4,228},{5,229},{6,230},{7,231},{8... | collective-permute-start | bytes 245768 | tf_op jit(solution)/shard_map/ppermute | solution.py:49
  48.7 5.2 %collective-permute-start.15 = (f32[160,128]{1,0:T(8,128)S(1)}, f32[160,128]{1,0:T(8,128)S(1)}, u32[]{:S(2)}, u32[]{:S(2)}) collective-permute-start(f32[160,128]{1,0:T(8,128)S(1)} %get-tuple-element.23), channel_id=1, source_target_pairs={{0,96},{1,97},{2,98},{3,99},{4,100},{5,101},{6,102},{7,103},{8,104... | collective-permute-start | bytes 245768 | tf_op jit(solution)/shard_map/ppermute | solution.py:49
  53.9 1.7 %collective-permute-start.17 = (f32[640,128]{1,0:T(8,128)S(1)}, f32[640,128]{1,0:T(8,128)S(1)}, u32[]{:S(2)}, u32[]{:S(2)}) collective-permute-start(f32[640,128]{1,0:T(8,128)S(1)} %get-tuple-element.12), channel_id=1, source_target_pairs={{0,32},{1,33},{2,34},{3,35},{4,36},{5,37},{6,38},{7,39},{8,40},{9,... | collective-permute-start | bytes 983048 | tf_op jit(solution)/shard_map/ppermute | solution.py:49

commit v9 on v8

--- a/solution.py
+++ b/solution.py
@@ -303,7 +303,7 @@
     spread = jnp.concatenate([q0, q1, q0], axis=1)
     v0, v1 = two_parts(v)
     v01 = jnp.concatenate([v0, v1], axis=0)
-    cuts = [*range(0, n, chunk), n - chunk // 2, n]
+    cuts = [0, *range(chunk // 2, n, chunk), n]
     bands = [slice(a, b) for a, b in zip(cuts, cuts[1:])]
     for c, here in enumerate(bands):
         xc = x[:, here]

time: 67.2 us -> 67.1 us (level)
  no operation moved by 1% of the time
where the time goes in v9:
time: 67.1 us
  starting transfers between devices  29.6 us (44%)
  waiting for transfers between devices  19.1 us (28%)
  Pallas kernels  17.8 us (27%)
    ppermute x18, starting transfers between devices, moved(): return lax.ppermute(v, AXES, pairs)  29.6 us
    ppermute x18, waiting for transfers between devices, moved(): return lax.ppermute(v, AXES, pairs)  19.1 us
    pallas_call x1, Pallas kernels, corrected(): pl.pallas_call(functools.partial(finish_kernel, pixel_total, chunk, order...  11.2 us
    pallas_call x1, Pallas kernels, upper_gram(): pl.pallas_call(gram_kernel, out_shape=jax.ShapeDtypeStruct((lines, TILE),...  4.52 us
    pallas_call x1, Pallas kernels, start_rows(): pl.pallas_call(start_kernel, out_shape=jax.ShapeDtypeStruct((k, m), F32),...  2.02 us
  transfers between devices with their start and end apart: 18, of which 12 were waited for; matrix products, arithmetic and copies ran while one was open for 0% of the time, Pallas kernels for 3%

profile of v9, /device:TPU:1, one launch (start us, length us, event | category | flops | bytes accessed | tf_op | source)
XLA Modules:
  0.0 67.1 jit_solution(4910046085457867014)
XLA Ops:
  0.0 0.0 copy-start
  0.0 4.5 %gram.1 = f32[1280,128]{1,0:T(8,128)S(1)} custom-call(f32[512,2048]{1,0:T(8,128)} %x_hbm.3), custom_call_target="tpu_custom_call" | custom-call | flops 3221225472 | bytes 4194304 | tf_op jit(solution)/shard_map/gram/pallas_call | solution.py:160
  4.6 3.3 %collective-permute-start = (f32[640,128]{1,0:T(8,128)S(1)}, f32[640,128]{1,0:T(8,128)S(1)}, u32[]{:S(2)}, u32[]{:S(2)}) collective-permute-start(f32[640,128]{1,0:T(8,128)S(1)} %constant_dynamic-slice_fusion.6), channel_id=1, source_target_pairs={{0,32},{1,33},{2,34},{3,35},{4,36},{5,37},{6,38},{7,39},{8,40},{9,... | collective-permute-start | bytes 983048 | tf_op jit(solution)/shard_map/ppermute | solution.py:49
  7.9 1.3 %collective-permute-done = f32[640,128]{1,0:T(8,128)S(1)} collective-permute-done((f32[640,128]{1,0:T(8,128)S(1)}, f32[640,128]{1,0:T(8,128)S(1)}, u32[]{:S(2)}, u32[]{:S(2)}) %collective-permute-start) | collective-permute-done | bytes 327712 | tf_op jit(solution)/shard_map/ppermute | solution.py:49
  9.2 1.3 %collective-permute-start.1 = (f32[160,128]{1,0:T(8,128)S(1)}, f32[160,128]{1,0:T(8,128)S(1)}, u32[]{:S(2)}, u32[]{:S(2)}) collective-permute-start(f32[160,128]{1,0:T(8,128)S(1)} %get-tuple-element.9), channel_id=1, source_target_pairs={{0,128},{1,129},{2,130},{3,131},{4,132},{5,133},{6,134},{7,135},{8... | collective-permute-start | bytes 245768 | tf_op jit(solution)/shard_map/ppermute | solution.py:49
  10.5 1.3 %collective-permute-start.3 = (f32[160,128]{1,0:T(8,128)S(1)}, f32[160,128]{1,0:T(8,128)S(1)}, u32[]{:S(2)}, u32[]{:S(2)}) collective-permute-start(f32[160,128]{1,0:T(8,128)S(1)} %get-tuple-element.10), channel_id=1, source_target_pairs={{0,224},{1,225},{2,226},{3,227},{4,228},{5,229},{6,230},{7,231},{8... | collective-permute-start | bytes 245768 | tf_op jit(solution)/shard_map/ppermute | solution.py:49
  11.8 0.4 collective-permute-start.2
  12.2 2.2 %collective-permute-done.1 = f32[160,128]{1,0:T(8,128)S(1)} collective-permute-done((f32[160,128]{1,0:T(8,128)S(1)}, f32[160,128]{1,0:T(8,128)S(1)}, u32[]{:S(2)}, u32[]{:S(2)}) %collective-permute-start.1) | collective-permute-done | bytes 81952 | tf_op jit(solution)/shard_map/ppermute | solution.py:49
  14.5 1.2 %collective-permute-done.3 = f32[160,128]{1,0:T(8,128)S(1)} collective-permute-done((f32[160,128]{1,0:T(8,128)S(1)}, f32[160,128]{1,0:T(8,128)S(1)}, u32[]{:S(2)}, u32[]{:S(2)}) %collective-permute-start.3) | collective-permute-done | bytes 81952 | tf_op jit(solution)/shard_map/ppermute | solution.py:49
  15.7 1.3 %collective-permute-done.2 = f32[160,128]{1,0:T(8,128)S(1)} collective-permute-done((f32[160,128]{1,0:T(8,128)S(1)}, f32[160,128]{1,0:T(8,128)S(1)}, u32[]{:S(2)}, u32[]{:S(2)}) %collective-permute-start.2) | collective-permute-done | bytes 81952 | tf_op jit(solution)/shard_map/ppermute | solution.py:49
  17.0 2.8 %collective-permute-start.4 = (f32[40,128]{1,0:T(8,128)S(1)}, f32[40,128]{1,0:T(8,128)S(1)}, u32[]{:S(2)}, u32[]{:S(2)}) collective-permute-start(f32[40,128]{1,0:T(8,128)S(1)} %get-tuple-element.18), channel_id=1, source_target_pairs={{0,16},{1,17},{2,18},{3,19},{4,20},{5,21},{6,22},{7,23},{8,24},{9,... | collective-permute-start | bytes 61448 | tf_op jit(solution)/shard_map/ppermute | solution.py:49
  19.8 0.9 %collective-permute-start.6 = (f32[40,128]{1,0:T(8,128)S(1)}, f32[40,128]{1,0:T(8,128)S(1)}, u32[]{:S(2)}, u32[]{:S(2)}) collective-permute-start(f32[40,128]{1,0:T(8,128)S(1)} %get-tuple-element.19), channel_id=1, source_target_pairs={{0,56},{1,57},{2,58},{3,59},{4,60},{5,61},{6,62},{7,63},{8,32},{9,... | collective-permute-start | bytes 61448 | tf_op jit(solution)/shard_map/ppermute | solution.py:49
  20.7 0.8 %collective-permute-start.5 = (f32[40,128]{1,0:T(8,128)S(1)}, f32[40,128]{1,0:T(8,128)S(1)}, u32[]{:S(2)}, u32[]{:S(2)}) collective-permute-start(f32[40,128]{1,0:T(8,128)S(1)} %get-tuple-element.20), channel_id=1, source_target_pairs={{0,40},{1,41},{2,42},{3,43},{4,44},{5,45},{6,46},{7,47},{8,48},{9,... | collective-permute-start | bytes 61448 | tf_op jit(solution)/shard_map/ppermute | solution.py:49
  21.5 0.0 collective-permute-done.4
  21.6 1.5 %collective-permute-done.6 = f32[40,128]{1,0:T(8,128)S(1)} collective-permute-done((f32[40,128]{1,0:T(8,128)S(1)}, f32[40,128]{1,0:T(8,128)S(1)}, u32[]{:S(2)}, u32[]{:S(2)}) %collective-permute-start.6) | collective-permute-done | bytes 20512 | tf_op jit(solution)/shard_map/ppermute | solution.py:49
  23.0 2.1 %collective-permute-done.5 = f32[40,128]{1,0:T(8,128)S(1)} collective-permute-done((f32[40,128]{1,0:T(8,128)S(1)}, f32[40,128]{1,0:T(8,128)S(1)}, u32[]{:S(2)}, u32[]{:S(2)}) %collective-permute-start.5) | collective-permute-done | bytes 20512 | tf_op jit(solution)/shard_map/ppermute | solution.py:49
  25.2 1.9 %collective-permute-start.7 = (f32[40,128]{1,0:T(8,128)S(1)}, f32[40,128]{1,0:T(8,128)S(1)}, u32[]{:S(2)}, u32[]{:S(2)}) collective-permute-start(f32[40,128]{1,0:T(8,128)S(1)} %add_add_fusion.2), channel_id=1, source_target_pairs={{0,33},{1,32},{2,35},{3,34},{4,37},{5,36},{6,39},{7,38},{8,41},{9,... | collective-permute-start | bytes 61448 | tf_op jit(solution)/shard_map/ppermute | solution.py:49
  27.1 1.5 %collective-permute-done.7 = f32[40,128]{1,0:T(8,128)S(1)} collective-permute-done((f32[40,128]{1,0:T(8,128)S(1)}, f32[40,128]{1,0:T(8,128)S(1)}, u32[]{:S(2)}, u32[]{:S(2)}) %collective-permute-start.7) | collective-permute-done | bytes 20512 | tf_op jit(solution)/shard_map/ppermute | solution.py:49
  28.6 6.6 %collective-permute-start.10 = (f32[40,128]{1,0:T(8,128)S(1)}, f32[40,128]{1,0:T(8,128)S(1)}, u32[]{:S(2)}, u32[]{:S(2)}) collective-permute-start(f32[40,128]{1,0:T(8,128)S(1)} %add.129), channel_id=1, source_target_pairs={{0,37},{1,36},{2,39},{3,38},{4,33},{5,32},{6,35},{7,34},{8,45},{9,... | collective-permute-start | bytes 61448 | tf_op jit(solution)/shard_map/ppermute | solution.py:49
  35.1 0.3 collective-permute-start.9
  35.4 3.2 %collective-permute-start.8 = (f32[40,128]{1,0:T(8,128)S(1)}, f32[40,128]{1,0:T(8,128)S(1)}, u32[]{:S(2)}, u32[]{:S(2)}) collective-permute-start(f32[40,128]{1,0:T(8,128)S(1)} %add.129), channel_id=1, source_target_pairs={{0,39},{1,34},{2,33},{3,36},{4,35},{5,38},{6,37},{7,32},{8,47},{9,... | collective-permute-start | bytes 61448 | tf_op jit(solution)/shard_map/ppermute | solution.py:49
  38.6 0.0 copy-done
  38.6 2.0 %start_rows.1.v_ref = f32[64,512]{1,0:T(8,128)S(1)} custom-call(f32[64,512]{1,0:T(8,128)S(1)} %bitcast.4), custom_call_target="tpu_custom_call" | custom-call | flops 8000000000 | bytes 262144 | tf_op jit(solution)/shard_map/start_rows/pallas_call | solution.py:229
  40.6 0.0 collective-permute-done.10
  40.6 0.0 collective-permute-done.9
  40.6 0.0 collective-permute-done.8
  40.7 0.1 collective-permute-start.13
  40.8 0.6 collective-permute-start.12
  41.4 2.6 %collective-permute-start.11 = (f32[40,128]{1,0:T(8,128)S(1)}, f32[40,128]{1,0:T(8,128)S(1)}, u32[]{:S(2)}, u32[]{:S(2)}) collective-permute-start(f32[40,128]{1,0:T(8,128)S(1)} %add_add_fusion.1), channel_id=1, source_target_pairs={{0,56},{1,57},{2,58},{3,59},{4,60},{5,61},{6,62},{7,63},{8,32},{9,... | collective-permute-start | bytes 61448 | tf_op jit(solution)/shard_map/ppermute | solution.py:49
  44.0 1.5 %collective-permute-done.11 = f32[40,128]{1,0:T(8,128)S(1)} collective-permute-done((f32[40,128]{1,0:T(8,128)S(1)}, f32[40,128]{1,0:T(8,128)S(1)}, u32[]{:S(2)}, u32[]{:S(2)}) %collective-permute-start.11) | collective-permute-done | bytes 20512 | tf_op jit(solution)/shard_map/ppermute | solution.py:49
  45.5 0.3 collective-permute-done.12
  45.7 0.0 collective-permute-done.13
  45.7 1.6 %collective-permute-start.14 = (f32[160,128]{1,0:T(8,128)S(1)}, f32[160,128]{1,0:T(8,128)S(1)}, u32[]{:S(2)}, u32[]{:S(2)}) collective-permute-start(f32[160,128]{1,0:T(8,128)S(1)} %get-tuple-element.23), channel_id=1, source_target_pairs={{0,128},{1,129},{2,130},{3,131},{4,132},{5,133},{6,134},{7,135},{8... | collective-permute-start | bytes 245768 | tf_op jit(solution)/shard_map/ppermute | solution.py:49
  47.3 1.3 %collective-permute-start.16 = (f32[160,128]{1,0:T(8,128)S(1)}, f32[160,128]{1,0:T(8,128)S(1)}, u32[]{:S(2)}, u32[]{:S(2)}) collective-permute-start(f32[160,128]{1,0:T(8,128)S(1)} %get-tuple-element.23), channel_id=1, source_target_pairs={{0,224},{1,225},{2,226},{3,227},{4,228},{5,229},{6,230},{7,231},{8... | collective-permute-start | bytes 245768 | tf_op jit(solution)/shard_map/ppermute | solution.py:49
  48.7 0.4 collective-permute-start.15
  49.1 2.0 %collective-permute-done.14 = f32[160,128]{1,0:T(8,128)S(1)} collective-permute-done((f32[160,128]{1,0:T(8,128)S(1)}, f32[160,128]{1,0:T(8,128)S(1)}, u32[]{:S(2)}, u32[]{:S(2)}) %collective-permute-start.14) | collective-permute-done | bytes 81952 | tf_op jit(solution)/shard_map/ppermute | solution.py:49
  51.1 2.8 %collective-permute-done.15 = f32[160,128]{1,0:T(8,128)S(1)} collective-permute-done((f32[160,128]{1,0:T(8,128)S(1)}, f32[160,128]{1,0:T(8,128)S(1)}, u32[]{:S(2)}, u32[]{:S(2)}) %collective-permute-start.15) | collective-permute-done | bytes 81952 | tf_op jit(solution)/shard_map/ppermute | solution.py:49
  53.9 0.0 collective-permute-done.16
  53.9 0.1 collective-permute-start.17
  54.0 0.1 pad_add_fusion.me_ref
  54.1 1.5 %collective-permute-done.17 = f32[640,128]{1,0:T(8,128)S(1)} collective-permute-done((f32[640,128]{1,0:T(8,128)S(1)}, f32[640,128]{1,0:T(8,128)S(1)}, u32[]{:S(2)}, u32[]{:S(2)}) %collective-permute-start.17) | collective-permute-done | bytes 327712 | tf_op jit(solution)/shard_map/ppermute | solution.py:49
  55.7 11.2 %finish.1 = f32[512,2048]{1,0:T(8,128)} custom-call(s32[3]{0:T(128)S(1)} %pad_add_fusion.me_ref, f32[1280,128]{1,0:T(8,128)S(1)} %constant_dynamic-update-slice_fusion.11.lines_ref, f32[64,512]{1,0:T(8,128)S(1)} %start_rows.1.v_ref, f32[512,2048]{1,0:T(8,128)} %x_hbm.3), custom_call_target="tpu_custom_call" | custom-call | flops 805306368 | bytes 8388608 | tf_op jit(solution)/shard_map/finish/pallas_call | solution.py:325
  (16 shorter events, 0.2 us)
Async XLA Ops:
  0.0 38.6 %copy-start = (f32[512,64]{0,1:T(8,128)S(1)}, f32[512,64]{0,1:T(8,128)}, u32[]{:S(2)}) copy-start(f32[512,64]{0,1:T(8,128)} %param.3) | copy-start | bytes 393220
  4.6 4.6 %collective-permute-start = (f32[640,128]{1,0:T(8,128)S(1)}, f32[640,128]{1,0:T(8,128)S(1)}, u32[]{:S(2)}, u32[]{:S(2)}) collective-permute-start(f32[640,128]{1,0:T(8,128)S(1)} %constant_dynamic-slice_fusion.6), channel_id=1, source_target_pairs={{0,32},{1,33},{2,34},{3,35},{4,36},{5,37},{6,38},{7,39},{8,40},{9,... | collective-permute-start | bytes 983048 | tf_op jit(solution)/shard_map/ppermute | solution.py:49
  9.2 5.2 %collective-permute-start.1 = (f32[160,128]{1,0:T(8,128)S(1)}, f32[160,128]{1,0:T(8,128)S(1)}, u32[]{:S(2)}, u32[]{:S(2)}) collective-permute-start(f32[160,128]{1,0:T(8,128)S(1)} %get-tuple-element.9), channel_id=1, source_target_pairs={{0,128},{1,129},{2,130},{3,131},{4,132},{5,133},{6,134},{7,135},{8... | collective-permute-start | bytes 245768 | tf_op jit(solution)/shard_map/ppermute | solution.py:49
  10.5 5.2 %collective-permute-start.3 = (f32[160,128]{1,0:T(8,128)S(1)}, f32[160,128]{1,0:T(8,128)S(1)}, u32[]{:S(2)}, u32[]{:S(2)}) collective-permute-start(f32[160,128]{1,0:T(8,128)S(1)} %get-tuple-element.10), channel_id=1, source_target_pairs={{0,224},{1,225},{2,226},{3,227},{4,228},{5,229},{6,230},{7,231},{8... | collective-permute-start | bytes 245768 | tf_op jit(solution)/shard_map/ppermute | solution.py:49
  11.8 5.1 %collective-permute-start.2 = (f32[160,128]{1,0:T(8,128)S(1)}, f32[160,128]{1,0:T(8,128)S(1)}, u32[]{:S(2)}, u32[]{:S(2)}) collective-permute-start(f32[160,128]{1,0:T(8,128)S(1)} %get-tuple-element.11), channel_id=1, source_target_pairs={{0,96},{1,97},{2,98},{3,99},{4,100},{5,101},{6,102},{7,103},{8,104... | collective-permute-start | bytes 245768 | tf_op jit(solution)/shard_map/ppermute | solution.py:49
  17.0 4.6 %collective-permute-start.4 = (f32[40,128]{1,0:T(8,128)S(1)}, f32[40,128]{1,0:T(8,128)S(1)}, u32[]{:S(2)}, u32[]{:S(2)}) collective-permute-start(f32[40,128]{1,0:T(8,128)S(1)} %get-tuple-element.18), channel_id=1, source_target_pairs={{0,16},{1,17},{2,18},{3,19},{4,20},{5,21},{6,22},{7,23},{8,24},{9,... | collective-permute-start | bytes 61448 | tf_op jit(solution)/shard_map/ppermute | solution.py:49
  19.8 3.2 %collective-permute-start.6 = (f32[40,128]{1,0:T(8,128)S(1)}, f32[40,128]{1,0:T(8,128)S(1)}, u32[]{:S(2)}, u32[]{:S(2)}) collective-permute-start(f32[40,128]{1,0:T(8,128)S(1)} %get-tuple-element.19), channel_id=1, source_target_pairs={{0,56},{1,57},{2,58},{3,59},{4,60},{5,61},{6,62},{7,63},{8,32},{9,... | collective-permute-start | bytes 61448 | tf_op jit(solution)/shard_map/ppermute | solution.py:49
  20.7 4.4 %collective-permute-start.5 = (f32[40,128]{1,0:T(8,128)S(1)}, f32[40,128]{1,0:T(8,128)S(1)}, u32[]{:S(2)}, u32[]{:S(2)}) collective-permute-start(f32[40,128]{1,0:T(8,128)S(1)} %get-tuple-element.20), channel_id=1, source_target_pairs={{0,40},{1,41},{2,42},{3,43},{4,44},{5,45},{6,46},{7,47},{8,48},{9,... | collective-permute-start | bytes 61448 | tf_op jit(solution)/shard_map/ppermute | solution.py:49
  25.2 3.4 %collective-permute-start.7 = (f32[40,128]{1,0:T(8,128)S(1)}, f32[40,128]{1,0:T(8,128)S(1)}, u32[]{:S(2)}, u32[]{:S(2)}) collective-permute-start(f32[40,128]{1,0:T(8,128)S(1)} %add_add_fusion.2), channel_id=1, source_target_pairs={{0,33},{1,32},{2,35},{3,34},{4,37},{5,36},{6,39},{7,38},{8,41},{9,... | collective-permute-start | bytes 61448 | tf_op jit(solution)/shard_map/ppermute | solution.py:49
  28.6 12.1 %collective-permute-start.10 = (f32[40,128]{1,0:T(8,128)S(1)}, f32[40,128]{1,0:T(8,128)S(1)}, u32[]{:S(2)}, u32[]{:S(2)}) collective-permute-start(f32[40,128]{1,0:T(8,128)S(1)} %add.129), channel_id=1, source_target_pairs={{0,37},{1,36},{2,39},{3,38},{4,33},{5,32},{6,35},{7,34},{8,45},{9,... | collective-permute-start | bytes 61448 | tf_op jit(solution)/shard_map/ppermute | solution.py:49
  35.1 5.5 %collective-permute-start.9 = (f32[40,128]{1,0:T(8,128)S(1)}, f32[40,128]{1,0:T(8,128)S(1)}, u32[]{:S(2)}, u32[]{:S(2)}) collective-permute-start(f32[40,128]{1,0:T(8,128)S(1)} %add.129), channel_id=1, source_target_pairs={{0,6},{1,3},{2,0},{3,5},{4,2},{5,7},{6,4},{7,1},{8,14},{9,11},{10,... | collective-permute-start | bytes 61448 | tf_op jit(solution)/shard_map/ppermute | solution.py:49
  35.4 5.2 %collective-permute-start.8 = (f32[40,128]{1,0:T(8,128)S(1)}, f32[40,128]{1,0:T(8,128)S(1)}, u32[]{:S(2)}, u32[]{:S(2)}) collective-permute-start(f32[40,128]{1,0:T(8,128)S(1)} %add.129), channel_id=1, source_target_pairs={{0,39},{1,34},{2,33},{3,36},{4,35},{5,38},{6,37},{7,32},{8,47},{9,... | collective-permute-start | bytes 61448 | tf_op jit(solution)/shard_map/ppermute | solution.py:49
  40.7 5.1 %collective-permute-start.13 = (f32[40,128]{1,0:T(8,128)S(1)}, f32[40,128]{1,0:T(8,128)S(1)}, u32[]{:S(2)}, u32[]{:S(2)}) collective-permute-start(f32[40,128]{1,0:T(8,128)S(1)} %add_add_fusion.1), channel_id=1, source_target_pairs={{0,16},{1,17},{2,18},{3,19},{4,20},{5,21},{6,22},{7,23},{8,24},{9,... | collective-permute-start | bytes 61448 | tf_op jit(solution)/shard_map/ppermute | solution.py:49
  40.8 4.9 %collective-permute-start.12 = (f32[40,128]{1,0:T(8,128)S(1)}, f32[40,128]{1,0:T(8,128)S(1)}, u32[]{:S(2)}, u32[]{:S(2)}) collective-permute-start(f32[40,128]{1,0:T(8,128)S(1)} %add_add_fusion.1), channel_id=1, source_target_pairs={{0,40},{1,41},{2,42},{3,43},{4,44},{5,45},{6,46},{7,47},{8,48},{9,... | collective-permute-start | bytes 61448 | tf_op jit(solution)/shard_map/ppermute | solution.py:49
  41.4 4.1 %collective-permute-start.11 = (f32[40,128]{1,0:T(8,128)S(1)}, f32[40,128]{1,0:T(8,128)S(1)}, u32[]{:S(2)}, u32[]{:S(2)}) collective-permute-start(f32[40,128]{1,0:T(8,128)S(1)} %add_add_fusion.1), channel_id=1, source_target_pairs={{0,56},{1,57},{2,58},{3,59},{4,60},{5,61},{6,62},{7,63},{8,32},{9,... | collective-permute-start | bytes 61448 | tf_op jit(solution)/shard_map/ppermute | solution.py:49
  45.7 5.3 %collective-permute-start.14 = (f32[160,128]{1,0:T(8,128)S(1)}, f32[160,128]{1,0:T(8,128)S(1)}, u32[]{:S(2)}, u32[]{:S(2)}) collective-permute-start(f32[160,128]{1,0:T(8,128)S(1)} %get-tuple-element.23), channel_id=1, source_target_pairs={{0,128},{1,129},{2,130},{3,131},{4,132},{5,133},{6,134},{7,135},{8... | collective-permute-start | bytes 245768 | tf_op jit(solution)/shard_map/ppermute | solution.py:49
  47.3 6.6 %collective-permute-start.16 = (f32[160,128]{1,0:T(8,128)S(1)}, f32[160,128]{1,0:T(8,128)S(1)}, u32[]{:S(2)}, u32[]{:S(2)}) collective-permute-start(f32[160,128]{1,0:T(8,128)S(1)} %get-tuple-element.23), channel_id=1, source_target_pairs={{0,224},{1,225},{2,226},{3,227},{4,228},{5,229},{6,230},{7,231},{8... | collective-permute-start | bytes 245768 | tf_op jit(solution)/shard_map/ppermute | solution.py:49
  48.7 5.2 %collective-permute-start.15 = (f32[160,128]{1,0:T(8,128)S(1)}, f32[160,128]{1,0:T(8,128)S(1)}, u32[]{:S(2)}, u32[]{:S(2)}) collective-permute-start(f32[160,128]{1,0:T(8,128)S(1)} %get-tuple-element.23), channel_id=1, source_target_pairs={{0,96},{1,97},{2,98},{3,99},{4,100},{5,101},{6,102},{7,103},{8,104... | collective-permute-start | bytes 245768 | tf_op jit(solution)/shard_map/ppermute | solution.py:49
  53.9 1.7 %collective-permute-start.17 = (f32[640,128]{1,0:T(8,128)S(1)}, f32[640,128]{1,0:T(8,128)S(1)}, u32[]{:S(2)}, u32[]{:S(2)}) collective-permute-start(f32[640,128]{1,0:T(8,128)S(1)} %get-tuple-element.12), channel_id=1, source_target_pairs={{0,32},{1,33},{2,34},{3,35},{4,36},{5,37},{6,38},{7,39},{8,40},{9,... | collective-permute-start | bytes 983048 | tf_op jit(solution)/shard_map/ppermute | solution.py:49
